TPU v7x, 32 devices: a whole 2x2x4 slice. The times are simulated.
32 devices in a mesh: wide: 8 (over z, y), narrow: 4 (over x, core).
Axes of the slice: x: 2, y: 2, z: 4, core: 2. Of those that a mesh axis runs over, the one named last changes fastest.
Arguments:
- tokens: bfloat16 [4, 1024, 1024], P(None, 'wide'), may hold values from -6 to 6
- documents: int32 [4, 1024], replicated, may hold values from 0 to 5, as said below
- prenorm: bfloat16 [1024], P('wide'), may hold values from 0.5 to 1.5
- qheads: bfloat16 [1024, 96], P('wide', 'narrow'), may hold values from -0.25 to 0.25
- qshared: bfloat16 [1024, 384], P('wide', 'narrow'), may hold values from -0.25 to 0.25
- kheads: bfloat16 [1024, 32], P('wide', 'narrow'), may hold values from -0.25 to 0.25
- kshared: bfloat16 [1024, 128], P('wide', 'narrow'), may hold values from -0.25 to 0.25
- vheads: bfloat16 [1024, 32], P('wide', 'narrow'), may hold values from -0.1875 to 0.1875
- vshared: bfloat16 [1024, 128], P('wide', 'narrow'), may hold values from -0.1875 to 0.1875
- project: bfloat16 [1024, 1024], P('narrow', 'wide'), may hold values from -1.5 to 1.5
- midnorm: bfloat16 [1024], P('wide'), may hold values from 0.5 to 1.5
- gating: bfloat16 [1024, 2816], P('wide', 'narrow'), may hold values from -0.1875 to 0.1875
- upward: bfloat16 [1024, 2816], P('wide', 'narrow'), may hold values from -0.1875 to 0.1875
- downward: bfloat16 [2816, 1024], P('narrow', 'wide'), may hold values from -0.109375 to 0.109375
- cotangent: bfloat16 [4, 1024, 1024], P(None, 'wide'), may hold values from -6 to 6
Outputs:
- output: bfloat16 [4, 1024, 1024], P(None, 'wide')
- tokens_gradient: float32 [4, 1024, 1024], P(None, 'wide')
- prenorm_gradient: float32 [1024], P('wide')
- qheads_gradient: float32 [1024, 96], P('wide', 'narrow')
- qshared_gradient: float32 [1024, 384], P('wide', 'narrow')
- kheads_gradient: float32 [1024, 32], P('wide', 'narrow')
- kshared_gradient: float32 [1024, 128], P('wide', 'narrow')
- vheads_gradient: float32 [1024, 32], P('wide', 'narrow')
- vshared_gradient: float32 [1024, 128], P('wide', 'narrow')
- project_gradient: float32 [1024, 1024], P('narrow', 'wide')
- midnorm_gradient: float32 [1024], P('wide')
- gating_gradient: float32 [1024, 2816], P('wide', 'narrow')
- upward_gradient: float32 [1024, 2816], P('wide', 'narrow')
- downward_gradient: float32 [2816, 1024], P('narrow', 'wide')
Inputs may be any that keep to these rules, and one draw needn't show every extreme that they name: Along each row the ids start at 0 and rise by one at each document boundary. One row, drawn from the seed, holds a single document; every other row holds 4 to 6 documents of 128 tokens or more, and the row after the single-document row (the first row after the last) holds 6.
All inputs are finite; a program needn't handle non-finite values.
Results may differ from a plain program's by a relative error of at most 0.024.
Values may be sent and summed in bfloat16 or wider, within the bound.
A program may use at most 128 MiB of HBM per device.

v0:
```python
import math

import jax
import jax.numpy as jnp
from jax import lax
from jax.sharding import PartitionSpec as P

DH = 64
QR = 6
KR = 2
VR = 2


epsilon = 1e-06
masked_score = -1e30
block_limit = 512
highest = lax.Precision.HIGHEST


def rotate(tensor, positions, direction):
    half_width = tensor.shape[-1] // 2
    frequency = 10000.0 ** (-jnp.arange(half_width, dtype=jnp.float32) / half_width)
    angles = positions.astype(jnp.float32)[:, None] * frequency[None, :]
    cosines = jnp.cos(angles)[:, None, :]
    sines_all = direction * jnp.sin(angles)[:, None, :]
    front_half = tensor[..., :half_width]
    back_half = tensor[..., half_width:]
    return jnp.concatenate(
        [
            front_half * cosines - back_half * sines_all,
            back_half * cosines + front_half * sines_all,
        ],
        axis=-1,
    )


def block_width(extent):
    return math.gcd(extent, block_limit)


def blockwise(running, extent, update):
    block_size = block_width(extent)

    def advance(state_now, block_index):
        return (update(state_now, block_index * block_size, block_size), None)

    running, _ = lax.scan(advance, running, jnp.arange(extent // block_size, dtype=jnp.int32))
    return running


def rebuild(head_part, shared_part, rank_size):
    batch_rows, extent, head_width = head_part.shape
    head_view = head_part.reshape(batch_rows, extent, head_width // rank_size, rank_size)
    shared_view = shared_part.reshape(
        batch_rows, extent, rank_size, shared_part.shape[-1] // rank_size
    )
    joined = (
        jnp.einsum("bnhr,bnrd->bnhd", head_view, shared_view, preferred_element_type=jnp.float32)
        / rank_size
    )
    return joined.reshape(batch_rows, extent, -1).astype(jnp.bfloat16)


def split_heads(tensor, heads_local):
    return tensor.reshape(
        tensor.shape[0], tensor.shape[1], heads_local, tensor.shape[2] // heads_local
    )


def normalize(source, scales):
    inverse = lax.rsqrt(jnp.mean(source * source, axis=-1, keepdims=True) + epsilon)
    return (source * inverse * scales, inverse)


def norm_back(normed_back, source, inverse, scales):
    scaled = normed_back * scales
    scale_back = jnp.sum(normed_back * source * inverse, axis=0)
    source_back = inverse * scaled - source * inverse**3 * jnp.mean(
        scaled * source, axis=-1, keepdims=True
    )
    return (source_back, scale_back)


def allowed_mask(key_places, key_docs, query_places, query_docs):
    causal = key_places[None, None, :] <= query_places[None, :, None]
    same_doc = key_docs[:, None, :] == query_docs[:, :, None]
    return (causal & same_doc)[:, None]


def back_through(gradient_low, weight_full):
    return jnp.einsum("nc,dc->nd", gradient_low, weight_full, preferred_element_type=jnp.float32)


def outer(left, right):
    return jnp.einsum("nc,nd->cd", left, right, preferred_element_type=jnp.float32)


def on_device(
    tokens,
    documents,
    prenorm,
    qheads,
    qshared,
    kheads,
    kshared,
    vheads,
    vshared,
    project,
    midnorm,
    gating,
    upward,
    downward,
    cotangent,
):
    batch_rows, local_tokens, model_width = tokens.shape
    flat_count = batch_rows * local_tokens
    heads_local = kheads.shape[1] // KR
    scale_score = DH ** (-0.5)
    offset = lax.axis_index("wide") * local_tokens
    local_places = offset + jnp.arange(local_tokens, dtype=jnp.int32)
    local_docs = lax.dynamic_slice_in_dim(documents, offset, local_tokens, 1)
    gathered = (
        lax.all_gather(prenorm, "wide", axis=0, tiled=True),
        lax.all_gather(qheads, "wide", axis=0, tiled=True),
        lax.all_gather(qshared, "wide", axis=0, tiled=True),
        lax.all_gather(kheads, "wide", axis=0, tiled=True),
        lax.all_gather(kshared, "wide", axis=0, tiled=True),
        lax.all_gather(vheads, "wide", axis=0, tiled=True),
        lax.all_gather(vshared, "wide", axis=0, tiled=True),
        lax.all_gather(project, "wide", axis=1, tiled=True),
        lax.all_gather(midnorm, "wide", axis=0, tiled=True),
        lax.all_gather(gating, "wide", axis=0, tiled=True),
        lax.all_gather(upward, "wide", axis=0, tiled=True),
        lax.all_gather(downward, "wide", axis=1, tiled=True),
    )
    (
        prenorm_full,
        qheads_full,
        qshared_cols,
        kheads_full,
        kshared_cols,
        vheads_full,
        vshared_cols,
        project_full,
        midnorm_full,
        gating_full,
        upward_full,
        downward_full,
    ) = gathered
    qshared_full, kshared_full, vshared_full = (
        lax.all_gather(qshared_cols, "narrow", axis=1, tiled=True),
        lax.all_gather(kshared_cols, "narrow", axis=1, tiled=True),
        lax.all_gather(vshared_cols, "narrow", axis=1, tiled=True),
    )
    source = tokens.reshape(flat_count, model_width).astype(jnp.float32)
    first_norm, first_inverse = normalize(source, prenorm_full.astype(jnp.float32))
    normed = first_norm.astype(jnp.bfloat16)
    query_heads = jnp.dot(normed, qheads_full, preferred_element_type=jnp.float32).reshape(
        batch_rows, local_tokens, heads_local, QR
    )
    query_rotated = rotate(
        jnp.dot(normed, qshared_full, preferred_element_type=jnp.float32).reshape(
            batch_rows, local_tokens, QR, DH
        ),
        local_places,
        1.0,
    )
    queries = (
        jnp.einsum("blhr,blrd->blhd", query_heads, query_rotated, precision=highest) / QR
    ).astype(jnp.bfloat16)
    key_heads = (
        jnp.dot(normed, kheads_full, preferred_element_type=jnp.float32)
        .astype(jnp.bfloat16)
        .reshape(batch_rows, local_tokens, -1)
    )
    key_shared = (
        rotate(
            jnp.dot(normed, kshared_full, preferred_element_type=jnp.float32).reshape(
                batch_rows, local_tokens, KR, DH
            ),
            local_places,
            1.0,
        )
        .astype(jnp.bfloat16)
        .reshape(batch_rows, local_tokens, -1)
    )
    value_heads = (
        jnp.dot(normed, vheads_full, preferred_element_type=jnp.float32)
        .astype(jnp.bfloat16)
        .reshape(batch_rows, local_tokens, -1)
    )
    value_shared = (
        jnp.dot(normed, vshared_full, preferred_element_type=jnp.float32)
        .astype(jnp.bfloat16)
        .reshape(batch_rows, local_tokens, -1)
    )
    key_rows = rebuild(key_heads, key_shared, KR)
    value_rows = rebuild(value_heads, value_shared, VR)

    def from_rebuilt(sliced):
        return (split_heads(sliced[0], heads_local), split_heads(sliced[1], heads_local))

    def forward_maker(convert, running, pieces):

        def update(state_now, first_row, block_size):
            sliced = tuple(
                (lax.dynamic_slice_in_dim(member, first_row, block_size, 1) for member in pieces)
            )
            key_block, value_block = convert(sliced)
            key_places = first_row + jnp.arange(block_size, dtype=jnp.int32)
            key_docs = lax.dynamic_slice_in_dim(documents, first_row, block_size, 1)
            allowed = allowed_mask(key_places, key_docs, local_places, local_docs)
            scores = (
                jnp.einsum(
                    "blhd,bkhd->bhlk", queries, key_block, preferred_element_type=jnp.float32
                )
                * scale_score
            )
            old_max, old_total, old_acc = state_now
            new_max = jnp.maximum(
                old_max, jnp.max(jnp.where(allowed, scores, masked_score), axis=-1)
            )
            weights = jnp.where(allowed, jnp.exp(scores - new_max[..., None]), 0.0)
            factor = jnp.exp(old_max - new_max)
            new_total = old_total * factor + jnp.sum(weights, axis=-1)
            new_acc = old_acc * factor[..., None] + jnp.einsum(
                "bhlk,bkhd->bhld",
                weights.astype(jnp.bfloat16),
                value_block,
                preferred_element_type=jnp.float32,
            )
            return (new_max, new_total, new_acc)

        return blockwise(running, pieces[0].shape[1], update)

    initial = (
        jnp.full((batch_rows, heads_local, local_tokens), masked_score, jnp.float32),
        jnp.zeros((batch_rows, heads_local, local_tokens), jnp.float32),
        jnp.zeros((batch_rows, heads_local, local_tokens, DH), jnp.float32),
    )
    forward_state = forward_maker(
        from_rebuilt,
        initial,
        (
            lax.all_gather(key_rows, "wide", axis=1, tiled=True),
            lax.all_gather(value_rows, "wide", axis=1, tiled=True),
        ),
    )
    run_max, run_total, run_acc = forward_state
    log_total = run_max + jnp.log(run_total)
    attended = jnp.transpose(run_acc / run_total[..., None], (0, 2, 1, 3))
    mixture = attended.reshape(flat_count, heads_local * DH).astype(jnp.bfloat16)
    branch_sum = lax.psum(
        jnp.dot(mixture, project_full, preferred_element_type=jnp.float32).astype(jnp.bfloat16),
        "narrow",
    ).astype(jnp.float32)
    middle = source + branch_sum
    second_norm, second_inverse = normalize(middle, midnorm_full.astype(jnp.float32))
    normed_mid = second_norm.astype(jnp.bfloat16)
    gate_values = jnp.dot(normed_mid, gating_full, preferred_element_type=jnp.float32)
    up_values = jnp.dot(normed_mid, upward_full, preferred_element_type=jnp.float32)
    sigmoid_gate = jax.nn.sigmoid(gate_values)
    silu_gate = gate_values * sigmoid_gate
    hidden = (silu_gate * up_values).astype(jnp.bfloat16)
    dense_out = lax.psum(
        jnp.dot(hidden, downward_full, preferred_element_type=jnp.float32).astype(jnp.bfloat16),
        "narrow",
    ).astype(jnp.float32)
    output = (
        (middle + dense_out).astype(jnp.bfloat16).reshape(batch_rows, local_tokens, model_width)
    )
    upstream = cotangent.reshape(flat_count, model_width)
    hidden_back = jnp.einsum(
        "nd,fd->nf", upstream, downward_full, preferred_element_type=jnp.float32
    )
    gate_gradient = (
        hidden_back * up_values * sigmoid_gate * (1.0 + gate_values * (1.0 - sigmoid_gate))
    ).astype(jnp.bfloat16)
    up_gradient = (hidden_back * silu_gate).astype(jnp.bfloat16)
    mid_back = lax.psum(
        (back_through(gate_gradient, gating_full) + back_through(up_gradient, upward_full)).astype(
            jnp.bfloat16
        ),
        "narrow",
    ).astype(jnp.float32)
    middle_part, midnorm_back = norm_back(
        mid_back, middle, second_inverse, midnorm_full.astype(jnp.float32)
    )
    middle_gradient = upstream.astype(jnp.float32) + middle_part
    branch_gradient = middle_gradient.astype(jnp.bfloat16)
    attended_gradient = (
        jnp.einsum("nd,cd->nc", branch_gradient, project_full, preferred_element_type=jnp.float32)
        .astype(jnp.bfloat16)
        .reshape(batch_rows, local_tokens, heads_local, DH)
    )
    delta_rows = jnp.transpose(
        jnp.sum(attended_gradient.astype(jnp.float32) * attended, axis=-1), (0, 2, 1)
    )
    zeros_keys = jnp.zeros((batch_rows, local_tokens, heads_local, DH), jnp.float32)

    def backward_maker(convert, running, pieces):

        def update(state_now, first_row, block_size):
            sliced = tuple(
                (lax.dynamic_slice_in_dim(member, first_row, block_size, 1) for member in pieces)
            )
            key_block, value_block = convert(sliced)
            key_places = first_row + jnp.arange(block_size, dtype=jnp.int32)
            key_docs = lax.dynamic_slice_in_dim(documents, first_row, block_size, 1)
            allowed = allowed_mask(key_places, key_docs, local_places, local_docs)
            scores = (
                jnp.einsum(
                    "blhd,bkhd->bhlk", queries, key_block, preferred_element_type=jnp.float32
                )
                * scale_score
            )
            chance = jnp.where(allowed, jnp.exp(scores - log_total[..., None]), 0.0)
            pushed = jnp.einsum(
                "blhd,bkhd->bhlk",
                attended_gradient,
                value_block,
                preferred_element_type=jnp.float32,
            )
            score_back = (chance * (pushed - delta_rows[..., None])).astype(jnp.bfloat16)
            return (
                state_now
                + jnp.einsum(
                    "bhlk,bkhd->blhd", score_back, key_block, preferred_element_type=jnp.float32
                )
                * scale_score
            )

        return blockwise(running, pieces[0].shape[1], update)

    query_back = backward_maker(
        from_rebuilt,
        zeros_keys,
        (
            lax.all_gather(key_rows, "wide", axis=1, tiled=True),
            lax.all_gather(value_rows, "wide", axis=1, tiled=True),
        ),
    )
    lse_all, delta_all = (
        lax.all_gather(log_total, "wide", axis=2, tiled=True),
        lax.all_gather(delta_rows, "wide", axis=2, tiled=True),
    )
    keys_local = split_heads(key_rows, heads_local)
    values_local = split_heads(value_rows, heads_local)

    def query_step(running, pieces):

        def update(state_now, first_row, block_size):
            query_block = split_heads(
                lax.dynamic_slice_in_dim(pieces[0], first_row, block_size, 1), heads_local
            )
            push_block = split_heads(
                lax.dynamic_slice_in_dim(pieces[1], first_row, block_size, 1), heads_local
            )
            query_places = first_row + jnp.arange(block_size, dtype=jnp.int32)
            query_docs = lax.dynamic_slice_in_dim(documents, first_row, block_size, 1)
            lse_block = lax.dynamic_slice_in_dim(lse_all, first_row, block_size, 2)
            delta_block = lax.dynamic_slice_in_dim(delta_all, first_row, block_size, 2)
            allowed = allowed_mask(local_places, local_docs, query_places, query_docs)
            scores = (
                jnp.einsum(
                    "bqhd,bkhd->bhqk", query_block, keys_local, preferred_element_type=jnp.float32
                )
                * scale_score
            )
            chance = jnp.where(allowed, jnp.exp(scores - lse_block[..., None]), 0.0)
            key_acc, value_acc = state_now
            value_acc = value_acc + jnp.einsum(
                "bhqk,bqhd->bkhd",
                chance.astype(jnp.bfloat16),
                push_block,
                preferred_element_type=jnp.float32,
            )
            pushed = jnp.einsum(
                "bqhd,bkhd->bhqk", push_block, values_local, preferred_element_type=jnp.float32
            )
            score_back = (chance * (pushed - delta_block[..., None])).astype(jnp.bfloat16)
            key_acc = (
                key_acc
                + jnp.einsum(
                    "bhqk,bqhd->bkhd", score_back, query_block, preferred_element_type=jnp.float32
                )
                * scale_score
            )
            return (key_acc, value_acc)

        return blockwise(running, pieces[0].shape[1], update)

    key_back, value_back = query_step(
        (zeros_keys, zeros_keys),
        (
            lax.all_gather(
                queries.reshape(batch_rows, local_tokens, -1), "wide", axis=1, tiled=True
            ),
            lax.all_gather(
                attended_gradient.reshape(batch_rows, local_tokens, -1), "wide", axis=1, tiled=True
            ),
        ),
    )
    key_heads_float = key_heads.reshape(batch_rows, local_tokens, heads_local, KR).astype(
        jnp.float32
    )
    key_shared_float = key_shared.reshape(batch_rows, local_tokens, KR, DH).astype(jnp.float32)
    value_heads_float = value_heads.reshape(batch_rows, local_tokens, heads_local, VR).astype(
        jnp.float32
    )
    value_shared_float = value_shared.reshape(batch_rows, local_tokens, VR, DH).astype(jnp.float32)
    key_heads_back = (
        (jnp.einsum("blhd,blrd->blhr", key_back, key_shared_float, precision=highest) / KR)
        .astype(jnp.bfloat16)
        .reshape(flat_count, -1)
    )
    value_heads_back = (
        (jnp.einsum("blhd,blrd->blhr", value_back, value_shared_float, precision=highest) / VR)
        .astype(jnp.bfloat16)
        .reshape(flat_count, -1)
    )
    key_shared_part = rotate(
        jnp.einsum("blhr,blhd->blrd", key_heads_float, key_back, precision=highest) / KR,
        local_places,
        -1.0,
    ).reshape(flat_count, -1)
    value_shared_part = (
        jnp.einsum("blhr,blhd->blrd", value_heads_float, value_back, precision=highest) / VR
    ).reshape(flat_count, -1)
    query_heads_back = (
        (jnp.einsum("blhd,blrd->blhr", query_back, query_rotated, precision=highest) / QR)
        .astype(jnp.bfloat16)
        .reshape(flat_count, -1)
    )
    query_shared_part = rotate(
        jnp.einsum("blhr,blhd->blrd", query_heads, query_back, precision=highest) / QR,
        local_places,
        -1.0,
    ).reshape(flat_count, -1)
    query_shared_sum, key_shared_sum, value_shared_sum = (
        lax.psum_scatter(
            query_shared_part.astype(jnp.bfloat16), "narrow", scatter_dimension=1, tiled=True
        ).astype(jnp.float32),
        lax.psum_scatter(
            key_shared_part.astype(jnp.bfloat16), "narrow", scatter_dimension=1, tiled=True
        ).astype(jnp.float32),
        lax.psum_scatter(
            value_shared_part.astype(jnp.bfloat16), "narrow", scatter_dimension=1, tiled=True
        ).astype(jnp.float32),
    )
    query_shared_back = query_shared_sum.astype(jnp.bfloat16)
    key_shared_back = key_shared_sum.astype(jnp.bfloat16)
    value_shared_back = value_shared_sum.astype(jnp.bfloat16)
    first_part = (
        back_through(query_heads_back, qheads_full)
        + back_through(key_heads_back, kheads_full)
        + back_through(value_heads_back, vheads_full)
    )
    first_part = (
        first_part
        + back_through(query_shared_back, qshared_cols)
        + back_through(key_shared_back, kshared_cols)
        + back_through(value_shared_back, vshared_cols)
    )
    first_back = lax.psum(first_part.astype(jnp.bfloat16), "narrow").astype(jnp.float32)
    source_part, prenorm_back = norm_back(
        first_back, source, first_inverse, prenorm_full.astype(jnp.float32)
    )
    tokens_gradient = (middle_gradient + source_part).reshape(batch_rows, local_tokens, model_width)
    summed = (
        lax.psum_scatter(prenorm_back, "wide", scatter_dimension=0, tiled=True),
        lax.psum_scatter(outer(normed, query_heads_back), "wide", scatter_dimension=0, tiled=True),
        lax.psum_scatter(outer(normed, query_shared_back), "wide", scatter_dimension=0, tiled=True),
        lax.psum_scatter(outer(normed, key_heads_back), "wide", scatter_dimension=0, tiled=True),
        lax.psum_scatter(outer(normed, key_shared_back), "wide", scatter_dimension=0, tiled=True),
        lax.psum_scatter(outer(normed, value_heads_back), "wide", scatter_dimension=0, tiled=True),
        lax.psum_scatter(outer(normed, value_shared_back), "wide", scatter_dimension=0, tiled=True),
        lax.psum_scatter(outer(mixture, branch_gradient), "wide", scatter_dimension=1, tiled=True),
        lax.psum_scatter(midnorm_back, "wide", scatter_dimension=0, tiled=True),
        lax.psum_scatter(outer(normed_mid, gate_gradient), "wide", scatter_dimension=0, tiled=True),
        lax.psum_scatter(outer(normed_mid, up_gradient), "wide", scatter_dimension=0, tiled=True),
        lax.psum_scatter(outer(hidden, upstream), "wide", scatter_dimension=1, tiled=True),
    )
    return (
        output,
        tokens_gradient,
        summed[0],
        summed[1],
        summed[2],
        summed[3],
        summed[4],
        summed[5],
        summed[6],
        summed[7],
        summed[8],
        summed[9],
        summed[10],
        summed[11],
    )


def solution(mesh):
    placed = (
        P(None, "wide", None),
        P(),
        P("wide"),
        P("wide", "narrow"),
        P("wide", "narrow"),
        P("wide", "narrow"),
        P("wide", "narrow"),
        P("wide", "narrow"),
        P("wide", "narrow"),
        P("narrow", "wide"),
        P("wide"),
        P("wide", "narrow"),
        P("wide", "narrow"),
        P("narrow", "wide"),
        P(None, "wide", None),
    )
    return jax.shard_map(
        on_device,
        mesh=mesh,
        in_specs=placed,
        out_specs=(
            P(None, "wide", None),
            P(None, "wide", None),
            P("wide"),
            P("wide", "narrow"),
            P("wide", "narrow"),
            P("wide", "narrow"),
            P("wide", "narrow"),
            P("wide", "narrow"),
            P("wide", "narrow"),
            P("narrow", "wide"),
            P("wide"),
            P("wide", "narrow"),
            P("wide", "narrow"),
            P("narrow", "wide"),
        ),
        check_vma=False,
    )
```

profile of v0, /device:TPU:0, one launch (start us, length us, event | category | flops | bytes accessed | tf_op | source)
XLA Modules:
  0.0 1511.2 jit_solution(97640536633949009)
XLA Ops:
  7.3 22.5 %all-gather = bf16[8,1,128]{2,1,0:T(2,128)(2,1)S(1)} all-gather(bf16[1,1,128]{2,1,0:T(2,128)(2,1)} %bitcast.386), channel_id=1, replica_groups=mesh['wide'=8,'narrow'=4] {'wide'}, dimensions={0}, use_global_device_ids=true | all-gather | bytes 2304 | tf_op jit(solution)/shard_map/all_gather | solution.py:123
  31.3 26.2 %all_gather.67 = bf16[1024,32]{0,1:T(8,128)(2,1)S(1)} all-gather(bf16[128,32]{0,1:T(8,128)(2,1)} %param.27), channel_id=1, replica_groups=mesh['wide'=8,'narrow'=4] {'wide'}, dimensions={0}, use_global_device_ids=true | all-gather | bytes 73728 | tf_op jit(solution)/shard_map/all_gather | solution.py:127
  58.1 5.8 all_gather.68
  65.5 26.0 %all_gather.66 = bf16[1024,8]{0,1:T(8,128)(2,1)S(1)} all-gather(bf16[128,8]{0,1:T(8,128)(2,1)S(1)} %copy-done.62), channel_id=1, replica_groups=mesh['wide'=8,'narrow'=4] {'wide'}, dimensions={0}, use_global_device_ids=true | all-gather | bytes 18432 | tf_op jit(solution)/shard_map/all_gather | solution.py:126
  97.4 26.3 %all_gather.74 = bf16[1024,32]{0,1:T(8,128)(2,1)S(1)} all-gather(bf16[128,32]{0,1:T(8,128)(2,1)S(1)} %copy-done.60), channel_id=1, replica_groups=mesh['wide'=8,'narrow'=4] {'wide'}, dimensions={0}, use_global_device_ids=true | all-gather | bytes 73728 | tf_op jit(solution)/shard_map/all_gather | solution.py:129
  124.3 5.8 all_gather.75
  131.3 26.0 %all_gather.73 = bf16[1024,8]{0,1:T(8,128)(2,1)S(1)} all-gather(bf16[128,8]{0,1:T(8,128)(2,1)S(1)} %copy-done.63), channel_id=1, replica_groups=mesh['wide'=8,'narrow'=4] {'wide'}, dimensions={0}, use_global_device_ids=true | all-gather | bytes 18432 | tf_op jit(solution)/shard_map/all_gather | solution.py:128
  162.9 27.0 %all_gather.71 = bf16[1024,96]{0,1:T(8,128)(2,1)S(1)} all-gather(bf16[128,96]{0,1:T(8,128)(2,1)S(1)} %copy-done.57), channel_id=1, replica_groups=mesh['wide'=8,'narrow'=4] {'wide'}, dimensions={0}, use_global_device_ids=true | all-gather | bytes 221184 | tf_op jit(solution)/shard_map/all_gather | solution.py:125
  189.9 8.5 all_gather.72
  203.2 26.2 %all_gather.70 = bf16[1024,24]{0,1:T(8,128)(2,1)S(1)} all-gather(bf16[128,24]{0,1:T(8,128)(2,1)S(1)} %copy-done.61), channel_id=1, replica_groups=mesh['wide'=8,'narrow'=4] {'wide'}, dimensions={0}, use_global_device_ids=true | all-gather | bytes 55296 | tf_op jit(solution)/shard_map/all_gather | solution.py:124
  230.3 6.2 fusion.74
  237.8 27.9 %all_gather.77 = bf16[256,1024]{1,0:T(8,128)(2,1)S(1)} all-gather(bf16[256,128]{1,0:T(8,128)(2,1)} %param.30), channel_id=1, replica_groups=mesh['wide'=8,'narrow'=4] {'wide'}, dimensions={1}, use_global_device_ids=true | all-gather | bytes 589824 | tf_op jit(solution)/shard_map/all_gather | solution.py:130
  265.8 28.4 %while.39 = (s32[]{:T(128)}, f32[4,4,128]{2,1,0:T(4,128)S(1)}, f32[4,4,128]{2,1,0:T(4,128)S(1)}, f32[4,4,128,64]{2,3,1,0:T(8,128)}, s32[2]{0:T(128)S(1)}, /*inde...) while((s32[]{:T(128)}, f32[4,4,128]{2,1,0:T(4,128)S(1)}, ...), condition=%wide.region_4.5_spmd.clone, body=%wide.region_1.4_spmd.clone.sunk | while | flops 280963712 | bytes 38305020 | solution.py:47
  299.6 16.2 %all-gather.1 = bf16[8,1,128]{2,1,0:T(2,128)(2,1)S(1)} all-gather(bf16[1,1,128]{2,1,0:T(2,128)(2,1)S(1)} %bitcast.387), channel_id=1, replica_groups=mesh['wide'=8,'narrow'=4] {'wide'}, dimensions={0}, use_global_device_ids=true | all-gather | bytes 2304 | tf_op jit(solution)/shard_map/all_gather | solution.py:131
  315.8 14.4 all-reduce.8.cloned.1.call-done
  333.3 43.2 %all-gather.14.cloned.1.call-done = bf16[1024,704]{0,1:T(8,128)(2,1)} async-done(((bf16[128,704]{0,1:T(8,128)(2,1)}), bf16[1024,704]{0,1:T(8,128)(2,1)}) %all-gather.14.cloned.1.call-update) | async-done | bytes 1441808 | tf_op jit(solution)/shard_map/all_gather | solution.py:132
  380.3 40.6 %all-gather.16.cloned.1.call-done = bf16[1024,704]{0,1:T(8,128)(2,1)} async-done(((bf16[128,704]{0,1:T(8,128)(2,1)}), bf16[1024,704]{0,1:T(8,128)(2,1)}) %all-gather.16.cloned.1.call-update) | async-done | bytes 1441808 | tf_op jit(solution)/shard_map/all_gather | solution.py:133
  424.6 40.6 %all-gather.18.cloned.1.call-done = bf16[704,1024]{1,0:T(8,128)(2,1)} async-done(((bf16[704,128]{1,0:T(8,128)(2,1)}), bf16[704,1024]{1,0:T(8,128)(2,1)}) %all-gather.18.cloned.1.call-update) | async-done | bytes 1441808 | tf_op jit(solution)/shard_map/all_gather | solution.py:134
  465.2 5.0 multiply_convert_fusion.2
  475.2 33.6 %all-reduce.10.cloned.1.call-done = bf16[512,1024]{1,0:T(8,128)(2,1)} async-done(((bf16[512,1024]{1,0:T(8,128)(2,1)}), bf16[512,1024]{1,0:T(8,128)(2,1)}) %all-reduce.10.cloned.1.call-update) | async-done | bytes 1048592 | tf_op jit(solution)/shard_map/psum | solution.py:280
  515.8 26.9 %while.40 = (s32[]{:T(128)}, f32[4,128,4,64]{1,3,2,0:T(8,128)}, s32[2]{0:T(128)S(1)}, bf16[4,1024,256]{1,2,0:T(8,128)(2,1)}, s32[4,1024]{1,0:T(4,128)S(1)}, /*in...) while((s32[]{:T(128)}, f32[4,128,4,64]{1,3,2,0:T(8,128)}, ...), condition=%wide.region_12.13_spmd.clone, body=%wide.region_11.12_spmd.clone.sunk | while | flops 409928320 | bytes 18005344 | solution.py:47
  523.9 5.4 fusion.245
  537.2 5.5 fusion.245
  545.2 6.9 fusion.116
  557.5 27.2 %all_gather.83 = f32[4,4,1024]{2,1,0:T(4,128)} all-gather(f32[4,4,128]{2,1,0:T(4,128)S(1)} %get-tuple-element.1053), channel_id=1, replica_groups=mesh['wide'=8,'narrow'=4] {'wide'}, dimensions={2}, use_global_device_ids=true | all-gather | bytes 73728 | tf_op jit(solution)/shard_map/all_gather | solution.py:344
  592.2 27.6 %all_gather.85 = f32[4,4,1024]{2,0,1:T(4,128)} all-gather(f32[4,4,128]{2,0,1:T(4,128)S(1)} %bitcast.381), channel_id=1, replica_groups=mesh['wide'=8,'narrow'=4] {'wide'}, dimensions={2}, use_global_device_ids=true | all-gather | bytes 73728 | tf_op jit(solution)/shard_map/all_gather | solution.py:345
  624.3 6.5 all-gather.20.cloned.1.call-done
  630.8 51.2 %all-gather.22.cloned.1.call-done = bf16[4,1024,256]{1,2,0:T(8,128)(2,1)} async-done(((bf16[4,128,256]{1,2,0:T(8,128)(2,1)}), bf16[4,1024,256]{1,2,0:T(8,128)(2,1)}) %all-gather.22.cloned.1.call-update) | async-done | bytes 2097168 | tf_op jit(solution)/shard_map/all_gather | solution.py:399
  682.0 40.8 %while.41 = (s32[]{:T(128)}, f32[4,128,4,64]{1,3,2,0:T(8,128)}, f32[4,128,4,64]{1,3,2,0:T(8,128)}, s32[2]{0:T(128)S(1)}, bf16[4,1024,256]{1,2,0:T(8,128)(2,1)}, ...) while((s32[]{:T(128)}, f32[4,128,4,64]{1,3,2,0:T(8,128)}, ...), condition=%wide.region_14.15_spmd.clone, body=%wide.region_13.14_spmd.clone.sunk | while | flops 548602496 | bytes 24837368 | solution.py:47
  695.7 6.5 fusion.254
  710.8 4.4 fusion.255
  716.0 6.6 fusion.254
  747.6 14.9 reduce-scatter.16.cloned.1.call-done
  765.1 20.1 %reduce-scatter.18.cloned.1.call-done = bf16[512,32]{0,1:T(8,128)(2,1)} async-done(((bf16[512,128]{0,1:T(8,128)(2,1)}), bf16[512,32]{0,1:T(8,128)(2,1)}) %reduce-scatter.18.cloned.1.call-update) | async-done | bytes 32784 | tf_op jit(solution)/shard_map/reduce_scatter | solution.py:447
  785.2 5.7 add_convert_fusion
  814.7 28.0 %all-reduce.12.cloned.1.call-done = (bf16[512,1024]{1,0:T(8,128)(2,1)}, bf16[512,1024]{1,0:T(8,128)(2,1)}) async-done(((bf16[512,1024]{1,0:T(8,128)(2,1)}, bf16[512,1024]{1,0:T(8,128)(2,1)}), (bf16[512,1024]{1,0:T(8,128)(2,1)}, bf16[512,1024]{1,0:T(8,128)(2,1)})) %all-reduce.12.cloned.1.call-update) | async-done | bytes 2097168 | tf_op jit(solution)/shard_map/psum | solution.py:265
  844.7 21.6 %all-reduce.2 = (f32[1024]{0:T(1024)S(1)}, f32[1024]{0:T(1024)S(1)}) all-reduce(f32[1024]{0:T(1024)S(1)} %get-tuple-element.469, f32[1024]{0:T(1024)S(1)} %get-tuple-element.467), channel_id=5, replica_groups=mesh['wide'=8,'narrow'=4] {'wide'}, use_global_device_ids=true, to_apply=%region_21.22.clone | all-reduce | flops 2048 | bytes 16384
  867.6 4.4 fusion.56
  872.0 32.8 %reduce-scatter.20.cloned.1.call-done = f32[128,24]{0,1:T(8,128)} async-done(((f32[1024,24]{0,1:T(8,128)}), f32[128,24]{0,1:T(8,128)}) %reduce-scatter.20.cloned.1.call-update) | async-done | bytes 12304 | tf_op jit(solution)/shard_map/reduce_scatter | solution.py:472
  904.8 65.2 %reduce-scatter.22.cloned.1.call-done = f32[128,96]{0,1:T(8,128)} async-done(((f32[1024,96]{0,1:T(8,128)}), f32[128,96]{0,1:T(8,128)}) %reduce-scatter.22.cloned.1.call-update) | async-done | bytes 49168 | tf_op jit(solution)/shard_map/reduce_scatter | solution.py:473
  970.0 67.2 %reduce-scatter.32.cloned.1.call-done = f32[256,128]{1,0:T(8,128)} async-done(((f32[256,1024]{1,0:T(8,128)}), f32[256,128]{1,0:T(8,128)}) %reduce-scatter.32.cloned.1.call-update) | async-done | bytes 131088 | tf_op jit(solution)/shard_map/reduce_scatter | solution.py:478
  1037.2 56.0 %reduce-scatter.24.cloned.1.call-done = f32[128,8]{0,1:T(8,128)} async-done(((f32[1024,8]{0,1:T(8,128)}), f32[128,8]{0,1:T(8,128)}) %reduce-scatter.24.cloned.1.call-update) | async-done | bytes 4112 | tf_op jit(solution)/shard_map/reduce_scatter | solution.py:474
  1093.3 56.1 %reduce-scatter.28.cloned.1.call-done = f32[128,8]{0,1:T(8,128)} async-done(((f32[1024,8]{0,1:T(8,128)}), f32[128,8]{0,1:T(8,128)}) %reduce-scatter.28.cloned.1.call-update) | async-done | bytes 4112 | tf_op jit(solution)/shard_map/reduce_scatter | solution.py:476
  1149.4 64.2 %reduce-scatter.30.cloned.1.call-done = f32[128,32]{0,1:T(8,128)} async-done(((f32[1024,32]{0,1:T(8,128)}), f32[128,32]{0,1:T(8,128)}) %reduce-scatter.30.cloned.1.call-update) | async-done | bytes 16400 | tf_op jit(solution)/shard_map/reduce_scatter | solution.py:477
  1213.6 64.1 %reduce-scatter.26.cloned.1.call-done = f32[128,32]{0,1:T(8,128)} async-done(((f32[1024,32]{0,1:T(8,128)}), f32[128,32]{0,1:T(8,128)}) %reduce-scatter.26.cloned.1.call-update) | async-done | bytes 16400 | tf_op jit(solution)/shard_map/reduce_scatter | solution.py:475
  1277.7 75.5 %reduce-scatter.34.cloned.1.call-done = f32[128,704]{0,1:T(8,128)} async-done(((f32[1024,704]{0,1:T(8,128)}), f32[128,704]{0,1:T(8,128)}) %reduce-scatter.34.cloned.1.call-update) | async-done | bytes 360464 | tf_op jit(solution)/shard_map/reduce_scatter | solution.py:480
  1353.2 75.6 %reduce-scatter.36.cloned.1.call-done = f32[128,704]{0,1:T(8,128)} async-done(((f32[1024,704]{0,1:T(8,128)}), f32[128,704]{0,1:T(8,128)}) %reduce-scatter.36.cloned.1.call-update) | async-done | bytes 360464 | tf_op jit(solution)/shard_map/reduce_scatter | solution.py:481
  1428.8 75.6 %reduce-scatter.38.cloned.1.call-done = f32[704,128]{1,0:T(8,128)} async-done(((f32[704,1024]{1,0:T(8,128)}), f32[704,128]{1,0:T(8,128)}) %reduce-scatter.38.cloned.1.call-update) | async-done | bytes 360464 | tf_op jit(solution)/shard_map/reduce_scatter | solution.py:482
  (379 shorter events, 188.1 us)
Async XLA Ops:
  7.2 56.8 %copy-start.1 = (bf16[4,128,1024]{2,1,0:T(8,128)(2,1)S(1)}, bf16[4,128,1024]{2,1,0:T(8,128)(2,1)}, u32[]{:S(2)}) copy-start(bf16[4,128,1024]{2,1,0:T(8,128)(2,1)} %param.21) | copy-start | bytes 3145732
  7.2 258.6 %all-gather.10.cloned.1.call-start = ((), (), s32[]{:S(2)}) async-start(), calls=%async_computation.13 | async-start | bytes 2359296 | tf_op jit(solution)/shard_map/all_gather | solution.py:245
  29.7 35.4 %copy-start.50 = (f32[8,1,128]{2,1,0:T(1,128)}, f32[8,1,128]{2,1,0:T(1,128)S(1)}, u32[]{:S(2)}) copy-start(f32[8,1,128]{2,1,0:T(1,128)S(1)} %convert_element_type.219) | copy-start | bytes 12292
  31.2 32.8 %copy-start.58 = (f32[4,128]{1,0:T(4,128)}, f32[4,128]{1,0:T(4,128)S(1)}, u32[]{:S(2)}) copy-start(f32[4,128]{1,0:T(4,128)S(1)} %fusion.65) | copy-start | bytes 6148
  31.3 33.9 %copy-start.55 = (f32[512]{0:T(512)}, f32[512]{0:T(512)S(1)}, u32[]{:S(2)}) copy-start(f32[512]{0:T(512)S(1)} %get-tuple-element.573) | copy-start | bytes 6148
  64.0 490.3 %copy-start.46 = (f32[128,32]{0,1:T(8,128)}, f32[128,32]{0,1:T(8,128)S(1)}, u32[]{:S(2)}) copy-start(f32[128,32]{0,1:T(8,128)S(1)} %get-tuple-element.574) | copy-start | bytes 49156
  64.3 165.1 %copy-start.2 = (bf16[4,128,1024]{2,1,0:T(8,128)(2,1)}, bf16[4,128,1024]{2,1,0:T(8,128)(2,1)S(1)}, u32[]{:S(2)}) copy-start(bf16[4,128,1024]{2,1,0:T(8,128)(2,1)S(1)} %fusion.67) | copy-start | bytes 3145732
  65.1 30.2 %copy-start.39 = (bf16[4,128,2,64]{3,2,1,0:T(2,128)(2,1)}, bf16[4,128,2,64]{3,2,1,0:T(2,128)(2,1)S(1)}, u32[]{:S(2)}) copy-start(bf16[4,128,2,64]{3,2,1,0:T(2,128)(2,1)S(1)} %copy.143) | copy-start | bytes 393220
  91.5 5.8 copy-start.44
  91.5 5.9 copy-start.60
  95.3 36.0 %copy-start.63 = (bf16[128,8]{0,1:T(8,128)(2,1)S(1)}, bf16[128,8]{0,1:T(8,128)(2,1)}, u32[]{:S(2)}) copy-start(bf16[128,8]{0,1:T(8,128)(2,1)} %param.28) | copy-start | bytes 6148
  97.3 168.5 %all-gather.12.cloned.1.call-start = ((), (), s32[]{:S(2)}) async-start(), calls=%async_computation.14 | async-start | bytes 2359296 | tf_op jit(solution)/shard_map/all_gather | solution.py:246
  158.2 40.2 %copy-start.41 = (bf16[4,128,4,2]{2,3,1,0:T(2,128)(2,1)}, bf16[4,128,4,2]{2,3,1,0:T(2,128)(2,1)S(1)}, u32[]{:S(2)}) copy-start(bf16[4,128,4,2]{2,3,1,0:T(2,128)(2,1)S(1)} %copy.148) | copy-start | bytes 24580
  162.8 167.4 %all-reduce.8.cloned.1.call-start = ((), (), s32[]{:S(2)}) async-start(), calls=%async_computation.15 | async-start | bytes 2097152 | tf_op jit(solution)/shard_map/psum | solution.py:253
  189.9 8.5 copy-start.29
  230.3 7.5 copy-start.10
  230.3 7.5 copy-start.31
  265.8 29.9 %copy-start.14 = (bf16[256,1024]{1,0:T(8,128)(2,1)}, bf16[256,1024]{1,0:T(8,128)(2,1)S(1)}, u32[]{:S(2)}) copy-start(bf16[256,1024]{1,0:T(8,128)(2,1)S(1)} %all_gather.77) | copy-start | bytes 1572868
  297.8 78.7 %all-gather.14.cloned.1.call-start = ((), (), s32[]{:S(2)}) async-start(), calls=%async_computation.16 | async-start | bytes 1622016 | tf_op jit(solution)/shard_map/all_gather | solution.py:132
  298.4 122.5 %all-gather.16.cloned.1.call-start = ((), (), s32[]{:S(2)}) async-start(), calls=%async_computation.17 | async-start | bytes 1622016 | tf_op jit(solution)/shard_map/all_gather | solution.py:133
  299.0 166.2 %all-gather.18.cloned.1.call-start = ((), (), s32[]{:S(2)}) async-start(), calls=%async_computation.18 | async-start | bytes 1622016 | tf_op jit(solution)/shard_map/all_gather | solution.py:134
  299.6 209.2 %all-reduce.10.cloned.1.call-start = ((), (), s32[]{:S(2)}) async-start(), calls=%async_computation.19 | async-start | bytes 2097152 | tf_op jit(solution)/shard_map/psum | solution.py:280
  474.2 147.4 %reduce-scatter.14.cloned.1.call-start = ((), (), s32[]{:S(2)}) async-start(), calls=%async_computation.22 | async-start | bytes 491520 | tf_op jit(solution)/shard_map/reduce_scatter | solution.py:441
  542.7 9.4 copy-start.4
  554.4 30.3 %copy-start.19 = (bf16[512,704]{0,1:T(8,128)(2,1)S(1)}, bf16[512,704]{0,1:T(8,128)(2,1)}, u32[]{:S(2)}) copy-start(bf16[512,704]{0,1:T(8,128)(2,1)} %get-tuple-element.559) | copy-start | bytes 2162692
  555.6 75.2 %all-gather.20.cloned.1.call-start = ((), (), s32[]{:S(2)}) async-start(), calls=%async_computation.20 | async-start | bytes 2359296 | tf_op jit(solution)/shard_map/all_gather | solution.py:396
  556.3 125.7 %all-gather.22.cloned.1.call-start = ((), (), s32[]{:S(2)}) async-start(), calls=%async_computation.21 | async-start | bytes 2359296 | tf_op jit(solution)/shard_map/all_gather | solution.py:399
  557.4 205.1 %reduce-scatter.16.cloned.1.call-start = ((), (), s32[]{:S(2)}) async-start(), calls=%async_computation.23 | async-start | bytes 163840 | tf_op jit(solution)/shard_map/reduce_scatter | solution.py:444
  592.2 29.4 %copy-start.30 = (bf16[1024,96]{0,1:T(8,128)(2,1)S(1)}, bf16[1024,96]{0,1:T(8,128)(2,1)}, u32[]{:S(2)}) copy-start(bf16[1024,96]{0,1:T(8,128)(2,1)} %copy-done.29) | copy-start | bytes 589828
  619.8 62.2 %copy-start.9 = (bf16[4,128,4,64]{1,3,2,0:T(8,128)(2,1)S(1)}, bf16[4,128,4,64]{1,3,2,0:T(8,128)(2,1)}, u32[]{:S(2)}) copy-start(bf16[4,128,4,64]{1,3,2,0:T(8,128)(2,1)} %copy.144) | copy-start | bytes 786436
  732.9 7.6 copy-start.45
  744.6 17.9 %copy-start.35 = (bf16[1024,32]{0,1:T(8,128)(2,1)S(1)}, bf16[1024,32]{0,1:T(8,128)(2,1)}, u32[]{:S(2)}) copy-start(bf16[1024,32]{0,1:T(8,128)(2,1)} %copy-done.34) | copy-start | bytes 196612
  744.7 40.5 %reduce-scatter.18.cloned.1.call-start = ((), (), s32[]{:S(2)}) async-start(), calls=%async_computation.24 | async-start | bytes 163840 | tf_op jit(solution)/shard_map/reduce_scatter | solution.py:447
  745.7 39.4 %copy-start.33 = (bf16[1024,32]{0,1:T(8,128)(2,1)S(1)}, bf16[1024,32]{0,1:T(8,128)(2,1)}, u32[]{:S(2)}) copy-start(bf16[1024,32]{0,1:T(8,128)(2,1)} %copy-done.32) | copy-start | bytes 196612
  747.6 95.1 %all-reduce.12.cloned.1.call-start = ((), (), s32[]{:S(2)}) async-start(), calls=%async_computation.35 | async-start | bytes 4194304 | tf_op jit(solution)/shard_map/psum | solution.py:265
  790.9 113.9 %reduce-scatter.20.cloned.1.call-start = ((), (), s32[]{:S(2)}) async-start(), calls=%async_computation.25 | async-start | bytes 110592 | tf_op jit(solution)/shard_map/reduce_scatter | solution.py:472
  793.0 177.0 %reduce-scatter.22.cloned.1.call-start = ((), (), s32[]{:S(2)}) async-start(), calls=%async_computation.26 | async-start | bytes 442368 | tf_op jit(solution)/shard_map/reduce_scatter | solution.py:473
  794.2 243.0 %reduce-scatter.32.cloned.1.call-start = ((), (), s32[]{:S(2)}) async-start(), calls=%async_computation.31 | async-start | bytes 1179648 | tf_op jit(solution)/shard_map/reduce_scatter | solution.py:478
  797.3 296.0 %reduce-scatter.24.cloned.1.call-start = ((), (), s32[]{:S(2)}) async-start(), calls=%async_computation.27 | async-start | bytes 36864 | tf_op jit(solution)/shard_map/reduce_scatter | solution.py:474
  798.3 351.1 %reduce-scatter.28.cloned.1.call-start = ((), (), s32[]{:S(2)}) async-start(), calls=%async_computation.29 | async-start | bytes 36864 | tf_op jit(solution)/shard_map/reduce_scatter | solution.py:476
  799.2 414.4 %reduce-scatter.30.cloned.1.call-start = ((), (), s32[]{:S(2)}) async-start(), calls=%async_computation.30 | async-start | bytes 147456 | tf_op jit(solution)/shard_map/reduce_scatter | solution.py:477
  800.5 477.2 %reduce-scatter.26.cloned.1.call-start = ((), (), s32[]{:S(2)}) async-start(), calls=%async_computation.28 | async-start | bytes 147456 | tf_op jit(solution)/shard_map/reduce_scatter | solution.py:475
  801.5 551.7 %reduce-scatter.34.cloned.1.call-start = ((), (), s32[]{:S(2)}) async-start(), calls=%async_computation.32 | async-start | bytes 3244032 | tf_op jit(solution)/shard_map/reduce_scatter | solution.py:480
  805.2 623.6 %reduce-scatter.36.cloned.1.call-start = ((), (), s32[]{:S(2)}) async-start(), calls=%async_computation.33 | async-start | bytes 3244032 | tf_op jit(solution)/shard_map/reduce_scatter | solution.py:481
  808.8 695.6 %reduce-scatter.38.cloned.1.call-start = ((), (), s32[]{:S(2)}) async-start(), calls=%async_computation.34 | async-start | bytes 3244032 | tf_op jit(solution)/shard_map/reduce_scatter | solution.py:482
  812.7 29.9 %copy-start.51 = (f32[8,1,128]{2,1,0:T(1,128)S(1)}, f32[8,1,128]{2,1,0:T(1,128)}, u32[]{:S(2)}) copy-start(f32[8,1,128]{2,1,0:T(1,128)} %copy-done.50) | copy-start | bytes 12292
  812.7 29.9 %copy-start.56 = (f32[512]{0:T(512)S(1)}, f32[512]{0:T(512)}, u32[]{:S(2)}) copy-start(f32[512]{0:T(512)} %copy-done.55) | copy-start | bytes 6148
  812.7 54.8 %copy-start.6 = (f32[512,1024]{1,0:T(8,128)S(1)}, f32[512,1024]{1,0:T(8,128)}, u32[]{:S(2)}) copy-start(f32[512,1024]{1,0:T(8,128)} %copy-done.5) | copy-start | bytes 6291460
  (48 other events, 119.1 us)
Sparse Core Ops, SparseCore 0:
  97.4 48.3 all-gather.9
  163.0 49.0 all-gather.11
  297.9 32.2 all-reduce.7
  332.3 44.1 all-gather.13
  378.6 42.1 all-gather.15
  423.0 42.1 all-gather.17
  474.3 34.4 all-reduce.9
  555.7 21.1 reduce-scatter.13
  579.0 51.7 all-gather.19
  632.7 49.2 all-gather.21
  744.8 17.7 reduce-scatter.15
  765.5 19.5 reduce-scatter.17
  791.0 51.5 all-reduce.11
  846.7 58.0 reduce-scatter.19
  908.9 61.1 reduce-scatter.21
  974.2 62.9 reduce-scatter.31
  1040.8 52.4 reduce-scatter.23
  1096.8 52.5 reduce-scatter.27
  1153.3 60.2 reduce-scatter.29
  1217.3 60.2 reduce-scatter.25
  1281.8 71.3 reduce-scatter.33
  1357.4 71.3 reduce-scatter.35
  1432.9 71.3 reduce-scatter.37
where the time goes:
time: 1520 us; the launch traced here: 1510 us
  waiting for transfers between devices  928 us (61%)
  blocking collectives  321 us (21%)
  matrix products  149 us (10%)
  local copies, waits for them, and re-layouts  60.6 us (4%)
  other arithmetic  31.2 us (2%)
  between operations  15.9 us (1%)
    reduce_scatter x1, waiting for transfers between devices, on_device(): lax.psum_scatter(outer(hidden, upstream), 'wide', scatter_dimension=1, ti...  75.6 us
    reduce_scatter x1, waiting for transfers between devices, on_device(): lax.psum_scatter(outer(normed_mid, up_gradient), 'wide', scatter_dimensio...  75.6 us
    reduce_scatter x1, waiting for transfers between devices, on_device(): lax.psum_scatter(outer(normed_mid, gate_gradient), 'wide', scatter_dimens...  75.5 us
    reduce_scatter x1, waiting for transfers between devices, on_device(): lax.psum_scatter(outer(mixture, branch_gradient), 'wide', scatter_dimensi...  67.2 us
    reduce_scatter x1, waiting for transfers between devices, on_device(): lax.psum_scatter(outer(normed, query_shared_back), 'wide', scatter_dimens...  65.2 us
    reduce_scatter x1, waiting for transfers between devices, on_device(): lax.psum_scatter(outer(normed, value_shared_back), 'wide', scatter_dimens...  64.2 us
    reduce_scatter x1, waiting for transfers between devices, on_device(): lax.psum_scatter(outer(normed, key_shared_back), 'wide', scatter_dimensio...  64.1 us
    reduce_scatter x1, waiting for transfers between devices, on_device(): lax.psum_scatter(outer(normed, value_heads_back), 'wide', scatter_dimensi...  56.1 us
  transfers between devices with their start and end apart: 23, of which 20 were waited for; matrix products, arithmetic and copies ran while one was open for 5% of the time, Pallas kernels for 0%

commit v1 on v0

v1 whole, which is shorter than its diff:
```python
import math
from types import SimpleNamespace

import jax
import jax.numpy as jnp
from jax import lax
from jax.experimental import pallas as pl
from jax.experimental.pallas import tpu as pltpu
from jax.sharding import PartitionSpec as P

DH = 64
QR = 6
KR = 2
VR = 2
LANES = 128

epsilon = 1e-06
masked_score = -1e30
MESH = pl.DeviceIdType.MESH
f32 = jnp.float32
bf16 = jnp.bfloat16


def dot_nn(a, b):
    return lax.dot_general(a, b, (((1,), (0,)), ((), ())), preferred_element_type=f32)


def dot_nt(a, b):
    return lax.dot_general(a, b, (((1,), (1,)), ((), ())), preferred_element_type=f32)


def dot_tn(a, b):
    return lax.dot_general(a, b, (((0,), (0,)), ((), ())), preferred_element_type=f32)


def lane_iota(rows, cols=LANES):
    return lax.broadcasted_iota(jnp.int32, (rows, cols), 1)


def row_iota(rows, cols=LANES):
    return lax.broadcasted_iota(jnp.int32, (rows, cols), 0)


def place_lanes(pieces):
    rows = pieces[0][0].shape[0]
    lane = lane_iota(rows)
    result = jnp.zeros((rows, LANES), f32)
    for tile, start, to, count in pieces:
        shift = (to - start) % LANES
        moved = pltpu.roll(tile, shift, 1) if shift else tile
        result = jnp.where((lane >= to) & (lane < to + count), moved, result)
    return result


def canonical_pieces(tiles, width, first, count, start, to):
    pieces = []
    while count:
        part, inside = divmod(first, width)
        take = min(count, width - inside)
        pieces.append((tiles[part], start + inside, to, take))
        first, to, count = first + take, to + take, count - take
    return pieces


def both_halves(tile):
    low = lane_iota(tile.shape[0]) < DH
    turned = pltpu.roll(tile, DH, 1)
    return jnp.where(low, tile, turned), jnp.where(low, turned, tile)


def swap_quarters(tile):
    low = lane_iota(tile.shape[0]) % DH < DH // 2
    return jnp.where(low, pltpu.roll(tile, LANES - DH // 2, 1), pltpu.roll(tile, DH // 2, 1))


def stack_pair(tile):
    low = lane_iota(tile.shape[0]) < DH
    zero = jnp.zeros_like(tile)
    return jnp.concatenate([jnp.where(low, tile, zero), jnp.where(low, zero, tile)], axis=0)


def unstack_pair(rows):
    half = rows.shape[0] // 2
    low = lane_iota(half) < DH
    return jnp.where(low, rows[:half], rows[half:])


def fold_halves(tile):
    return tile + pltpu.roll(tile, DH, 1)


def row_scale(values):
    return lax.rsqrt(jnp.mean(values * values, axis=-1, keepdims=True) + epsilon)


def make_layout(W, N, T, D, F, L, heads):
    lay = SimpleNamespace()
    lay.W, lay.N, lay.T, lay.D, lay.F, lay.L, lay.heads = W, N, T, D, F, L, heads
    lay.A = W // 2
    lay.RW = D // W
    lay.M = N * T
    lay.FM = F // LANES * LANES
    lay.FP = lay.FM + LANES
    lay.pairs = heads // 2
    lay.KB = L if L <= 1024 else 512
    lay.NB = L // lay.KB
    lay.SQ = QR * DH // N
    lay.SK = KR * DH // N
    lay.HQ = heads * QR // N
    lay.HK = heads * KR // N
    lay.oK, lay.oV = 0, lay.SK
    lay.oq = 2 * lay.SK
    lay.ok = lay.oq + lay.HQ
    lay.ov = lay.ok + lay.HK
    lay.og = lay.ov + lay.HK
    assert N == 4 and W % 8 == 0 and T == LANES and D == heads * DH == 1024
    assert F % LANES == DH and lay.SQ <= LANES and lay.og + 2 <= LANES
    return lay


def scratch_list(y):
    W, N, T, D, L, A, RW, M = y.W, y.N, y.T, y.D, y.L, y.A, y.RW, y.M
    vm = lambda *shape, kind=bf16: pltpu.VMEM(shape, kind)
    GUc = 2 * y.FM + LANES
    return dict(
        WQ=vm(N, D, 256),
        PT=vm(N, D, 256),
        GU=vm(D, GUc),
        DT=vm(D, y.FP),
        KVF=vm(L, 384),
        KP=vm(y.pairs, y.KB, LANES),
        VP=vm(y.pairs, y.KB, LANES),
        EQ=vm(QR, 256, D),
        EK=vm(4, LANES, D),
        BIAS=vm(T, y.KB, kind=f32),
        DOC=vm(T, LANES, kind=f32),
        ROPE=vm(2, T, LANES, kind=f32),
        GAIN=vm(8, D, kind=f32),
        QROT=vm(QR, T, LANES, kind=f32),
        QH=vm(T, 256),
        QP=vm(y.pairs, T, LANES),
        ATT=vm(y.pairs, T, LANES, kind=f32),
        LSE=vm(y.pairs, 2 * T, LANES, kind=f32),
        RUN=vm(y.pairs, 2 * T, LANES, kind=f32),
        MIX=vm(M, D),
        NORM=vm(M, D),
        MID=vm(M, D, kind=f32),
        NM=vm(M, D),
        R2=vm(M, LANES, kind=f32),
        HID=vm(M, y.FP),
        GG=vm(M, GUc),
        MB=vm(M, D),
        MBC=vm(2, T, D),
        MBX=vm(T, D),
        MBS=vm(T, D),
        OP=vm(M, D),
        OPC=vm(2, T, D),
        OPX=vm(T, D),
        OPS=vm(T, D),
        BG=vm(M, D),
        MG=vm(T, D, kind=f32),
        DO=vm(y.pairs, T, LANES),
        QB=vm(y.pairs, T, LANES, kind=f32),
        DKS=vm(4, y.KB, LANES, kind=f32),
        DHD=vm(y.KB, LANES, kind=f32),
        DKVY=vm(A * T, 384),
        DKVR=vm((A - 1) * T, 384),
        DKVO=vm(T, 384, kind=f32),
        QGS=vm(N, T, 256),
        QGR=vm(N, T, 256),
        GS=vm(8, D, kind=f32),
        GR=vm(3, 8, D, kind=f32),
        YGU=vm(A * RW, GUc),
        RGU=vm((A - 1) * RW, GUc),
        PDT=vm(D, y.FP),
        YDT=vm(A * RW, y.FP),
        RDT=vm((A - 1) * RW, y.FP),
        PPT=vm(D, 256),
        YPT=vm(A * RW, 256),
        RPT=vm((A - 1) * RW, 256),
        PQ=vm(D, 256),
        YQ=vm(A * RW, 256),
        RQ=vm((A - 1) * RW, 256),
    )


def block_kernel(y, names, *refs):
    tok, docs, wq_own, gu_own, dt_own, pt_own, cot = refs[:7]
    o_out, o_tok, o_gu, o_dt, o_pt, o_q = refs[7:13]
    s = SimpleNamespace(**dict(zip(names, refs[13:])))
    ssem, rsem = refs[13 + len(names) :]
    W, N, T, D, F, L, A, RW, M = y.W, y.N, y.T, y.D, y.F, y.L, y.A, y.RW, y.M
    FM, FP, KB, pairs = y.FM, y.FP, y.KB, y.pairs
    w = lax.axis_index("wide")
    n = lax.axis_index("narrow")
    zi, yi = w // 2, w % 2
    xo, co = n // 2, n % 2
    y_peer = (zi * 2 + 1 - yi, n)
    c_peer = (w, xo * 2 + 1 - co)
    x_peer = (w, (1 - xo) * 2 + co)
    d_peer = (w, (1 - xo) * 2 + 1 - co)
    turn = lambda step: (zi + step) % A
    z_peer = lambda step: (turn(step) * 2 + yi, n)
    narrow_peers = (c_peer, x_peer, d_peer)
    taken = [0]

    def take(count=1):
        first = taken[0]
        taken[0] += count
        assert taken[0] <= ssem.shape[0]
        return first

    def remote(src, dst, k, peer):
        return pltpu.make_async_remote_copy(
            src_ref=src,
            dst_ref=dst,
            send_sem=ssem.at[k],
            recv_sem=rsem.at[k],
            device_id=peer,
            device_id_type=MESH,
        )

    pending = []

    def send(src, dst, k, peer, started=pending):
        copy = remote(src, dst, k, peer)
        copy.start()
        started.append(copy)

    def arrive(dst, k):
        remote(dst, dst, k, y_peer).wait_recv()

    def rows(ref, first, count):
        return ref.at[pl.ds(pl.multiple_of(first, 16), count)]

    barrier = pltpu.get_barrier_semaphore()
    peers = [y_peer, *narrow_peers] + [z_peer(step) for step in range(1, A)]
    for peer in peers:
        pl.semaphore_signal(barrier, inc=1, device_id=peer, device_id_type=MESH)
    pl.semaphore_wait(barrier, len(peers))

    class Gather:
        def __init__(self, ref, count, first=0, size=None):
            self.ref, self.count, self.first = ref, count, first
            self.size = count if size is None else size
            self.kz, self.ky = take(A), take(A)
            self.started = []

        def sent(self):
            for copy in self.started:
                copy.wait_send()

        def part(self, wide):
            return rows(self.ref, wide * self.count + self.first, self.size)

        def start(self):
            for step in range(1, A):
                send(self.part(w), self.part(w), self.kz + step, z_peer(step), self.started)

        def start_y(self, step):
            part = self.part(turn(-step) * 2 + yi)
            send(part, part, self.ky + step, y_peer, self.started)

        def forward(self, step):
            arrive(self.part(turn(-step) * 2 + yi), self.kz + step)
            self.start_y(step)

        def forward_all(self):
            for step in range(1, A):
                self.forward(step)

        def landed(self, step):
            arrive(self.part(turn(-step) * 2 + 1 - yi), self.ky + step)

        def landed_all(self):
            for step in range(A):
                self.landed(step)

    class Spread:
        def __init__(self, ref):
            self.ref = ref
            self.kx, self.kc, self.kd = take(A), take(A), take(A)

        def part(self, owner, step):
            return rows(self.ref.at[owner], turn(-step) * 2 * RW, 2 * RW)

        def start(self, step):
            send(self.part(n, step), self.part(n, step), self.kx + step, x_peer)
            send(self.part(n, step), self.part(n, step), self.kc + step, c_peer)

        def forward(self, step):
            part = self.part(x_peer[1], step)
            arrive(part, self.kx + step)
            send(part, part, self.kd + step, c_peer)

        def landed(self, step):
            arrive(self.part(c_peer[1], step), self.kc + step)
            arrive(self.part(d_peer[1], step), self.kd + step)

    class Share:
        def __init__(self, ref, chunks):
            self.ref, self.chunks = ref, chunks
            self.kx, self.kc, self.kd = take(chunks), take(chunks), take(chunks)
            self.width = D // chunks

        def part(self, owner, chunk):
            lanes = pl.ds(pl.multiple_of(chunk * self.width, LANES), self.width)
            return self.ref.at[pl.ds(pl.multiple_of(owner * T, T), T), lanes]

        def start(self, chunk):
            send(self.part(n, chunk), self.part(n, chunk), self.kx + chunk, x_peer)
            send(self.part(n, chunk), self.part(n, chunk), self.kc + chunk, c_peer)

        def forward(self, chunk):
            part = self.part(x_peer[1], chunk)
            arrive(part, self.kx + chunk)
            send(part, part, self.kd + chunk, c_peer)

        def landed(self, chunk):
            arrive(self.part(c_peer[1], chunk), self.kc + chunk)
            arrive(self.part(d_peer[1], chunk), self.kd + chunk)

        def finish(self):
            for chunk in range(self.chunks):
                self.forward(chunk)
            for chunk in range(self.chunks):
                self.landed(chunk)

    class NarrowSum:
        def __init__(self, part_ref, core_ref, x_ref, send_ref):
            self.ref, self.core, self.x, self.out = part_ref, core_ref, x_ref, send_ref
            self.kc, self.kx = take(2), take(1)

        def part(self, owner):
            return rows(self.ref, owner * T, T)

        def start(self, far):
            owner = ((1 - xo) if far else xo) * 2 + 1 - co
            send(self.part(owner), self.core.at[int(far)], self.kc + int(far), c_peer)

        def pass_on(self):
            arrive(self.core.at[1], self.kc + 1)
            total = self.part((1 - xo) * 2 + co)[...].astype(f32) + self.core[1].astype(f32)
            self.out[...] = total.astype(bf16)
            send(self.out, self.x, self.kx, x_peer)

        def result(self):
            arrive(self.core.at[0], self.kc)
            arrive(self.x, self.kx)
            return (
                self.part(n)[...].astype(f32) + self.core[0].astype(f32) + self.x[...].astype(f32)
            )

    class WideSum:
        def __init__(self, part_ref, y_ref, z_ref, out_ref, count):
            self.ref, self.y, self.z, self.total = part_ref, y_ref, z_ref, out_ref
            self.count = count
            self.ky, self.kz = take(A), take(A)

        def start(self, group):
            step = (group - zi + A) % A
            send(
                rows(self.ref, (group * 2 + 1 - yi) * self.count, self.count),
                rows(self.y, group * self.count, self.count),
                self.ky + step,
                y_peer,
            )

        def start_all(self):
            for step in range(A):
                self.start(turn(step + 1))

        def pass_on(self, step):
            group = turn(step)
            got = rows(self.y, group * self.count, self.count)
            arrive(got, self.ky + step)
            mine = rows(self.ref, (group * 2 + yi) * self.count, self.count)
            total = mine[...].astype(f32) + got[...].astype(f32)
            if step == 0:
                self.total[...] = total
                return
            mine[...] = total.astype(bf16)
            send(
                mine,
                rows(self.z, (step - 1) * self.count, self.count),
                self.kz + step,
                z_peer(step),
            )

        def finish(self):
            total = self.total[...]
            for step in range(1, A):
                got = rows(self.z, (step - 1) * self.count, self.count)
                arrive(got, self.kz + step)
                total = total + got[...].astype(f32)
            self.total[...] = total

    halves = 2 if RW % 32 == 0 else 1
    part_size = RW // halves
    g_wq = Gather(s.WQ.at[n], RW)
    g_pt = Gather(s.PT.at[n], RW)
    g_kv = Gather(s.KVF, T)
    g_dt = [Gather(s.DT, RW, i * part_size, part_size) for i in range(halves)]
    g_gu = [Gather(s.GU, RW, i * part_size, part_size) for i in range(halves)]
    f_wq, f_pt = Spread(s.WQ), Spread(s.PT)
    h_mix, h_bg, h_og, h_tg = Share(s.MIX, 4), Share(s.BG, 1), Share(o_out, 1), Share(o_tok, 2)
    n_mb = NarrowSum(s.MB, s.MBC, s.MBX, s.MBS)
    n_op = NarrowSum(s.OP, s.OPC, s.OPX, s.OPS)
    w_kv = WideSum(s.KVF, s.DKVY, s.DKVR, s.DKVO, T)
    w_gu = WideSum(s.GU, s.YGU, s.RGU, o_gu, RW)
    w_dt = WideSum(s.PDT, s.YDT, s.RDT, o_dt, RW)
    w_pt = WideSum(s.PPT, s.YPT, s.RPT, o_pt, RW)
    w_q = WideSum(s.PQ, s.YQ, s.RQ, o_q, RW)
    k_a2a, k_gain = take(3), take(3)

    own = pl.ds(pl.multiple_of(w * RW, RW), RW)
    s.WQ[n, own, :] = wq_own[...]
    g_wq.start()
    g_wq.start_y(0)
    s.PT[n, own, :] = pt_own[...]
    s.GU[own, :] = gu_own[...]
    s.DT[own, :] = dt_own[...]

    column, head = row_iota(256, D) & (LANES - 1), lane_iota(256, D) >> 6
    for r in range(QR):
        s.EQ[r] = jnp.where(column == head * QR + r, 1.0, 0.0).astype(bf16)
    column, head = row_iota(LANES, D), lane_iota(LANES, D) >> 6
    for r in range(KR):
        s.EK[r] = jnp.where(column == head * KR + r, 1.0, 0.0).astype(bf16)
        s.EK[KR + r] = jnp.where(column == y.heads * KR + head * VR + r, 1.0, 0.0).astype(bf16)
    place = (w * T + row_iota(T)).astype(f32)
    lane = lane_iota(T)
    angle = place * jnp.exp((lane % (DH // 2)).astype(f32) * (-math.log(10000.0) / (DH // 2)))
    s.ROPE[0] = jnp.cos(angle)
    s.ROPE[1] = jnp.where(lane % DH < DH // 2, -jnp.sin(angle), jnp.sin(angle))

    def own_row(values):
        mine = row_iota(N, values.shape[1]) == n
        return jnp.sum(jnp.where(mine, values.astype(f32), 0.0), axis=0, keepdims=True)

    own_docs = own_row(docs[:, pl.ds(pl.multiple_of(w * T, T), T)])
    own_docs = jnp.transpose(jnp.broadcast_to(own_docs, (T, T)))
    s.DOC[...] = own_docs

    def mask_block(block):
        first = block * KB
        key_docs = own_row(docs[:, pl.ds(pl.multiple_of(first, KB), KB)])
        allowed = (lane_iota(T, KB) + first <= row_iota(T, KB) + w * T) & (
            key_docs == s.DOC[:, :1]
        )
        s.BIAS[...] = jnp.where(allowed, 0.0, masked_score)

    mask_block(0)

    g_wq.forward_all()
    g_pt.start()
    g_pt.start_y(0)
    g_dt[0].start()
    for step in range(A):
        g_wq.landed(step)
        f_wq.start(step)
    for step in range(A):
        f_wq.forward(step)
    for step in range(A):
        f_wq.landed(step)

    gains = s.WQ[0, :, LANES:].astype(f32).T
    s.GAIN[0:1, :] = gains[y.og : y.og + 1]
    s.GAIN[1:2, :] = gains[y.og + 1 : y.og + 2]

    def rotated(tile, back=False):
        turned = swap_quarters(tile) * s.ROPE[1]
        return tile * s.ROPE[0] - turned if back else tile * s.ROPE[0] + turned

    own_rows = pl.ds(pl.multiple_of(n * T, T), T)
    x_own = tok[own_rows, :].astype(f32)
    r1_own = row_scale(x_own)
    normed_own = (x_own * r1_own * s.GAIN[0:1, :]).astype(bf16)
    factors = [dot_nn(normed_own, s.WQ[p]) for p in range(N)]
    first_tiles = [part[:, :LANES] for part in factors]
    second_tiles = [part[:, LANES:] for part in factors]

    def collect(start, width):
        pieces = []
        for p in range(N):
            pieces += [(second_tiles[p], start, p * width, width)]
        return place_lanes(pieces)

    kv_own = pl.ds(pl.multiple_of(w * T, T), T)
    s.KVF[kv_own, 0:128] = rotated(collect(y.oK, y.SK)).astype(bf16)
    s.KVF[kv_own, 128:256] = collect(y.oV, y.SK).astype(bf16)
    s.KVF[kv_own, 256:384] = place_lanes(
        [(second_tiles[p], y.ok, p * y.HK, y.HK) for p in range(N)]
        + [(second_tiles[p], y.ov, (N + p) * y.HK, y.HK) for p in range(N)]
    ).astype(bf16)
    g_kv.start()
    g_kv.start_y(0)

    query_heads = collect(y.oq, y.HQ)
    heads_high = query_heads.astype(bf16)
    s.QH[:, :LANES] = heads_high
    s.QH[:, LANES:] = (query_heads - heads_high.astype(f32)).astype(bf16)
    queries = jnp.zeros((T, D), f32)
    for r in range(QR):
        pieces = canonical_pieces(first_tiles, y.SQ, r * DH, DH, 0, 0)
        pieces += canonical_pieces(first_tiles, y.SQ, r * DH, DH, 0, DH)
        turned = rotated(place_lanes(pieces))
        s.QROT[r] = turned
        queries = queries + dot_nn(s.QH[...], s.EQ[r]) * jnp.concatenate([turned] * pairs, axis=1)
    for i in range(pairs):
        tile = (queries[:, i * LANES : (i + 1) * LANES] * (1.0 / QR)).astype(bf16)
        s.QP[i] = tile * jnp.asarray(DH**-0.5, bf16)

    def norm_rows(block, _):
        at = pl.ds(pl.multiple_of(block * T, T), T)
        values = tok[at, :].astype(f32)
        s.NORM[at, :] = (values * row_scale(values) * s.GAIN[0:1, :]).astype(bf16)
        return 0

    lax.fori_loop(0, N, norm_rows, 0)

    g_kv.forward_all()
    bulk = g_dt[1:] + g_gu
    g_pt.forward_all()
    for g in bulk:
        g.start()
    g_dt[0].start_y(0)
    g_dt[0].forward_all()
    for g in bulk:
        g.start_y(0)
    g_kv.landed_all()

    def expand_block(block):
        chunk_rows = 256

        def expand(chunk, _):
            at = pl.ds(pl.multiple_of(block * KB + chunk * chunk_rows, chunk_rows), chunk_rows)
            to = pl.ds(pl.multiple_of(chunk * chunk_rows, chunk_rows), chunk_rows)
            heads = s.KVF[at, 256:384]
            for ref, lanes, e in ((s.KP, 0, 0), (s.VP, 128, KR)):
                one, two = both_halves(s.KVF[at, lanes : lanes + 128].astype(f32))
                left = dot_nn(heads, s.EK[e])
                right = dot_nn(heads, s.EK[e + 1])
                for i in range(pairs):
                    cut = slice(i * LANES, (i + 1) * LANES)
                    ref[i, to, :] = ((left[:, cut] * one + right[:, cut] * two) * 0.5).astype(bf16)
            return 0

        lax.fori_loop(0, KB // chunk_rows, expand, 0)

    def pair_bias():
        bias = s.BIAS[...]
        return jnp.concatenate([bias, bias], axis=0)

    def forward_pair(i):
        scores = dot_nt(stack_pair(s.QP[i]), s.KP[i]) + pair_bias()
        top = jnp.max(scores, axis=1, keepdims=True)
        if y.NB > 1:
            old_top = s.LSE[i][:, :1]
            top = jnp.maximum(top, old_top)
        weights = jnp.exp(scores - top)
        total = jnp.sum(weights, axis=1, keepdims=True)
        rows_out = dot_nn(weights.astype(bf16), s.VP[i])
        if y.NB > 1:
            factor = jnp.exp(old_top - top)
            total = total + s.RUN[i][:, :1] * factor
            s.LSE[i] = jnp.broadcast_to(top, (2 * T, LANES))
            s.RUN[i] = jnp.broadcast_to(total, (2 * T, LANES))
            keep = stack_pair(s.ATT[i]) * factor
            s.ATT[i] = unstack_pair(rows_out + keep)
        return top, total, rows_out

    def store_mixture(i, attended, top, total):
        s.ATT[i] = attended
        s.LSE[i] = jnp.broadcast_to(top + jnp.log(total), (2 * T, LANES))
        s.MIX[own_rows, pl.ds(pl.multiple_of(i * LANES, LANES), LANES)] = attended.astype(bf16)

    if y.NB == 1:
        expand_block(0)

        def forward_step(i, _):
            top, total, rows_out = forward_pair(i)
            store_mixture(i, unstack_pair(rows_out / total), top, total)
            return 0

        per = pairs // h_mix.chunks
        for chunk in range(h_mix.chunks):
            lax.fori_loop(chunk * per, (chunk + 1) * per, forward_step, 0)
            h_mix.start(chunk)
    else:
        s.LSE[...] = jnp.full(s.LSE.shape, masked_score, f32)
        s.RUN[...] = jnp.zeros(s.RUN.shape, f32)
        s.ATT[...] = jnp.zeros(s.ATT.shape, f32)

        def forward_block(block, _):
            mask_block(block)
            expand_block(block)

            def step(i, _):
                forward_pair(i)
                return 0

            lax.fori_loop(0, pairs, step, 0)
            return 0

        lax.fori_loop(0, y.NB, forward_block, 0)

        def finish_step(i, _):
            total = s.RUN[i][:, :1]
            store_mixture(i, unstack_pair(stack_pair(s.ATT[i]) / total), s.LSE[i][:, :1], total)
            return 0

        lax.fori_loop(0, pairs, finish_step, 0)
        for chunk in range(h_mix.chunks):
            h_mix.start(chunk)

    for step in range(A):
        g_pt.landed(step)
        f_pt.start(step)
    h_mix.finish()
    for step in range(A):
        f_pt.forward(step)
    for g in bulk:
        g.forward_all()
    for step in range(A):
        f_pt.landed(step)

    def middle_rows(block, _):
        at = pl.ds(pl.multiple_of(block * 2 * T, 2 * T), 2 * T)
        values = tok[at, :].astype(f32)
        for p in range(N):
            values = values + dot_nt(s.MIX[at, p * 256 : (p + 1) * 256], s.PT[p])
        scale = row_scale(values)
        s.MID[at, :] = values
        s.R2[at, :] = jnp.broadcast_to(scale, (2 * T, LANES))
        s.NM[at, :] = (values * scale * s.GAIN[1:2, :]).astype(bf16)
        return 0

    lax.fori_loop(0, 2, middle_rows, 0)
    for g in g_dt + g_gu:
        g.landed_all()

    tail_low = lane_iota(2 * T) < DH

    def dense_rows(far):
        block = (1 - xo) if far else xo
        at = pl.ds(pl.multiple_of(block * 2 * T, 2 * T), 2 * T)
        both = dot_nn(s.NM[at, :], s.GU[...])
        back = dot_nn(cot[at, :], s.DT[...])
        tail = both[:, 2 * FM :]
        up_tail = pltpu.roll(tail, DH, 1)

        def gates(gate, up, pushed):
            chance = 1.0 / (1.0 + jnp.exp(-gate))
            silu = gate * chance
            return (
                silu * up,
                pushed * up * chance * (1.0 + gate * (1.0 - chance)),
                pushed * silu,
            )

        hidden, gate_gradient, up_gradient = gates(both[:, :FM], both[:, FM : 2 * FM], back[:, :FM])
        s.HID[at, :FM] = hidden.astype(bf16)
        s.GG[at, :FM] = gate_gradient.astype(bf16)
        s.GG[at, FM : 2 * FM] = up_gradient.astype(bf16)
        hidden, gate_gradient, up_gradient = gates(tail, up_tail, back[:, FM:])
        s.HID[at, FM:] = jnp.where(tail_low, hidden, 0.0).astype(bf16)
        s.GG[at, 2 * FM :] = jnp.where(
            tail_low, gate_gradient, pltpu.roll(up_gradient, DH, 1)
        ).astype(bf16)
        s.MB[at, :] = dot_nt(s.GG[at, :], s.GU[...]).astype(bf16)

    dense_rows(True)
    n_mb.start(True)
    dense_rows(False)
    n_mb.start(False)
    n_mb.pass_on()

    def grad_blocks(target, left, right, exchange):
        per = A // 4
        for j in range(4):
            block = (zi // per + 1 + j) % 4
            lanes = pl.ds(pl.multiple_of(block * 256, 256), 256)
            value = dot_tn(left[:, lanes], right[...]).astype(bf16)
            target[pl.ds(pl.multiple_of(block * 256, 256), 256), :] = value
            for q in range(per):
                exchange.start(block * per + q)

    for g in g_gu:
        g.sent()
    grad_blocks(s.GU, s.NM, s.GG, w_gu)

    mid_back = n_mb.result()
    mid_own = s.MID[own_rows, :]
    r2_own = s.R2[own_rows, :][:, :1]
    scaled = mid_back * s.GAIN[1:2, :]
    s.GS[1:2, :] = jnp.sum(mid_back * mid_own * r2_own, axis=0, keepdims=True)
    middle_gradient = (
        cot[own_rows, :].astype(f32)
        + r2_own * scaled
        - mid_own * (r2_own * r2_own * r2_own) * jnp.mean(scaled * mid_own, axis=-1, keepdims=True)
    )
    s.MG[...] = middle_gradient
    branch = middle_gradient.astype(bf16)
    s.BG[own_rows, :] = branch
    h_bg.start(0)
    for p in range(N):
        part = dot_nn(branch, s.PT[p]).astype(bf16)
        s.DO[2 * p] = part[:, :LANES]
        s.DO[2 * p + 1] = part[:, LANES:]

    def backward_block(block):
        s.DKS[...] = jnp.zeros(s.DKS.shape, f32)
        s.DHD[...] = jnp.zeros(s.DHD.shape, f32)

        def step(i, _):
            query, pushed = s.QP[i], s.DO[i]
            query2, pushed2 = stack_pair(query), stack_pair(pushed)
            product = pushed.astype(f32) * s.ATT[i]
            delta = jnp.sum(stack_pair(product), axis=1, keepdims=True)
            scores = dot_nt(query2, s.KP[i]) + pair_bias()
            chance = jnp.exp(scores - s.LSE[i][:, :1])
            gradient = (chance * (dot_nt(pushed2, s.VP[i]) - delta)).astype(bf16)
            s.QB[i] = s.QB[i] + unstack_pair(dot_nn(gradient, s.KP[i])) * DH**-0.5
            key_back = dot_tn(gradient, query2)
            value_back = dot_tn(chance.astype(bf16), pushed2)
            at = pl.ds(pl.multiple_of(block * KB, KB), KB)
            lanes = pl.ds(pl.multiple_of(i * LANES, LANES), LANES)
            heads = s.KVF[at, 256:384]
            found = s.DHD[...]
            for back, first, e in ((key_back, 0, 0), (value_back, 128, KR)):
                one, two = both_halves(s.KVF[at, first : first + 128].astype(f32))
                spread = jnp.concatenate([s.EK[e, :, lanes], s.EK[e + 1, :, lanes]], axis=1)
                joined = jnp.concatenate([back * one, back * two], axis=1).astype(bf16)
                found = found + dot_nt(joined, spread)
                wide = dot_nn(heads, spread)
                s.DKS[e] = s.DKS[e] + wide[:, :LANES] * back
                s.DKS[e + 1] = s.DKS[e + 1] + wide[:, LANES:] * back
            s.DHD[...] = found
            return 0

        lax.fori_loop(0, pairs, step, 0)
        at = pl.ds(pl.multiple_of(block * KB, KB), KB)
        low = lane_iota(KB) < DH
        for e in (0, KR):
            both = jnp.where(low, fold_halves(s.DKS[e]), fold_halves(s.DKS[e + 1])) * 0.5
            s.KVF[at, e * DH : e * DH + 128] = both.astype(bf16)
        s.KVF[at, 256:384] = (s.DHD[...] * 0.5).astype(bf16)

    s.QB[...] = jnp.zeros(s.QB.shape, f32)
    g_kv.sent()
    if y.NB == 1:
        backward_block(0)
    else:

        def backward_step(block, _):
            mask_block(block)
            expand_block(block)
            backward_block(block)
            return 0

        lax.fori_loop(0, y.NB, backward_step, 0)
    w_kv.start_all()
    grad_blocks(s.PDT, cot, s.HID, w_dt)

    query_back = jnp.concatenate([s.QB[i] for i in range(pairs)], axis=1)
    heads_back = jnp.zeros((T, LANES), f32)
    shared_back = []
    for r in range(QR):
        turned = s.QROT[r]
        product = (query_back * jnp.concatenate([turned] * pairs, axis=1)).astype(bf16)
        heads_back = heads_back + dot_nt(product, s.EQ[r, :LANES, :])
        product = dot_nn(s.QH[...], s.EQ[r]) * query_back
        total = product[:, :LANES]
        for i in range(1, pairs):
            total = total + product[:, i * LANES : (i + 1) * LANES]
        shared_back.append(fold_halves(total))
    low = lane_iota(T) < DH
    shared_tiles = [
        rotated(jnp.where(low, shared_back[2 * t], shared_back[2 * t + 1]), back=True) * (1.0 / QR)
        for t in range(QR // 2)
    ]
    heads_back = heads_back * (1.0 / QR)

    for far in (True, False):
        block = (1 - xo) if far else xo
        at = pl.ds(pl.multiple_of(block * 2 * T, 2 * T), 2 * T)
        s.OP[at, :] = dot_nt(s.HID[at, :], s.DT[...]).astype(bf16)
        n_op.start(far)
    n_op.pass_on()

    for step in list(range(1, A)) + [0]:
        w_kv.pass_on(step)
    w_kv.finish()

    key_shared = rotated(s.DKVO[:, 0:128], back=True)
    value_shared = s.DKVO[:, 128:256]
    head_tile = s.DKVO[:, 256:384]
    for p in range(N):
        s.QGS[p, :, :LANES] = place_lanes(
            canonical_pieces(shared_tiles, LANES, p * y.SQ, y.SQ, 0, 0)
        ).astype(bf16)
        s.QGS[p, :, LANES:] = place_lanes(
            [
                (key_shared, p * y.SK, y.oK, y.SK),
                (value_shared, p * y.SK, y.oV, y.SK),
                (heads_back, p * y.HQ, y.oq, y.HQ),
                (head_tile, p * y.HK, y.ok, y.HK),
                (head_tile, (N + p) * y.HK, y.ov, y.HK),
            ]
        ).astype(bf16)
    for k, peer in enumerate(narrow_peers):
        send(s.QGS.at[peer[1]], s.QGR.at[n], k_a2a + k, peer)
    s.QGR[n] = s.QGS[n]

    first_back = jnp.zeros((T, D), f32)
    for p in range(N):
        first_back = first_back + dot_nt(s.QGS[p], s.WQ[p])
    x_own = tok[own_rows, :].astype(f32)
    r1_own = row_scale(x_own)
    s.GS[0:1, :] = jnp.sum(first_back * x_own * r1_own, axis=0, keepdims=True)
    for k, peer in enumerate(narrow_peers):
        send(s.GS, s.GR.at[k], k_gain + k, peer)
    scaled = first_back * s.GAIN[0:1, :]
    tokens_gradient = (
        s.MG[...]
        + r1_own * scaled
        - x_own * (r1_own * r1_own * r1_own) * jnp.mean(scaled * x_own, axis=-1, keepdims=True)
    )
    o_tok[own_rows, :] = tokens_gradient.astype(bf16)
    for chunk in range(h_tg.chunks):
        h_tg.start(chunk)

    o_out[own_rows, :] = (s.MID[own_rows, :] + n_op.result()).astype(bf16)
    h_og.start(0)

    h_bg.finish()
    grad_blocks(s.PPT, s.BG, s.MIX.at[:, pl.ds(pl.multiple_of(n * 256, 256), 256)], w_pt)

    for k, peer in enumerate(narrow_peers):
        arrive(s.QGR.at[peer[1]], k_a2a + k)
    for k in range(3):
        arrive(s.GR.at[k], k_gain + k)
    gain_rows = s.GS[...]
    for k in range(3):
        gain_rows = gain_rows + s.GR[k]
    lane_row = row_iota(LANES, D)
    spread = jnp.where(
        lane_row == y.og,
        gain_rows[0:1],
        jnp.where(lane_row == y.og + 1, gain_rows[1:2], 0.0),
    )
    gain_columns = spread.T
    per = A // 4
    for j in range(4):
        block = (zi // per + 1 + j) % 4
        lanes = pl.ds(pl.multiple_of(block * 256, 256), 256)
        value = jnp.zeros((256, 256), f32)
        for p in range(N):
            value = value + dot_tn(s.NORM[p * T : (p + 1) * T, lanes], s.QGR[p])
        s.PQ[pl.ds(pl.multiple_of(block * 256, 256), 256), :] = value.astype(bf16)
    s.PQ[:, LANES:] = (s.PQ[:, LANES:].astype(f32) + gain_columns).astype(bf16)
    w_q.start_all()

    for exchange in (w_gu, w_dt, w_pt, w_q):
        for step in list(range(1, A)) + [0]:
            exchange.pass_on(step)

    h_tg.finish()
    h_og.finish()
    for exchange in (w_gu, w_dt, w_pt, w_q):
        exchange.finish()
    for g in [g_wq, g_pt] + g_dt:
        g.sent()
    for copy in pending:
        copy.wait_send()


def solution(mesh):
    W, N = mesh.shape["wide"], mesh.shape["narrow"]

    def on_device(
        tokens,
        documents,
        prenorm,
        qheads,
        qshared,
        kheads,
        kshared,
        vheads,
        vshared,
        project,
        midnorm,
        gating,
        upward,
        downward,
        cotangent,
    ):
        R, T, D = tokens.shape
        L = documents.shape[1]
        RW, F = gating.shape
        y = make_layout(W, N, T, D, F, L, N * kheads.shape[1] // KR)
        assert R == N
        FM = y.FM
        zeros = lambda count: jnp.zeros((RW, count), bf16)
        wq = jnp.concatenate(
            [
                qshared,
                zeros(LANES - y.SQ),
                kshared,
                vshared,
                qheads,
                kheads,
                vheads,
                prenorm[:, None],
                midnorm[:, None],
                zeros(LANES - y.og - 2),
            ],
            axis=1,
        )
        gu = jnp.concatenate([gating[:, :FM], upward[:, :FM], gating[:, FM:], upward[:, FM:]], axis=1)
        dt = jnp.pad(downward.T, ((0, 0), (0, y.FP - F)))
        pt = project.T
        scratch = scratch_list(y)
        copies = 256 + 48 * y.A
        vmem = pl.BlockSpec(memory_space=pltpu.VMEM)

        def kernel(*refs):
            block_kernel(y, tuple(scratch), *refs)

        shape = jax.ShapeDtypeStruct
        out, tok, gu_back, dt_back, pt_back, q_back = pl.pallas_call(
            kernel,
            out_shape=(
                shape((y.M, D), bf16),
                shape((y.M, D), bf16),
                shape((RW, 2 * FM + LANES), f32),
                shape((RW, y.FP), f32),
                shape((RW, 256), f32),
                shape((RW, 256), f32),
            ),
            in_specs=[vmem] * 7,
            out_specs=[vmem] * 6,
            scratch_shapes=[*scratch.values()] + [pltpu.SemaphoreType.DMA((copies,))] * 2,
            compiler_params=pltpu.CompilerParams(
                collective_id=0, has_side_effects=True, vmem_limit_bytes=63 * 2**20
            ),
            name="block",
        )(
            tokens.reshape(y.M, D),
            documents,
            wq,
            gu,
            dt,
            pt,
            cotangent.reshape(y.M, D),
        )
        second = lambda first, count: q_back[:, LANES + first : LANES + first + count]
        half = F - FM
        return (
            out.reshape(R, T, D),
            tok.astype(f32).reshape(R, T, D),
            second(y.og, 1).reshape(RW),
            second(y.oq, y.HQ),
            q_back[:, : y.SQ],
            second(y.ok, y.HK),
            second(y.oK, y.SK),
            second(y.ov, y.HK),
            second(y.oV, y.SK),
            pt_back.T,
            second(y.og + 1, 1).reshape(RW),
            jnp.concatenate([gu_back[:, :FM], gu_back[:, 2 * FM : 2 * FM + half]], axis=1),
            jnp.concatenate([gu_back[:, FM : 2 * FM], gu_back[:, 2 * FM + half :]], axis=1),
            dt_back[:, :F].T,
        )

    split = P("wide", "narrow")
    flipped = P("narrow", "wide")
    whole = P(None, "wide", None)
    gain = P("wide")
    return jax.shard_map(
        on_device,
        mesh=mesh,
        in_specs=(
            whole,
            P(),
            gain,
            split,
            split,
            split,
            split,
            split,
            split,
            flipped,
            gain,
            split,
            split,
            flipped,
            whole,
        ),
        out_specs=(
            whole,
            whole,
            gain,
            split,
            split,
            split,
            split,
            split,
            split,
            flipped,
            gain,
            split,
            split,
            flipped,
        ),
        check_vma=False,
    )
```

time: 1520 us -> 257 us (0.17)
  waiting for transfers between devices: 928 us -> 0 us
  blocking collectives: 321 us -> 0 us
  Pallas kernels: 0 us -> 225 us
  matrix products: 149 us -> 0 us
  local copies, waits for them, and re-layouts: 60.6 us -> 28.7 us
  other arithmetic: 31.2 us -> 1.63 us
    reduce_scatter x13 -> x0, waiting for transfers between devices: 667 us -> none  [the longest x1 75.6 us: on_device(): lax.psum_scatter(outer(hidden, upstream), 'wide', scatter_dimension=1, ti...]
    all_gather x14 -> x0, blocking collectives: 299 us -> none  [the longest x1 27.9 us: on_device(): lax.all_gather(project, 'wide', axis=1, tiled=True)]
    pallas_call x0 -> x1, Pallas kernels: none -> 225 us  [on_device(): pl.pallas_call(kernel, out_shape=(shape((y.M, D), bf16), shape((y.M, D),...]
    all_gather x7 -> x0, waiting for transfers between devices: 182 us -> none  [the longest x1 51.2 us: on_device(): lax.all_gather(attended_gradient.reshape(batch_rows, local_tokens, -1), '...]
    dot_general x53 -> x0, matrix products: 149 us -> none  [the longest x8 19.3 us: back_through(): jnp.einsum('nc,dc->nd', gradient_low, weight_full, preferred_element_type...]
    psum x3 -> x0, waiting for transfers between devices: 76 us -> none  [the longest x1 33.6 us: on_device(): lax.psum((back_through(gate_gradient, gating_full) + back_through(up_grad...]
    dynamic_slice x25 -> x0, local copies, waits for them, and re-layouts: 23.1 us -> none  [the longest x4 11 us: update(): lax.dynamic_slice_in_dim(member, first_row, block_size, 1)]
    unnamed x1 -> x0, blocking collectives: 21.6 us -> none
  transfers between devices with their start and end apart: 23 -> 0, of which waited for: 20 -> 0; matrix products, arithmetic and copies ran while one was open for 5% -> 0% of each run, Pallas kernels for 0% -> 0%
where the time goes in v1:
time: 257 us; the launch traced here: 256 us
  Pallas kernels  225 us (88%)
  local copies, waits for them, and re-layouts  28.7 us (11%)
    pallas_call x1, Pallas kernels, on_device(): pl.pallas_call(kernel, out_shape=(shape((y.M, D), bf16), shape((y.M, D),...  225 us
    unnamed x33, local copies, waits for them, and re-layouts  16.6 us

profile of v1, /device:TPU:0, one launch (start us, length us, event | category | flops | bytes accessed | tf_op | source)
XLA Modules:
  0.0 256.2 jit_solution(1655133839740262769)
XLA Ops:
  0.6 0.0 slice-start
  0.7 0.0 copy-start.4
  0.7 0.8 slice.53
  1.4 0.1 copy.79
  1.6 0.7 slice.54
  2.3 0.1 copy.80
  2.4 0.8 copy.59
  3.2 0.8 copy.56
  4.0 0.8 copy.53
  4.9 0.8 copy.57
  5.7 0.8 copy.54
  6.5 0.8 copy.58
  7.3 0.8 copy.55
  8.1 0.8 copy.60
  8.9 0.8 concatenate.12.refs_2_
  9.7 1.6 copy.66
  11.3 0.9 slice.51
  12.2 0.2 copy.77
  12.4 0.0 slice-done
  12.4 0.2 copy.78
  12.5 0.8 concatenate.13.refs_3_
  13.4 0.1 copy.65
  13.5 0.7 pad.4.refs_4_
  14.2 225.1 %block.1 = (bf16[512,1024]{1,0:T(8,128)(2,1)}, bf16[512,1024]{1,0:T(8,128)(2,1)}, f32[128,1408]{1,0:T(8,128)}, f32[128,768]{1,0:T(8,128)}, f32[128,256]{1,0:T(8,128)}, /*index=5*/f32[128,256]{1,0:T(8,128)}) custom-call(bf16[512,1024]{1,0:T(8,128)(2,1)} %bitcast.13, s32[4,1024]{1,0:T(4,128)} %refs_1_.1, bf16[128,256]{1,0:T(8,128)(2,1)} %concatenate.12.refs_2_, ...), custom_call_target="tpu_custom_call" | custom-call | tf_op jit(solution)/shard_map/block/pallas_call | solution.py:932
  239.4 1.6 slice_reduce_fusion
  241.0 0.8 slice.57
  241.8 0.7 copy.68
  242.5 0.9 slice.56
  243.4 0.7 copy.67
  244.1 1.7 copy.73
  245.8 1.0 fusion.1
  246.8 1.1 fusion
  248.0 0.1 pad_maximum_fusion
  248.0 0.9 copy.74
  248.9 0.0 copy-done
  248.9 0.1 fusion.2
  249.0 0.7 copy.72
  249.7 0.1 fusion.3
  249.8 0.7 copy.71
  250.5 0.7 copy.69
  251.1 0.7 copy.70
  251.8 0.9 copy.75
  252.7 0.0 copy-done.3
  252.8 0.9 copy.76
  253.7 0.0 copy-done.1
  253.7 1.6 convert.1
  255.2 0.0 copy-done.2
  255.2 1.0 copy.82
  (8 shorter events, 0.0 us)
Async XLA Ops:
  0.6 11.7 %slice-start = ((bf16[128,704]{0,1:T(8,128)(2,1)}), bf16[128,640]{0,1:T(8,128)(2,1)S(1)}, s32[]{:S(2)}) async-start(bf16[128,704]{0,1:T(8,128)(2,1)} %param.27), calls=%async_computation | async-start | bytes 327680 | tf_op jit(solution)/shard_map/slice | solution.py:921
  0.7 12.7 %copy-start.4 = (bf16[704,128]{1,0:T(8,128)(2,1)S(1)}, bf16[704,128]{1,0:T(8,128)(2,1)}, u32[]{:S(2)}) copy-start(bf16[704,128]{1,0:T(8,128)(2,1)} %param.28) | copy-start | bytes 540676
  244.1 4.8 %copy-start = (f32[128,256]{1,0:T(8,128)S(1)}, f32[128,256]{1,0:T(8,128)}, u32[]{:S(2)}) copy-start(f32[128,256]{1,0:T(8,128)} %get-tuple-element.22) | copy-start | bytes 393220
  247.9 4.8 %copy-start.3 = (f32[128,768]{1,0:T(8,128)S(1)}, f32[128,768]{1,0:T(8,128)}, u32[]{:S(2)}) copy-start(f32[128,768]{1,0:T(8,128)} %get-tuple-element.25) | copy-start | bytes 1179652
  248.0 5.6 %copy-start.1 = (bf16[512,1024]{1,0:T(8,128)(2,1)S(1)}, bf16[512,1024]{1,0:T(8,128)(2,1)}, u32[]{:S(2)}) copy-start(bf16[512,1024]{1,0:T(8,128)(2,1)} %get-tuple-element.21) | copy-start | bytes 3145732
  252.7 2.5 copy-start.2

commit v2 on v1

--- a/solution.py
+++ b/solution.py
@@ -130,7 +130,7 @@
         KVF=vm(L, 384),
         KP=vm(y.pairs, y.KB, LANES),
         VP=vm(y.pairs, y.KB, LANES),
-        EQ=vm(QR, 256, D),
+        EQ=vm(QR, LANES, D),
         EK=vm(4, LANES, D),
         BIAS=vm(T, y.KB, kind=f32),
         DOC=vm(T, LANES, kind=f32),
@@ -141,7 +141,7 @@
         QP=vm(y.pairs, T, LANES),
         ATT=vm(y.pairs, T, LANES, kind=f32),
         LSE=vm(y.pairs, 2 * T, LANES, kind=f32),
-        RUN=vm(y.pairs, 2 * T, LANES, kind=f32),
+        RUN=vm(y.pairs if y.NB > 1 else 1, 2 * T, LANES, kind=f32),
         MIX=vm(M, D),
         NORM=vm(M, D),
         MID=vm(M, D, kind=f32),
@@ -164,31 +164,47 @@
         DKS=vm(4, y.KB, LANES, kind=f32),
         DHD=vm(y.KB, LANES, kind=f32),
         DKVY=vm(A * T, 384),
-        DKVR=vm((A - 1) * T, 384),
+        DKVR=vm((A + 1) * T, 384),
         DKVO=vm(T, 384, kind=f32),
         QGS=vm(N, T, 256),
         QGR=vm(N, T, 256),
+        OUT=vm(M, D),
+        TOK=vm(M, D),
+        TGU=vm(RW, GUc, kind=f32),
+        TDT=vm(RW, y.FP, kind=f32),
+        TPT=vm(RW, 256, kind=f32),
+        TQ=vm(RW, 256, kind=f32),
         GS=vm(8, D, kind=f32),
         GR=vm(3, 8, D, kind=f32),
         YGU=vm(A * RW, GUc),
-        RGU=vm((A - 1) * RW, GUc),
+        RGU=vm((A + 1) * RW, 1024),
+        RZF=vm((A + 1) * 2 * RW, GUc - 1024),
         PDT=vm(D, y.FP),
         YDT=vm(A * RW, y.FP),
-        RDT=vm((A - 1) * RW, y.FP),
+        RDT=vm((A + 1) * RW, y.FP),
         PPT=vm(D, 256),
         YPT=vm(A * RW, 256),
-        RPT=vm((A - 1) * RW, 256),
+        RPT=vm((A + 1) * RW, 256),
         PQ=vm(D, 256),
         YQ=vm(A * RW, 256),
-        RQ=vm((A - 1) * RW, 256),
+        RQ=vm((A + 1) * RW, 256),
     )
 
 
 def block_kernel(y, names, *refs):
-    tok, docs, wq_own, gu_own, dt_own, pt_own, cot = refs[:7]
-    o_out, o_tok, o_gu, o_dt, o_pt, o_q = refs[7:13]
-    s = SimpleNamespace(**dict(zip(names, refs[13:])))
-    ssem, rsem = refs[13 + len(names) :]
+    tok, docs, prenorm, qheads, qshared, kheads, kshared, vheads, vshared = refs[:9]
+    project, midnorm, gating, upward, downward, cot = refs[9:15]
+    r_out, r_tok, r_gu, r_dt, r_pt, r_q = refs[15:21]
+    s = SimpleNamespace(**dict(zip(names, refs[21:])))
+    ssem, rsem, wsem = refs[21 + len(names) :]
+    o_out, o_tok, o_gu, o_dt, o_pt, o_q = s.OUT, s.TOK, s.TGU, s.TDT, s.TPT, s.TQ
+    written = []
+
+    def write(src, dst):
+        copy = pltpu.make_async_copy(src, dst, wsem.at[len(written)])
+        copy.start()
+        written.append(copy)
+
     W, N, T, D, F, L, A, RW, M = y.W, y.N, y.T, y.D, y.F, y.L, y.A, y.RW, y.M
     FM, FP, KB, pairs = y.FM, y.FP, y.KB, y.pairs
     w = lax.axis_index("wide")
@@ -199,22 +215,22 @@
     c_peer = (w, xo * 2 + 1 - co)
     x_peer = (w, (1 - xo) * 2 + co)
     d_peer = (w, (1 - xo) * 2 + 1 - co)
-    turn = lambda step: (zi + step) % A
-    z_peer = lambda step: (turn(step) * 2 + yi, n)
     narrow_peers = (c_peer, x_peer, d_peer)
-    taken = [0]
+    taken = [0, rsem.shape[0]]
 
     def take(count=1):
-        first = taken[0]
         taken[0] += count
-        assert taken[0] <= ssem.shape[0]
-        return first
-
-    def remote(src, dst, k, peer):
+        return taken[0] - count
+
+    def take_send(count):
+        taken[1] += count
+        return taken[1] - count
+
+    def remote(src, dst, k, peer, send_k=None):
         return pltpu.make_async_remote_copy(
             src_ref=src,
             dst_ref=dst,
-            send_sem=ssem.at[k],
+            send_sem=ssem.at[k if send_k is None else send_k],
             recv_sem=rsem.at[k],
             device_id=peer,
             device_id_type=MESH,
@@ -230,72 +246,156 @@
     def arrive(dst, k):
         remote(dst, dst, k, y_peer).wait_recv()
 
-    def rows(ref, first, count):
-        return ref.at[pl.ds(pl.multiple_of(first, 16), count)]
+    def rows(ref, first, count, lanes=None):
+        at = pl.ds(pl.multiple_of(first, 16), count)
+        return ref.at[at] if lanes is None else ref.at[at, pl.ds(*lanes)]
+
+    def each_at(distance, act):
+        if distance == 0:
+            act(zi, None)
+            return
+        pl.when(zi >= distance)(lambda: act(zi - distance, True))
+        pl.when(zi + distance < A)(lambda: act(zi + distance, False))
+
+    right_peer = ((zi + 1) * 2 + yi, n)
+    left_peer = ((zi - 1) * 2 + yi, n)
 
     barrier = pltpu.get_barrier_semaphore()
-    peers = [y_peer, *narrow_peers] + [z_peer(step) for step in range(1, A)]
-    for peer in peers:
+    for peer in (y_peer, *narrow_peers):
         pl.semaphore_signal(barrier, inc=1, device_id=peer, device_id_type=MESH)
-    pl.semaphore_wait(barrier, len(peers))
+
+    @pl.when(zi > 0)
+    def _():
+        pl.semaphore_signal(barrier, inc=1, device_id=left_peer, device_id_type=MESH)
+
+    @pl.when(zi < A - 1)
+    def _():
+        pl.semaphore_signal(barrier, inc=1, device_id=right_peer, device_id_type=MESH)
+
+    pl.semaphore_wait(barrier, jnp.where((zi > 0) & (zi < A - 1), 6, 5))
 
     class Gather:
-        def __init__(self, ref, count, first=0, size=None):
-            self.ref, self.count, self.first = ref, count, first
-            self.size = count if size is None else size
-            self.kz, self.ky = take(A), take(A)
-            self.started = []
+        def __init__(self, ref, count, lanes=None, y_first=False):
+            self.ref, self.count, self.lanes, self.y_first = ref, count, lanes, y_first
+            self.kz, self.ky, self.kl = take(A), take(A), take_send(A)
+            self.next = 1
+
+        def part(self, wide):
+            return rows(self.ref, wide * self.count, self.count, self.lanes)
+
+        def block(self, z):
+            if self.y_first:
+                return rows(self.ref, z * 2 * self.count, 2 * self.count, self.lanes)
+            return self.part(z * 2 + yi)
+
+        def along(self, z, to_right):
+            block = self.block(z)
+            if to_right:
+                return remote(block, block, self.kz + z, right_peer)
+            return remote(block, block, self.kz + z, left_peer, self.kl + z)
+
+        def across(self, z):
+            part = self.part(z * 2 + yi)
+            return remote(part, part, self.ky + z, y_peer)
+
+        def landed(self, z):
+            arrive(self.part(z * 2 + 1 - yi), self.ky + z)
+
+        def launch_y(self):
+            self.across(zi).start()
+
+        def launch(self):
+            if self.y_first:
+                self.landed(zi)
+            pl.when(zi < A - 1)(lambda: self.along(zi, True).start())
+            pl.when(zi > 0)(lambda: self.along(zi, False).start())
+
+        def hop(self, distance):
+            def act(z, to_right):
+                arrive(self.block(z), self.kz + z)
+                more = zi < A - 1 if to_right else zi > 0
+                pl.when(more)(lambda: self.along(z, to_right).start())
+                if not self.y_first:
+                    self.across(z).start()
+
+            each_at(distance, act)
+
+        def pump(self, count=A):
+            for _ in range(min(count, A - self.next)):
+                self.hop(self.next)
+                self.next += 1
+
+        def landed_all(self):
+            if not self.y_first:
+                for z in range(A):
+                    self.landed(z)
 
         def sent(self):
-            for copy in self.started:
-                copy.wait_send()
-
-        def part(self, wide):
-            return rows(self.ref, wide * self.count + self.first, self.size)
-
-        def start(self):
-            for step in range(1, A):
-                send(self.part(w), self.part(w), self.kz + step, z_peer(step), self.started)
-
-        def start_y(self, step):
-            part = self.part(turn(-step) * 2 + yi)
-            send(part, part, self.ky + step, y_peer, self.started)
-
-        def forward(self, step):
-            arrive(self.part(turn(-step) * 2 + yi), self.kz + step)
-            self.start_y(step)
-
-        def forward_all(self):
-            for step in range(1, A):
-                self.forward(step)
-
-        def landed(self, step):
-            arrive(self.part(turn(-step) * 2 + 1 - yi), self.ky + step)
-
-        def landed_all(self):
-            for step in range(A):
-                self.landed(step)
+            self.across(zi).wait_send()
+            pl.when(zi < A - 1)(lambda: self.along(zi, True).wait_send())
+            pl.when(zi > 0)(lambda: self.along(zi, False).wait_send())
+            for distance in range(1, A):
+
+                def act(z, to_right):
+                    more = zi < A - 1 if to_right else zi > 0
+                    pl.when(more)(lambda: self.along(z, to_right).wait_send())
+                    if not self.y_first:
+                        self.across(z).wait_send()
+
+                each_at(distance, act)
 
     class Spread:
-        def __init__(self, ref):
-            self.ref = ref
+        def __init__(self, gather, ref):
+            self.gather, self.ref = gather, ref
+            self.next = self.passed = 0
             self.kx, self.kc, self.kd = take(A), take(A), take(A)
 
-        def part(self, owner, step):
-            return rows(self.ref.at[owner], turn(-step) * 2 * RW, 2 * RW)
-
-        def start(self, step):
-            send(self.part(n, step), self.part(n, step), self.kx + step, x_peer)
-            send(self.part(n, step), self.part(n, step), self.kc + step, c_peer)
-
-        def forward(self, step):
-            part = self.part(x_peer[1], step)
-            arrive(part, self.kx + step)
-            send(part, part, self.kd + step, c_peer)
-
-        def landed(self, step):
-            arrive(self.part(c_peer[1], step), self.kc + step)
-            arrive(self.part(d_peer[1], step), self.kd + step)
+        def part(self, owner, z):
+            return rows(self.ref.at[owner], z * 2 * RW, 2 * RW)
+
+        def copies(self, z):
+            part = self.part(n, z)
+            return remote(part, part, self.kx + z, x_peer), remote(part, part, self.kc + z, c_peer)
+
+        def onward(self, z):
+            part = self.part(x_peer[1], z)
+            return remote(part, part, self.kd + z, c_peer)
+
+        def start(self, distance):
+            def act(z, _):
+                self.gather.landed(z)
+                for copy in self.copies(z):
+                    copy.start()
+
+            each_at(distance, act)
+
+        def pump(self, count=A):
+            for _ in range(min(count, A - self.next)):
+                self.start(self.next)
+                self.next += 1
+
+        def pump_forward(self, count=A):
+            for _ in range(min(count, A - self.passed)):
+                self.forward(self.passed)
+                self.passed += 1
+
+        def forward(self, distance):
+            def act(z, _):
+                arrive(self.part(x_peer[1], z), self.kx + z)
+                self.onward(z).start()
+
+            each_at(distance, act)
+
+        def landed(self):
+            for z in range(A):
+                arrive(self.part(c_peer[1], z), self.kc + z)
+                arrive(self.part(d_peer[1], z), self.kd + z)
+
+        def sent(self):
+            for z in range(A):
+                for copy in self.copies(z):
+                    copy.wait_send()
+                self.onward(z).wait_send()
 
     class Share:
         def __init__(self, ref, chunks):
@@ -320,11 +420,17 @@
             arrive(self.part(c_peer[1], chunk), self.kc + chunk)
             arrive(self.part(d_peer[1], chunk), self.kd + chunk)
 
-        def finish(self):
+        def forward_all(self):
             for chunk in range(self.chunks):
                 self.forward(chunk)
+
+        def landed_all(self):
             for chunk in range(self.chunks):
                 self.landed(chunk)
+
+        def finish(self):
+            self.forward_all()
+            self.landed_all()
 
     class NarrowSum:
         def __init__(self, part_ref, core_ref, x_ref, send_ref):
@@ -352,79 +458,181 @@
             )
 
     class WideSum:
-        def __init__(self, part_ref, y_ref, z_ref, out_ref, count):
+        def __init__(self, part_ref, y_ref, z_ref, out_ref, count, lanes=None, z_first=False):
             self.ref, self.y, self.z, self.total = part_ref, y_ref, z_ref, out_ref
-            self.count = count
-            self.ky, self.kz = take(A), take(A)
-
-        def start(self, group):
-            step = (group - zi + A) % A
-            send(
-                rows(self.ref, (group * 2 + 1 - yi) * self.count, self.count),
-                rows(self.y, group * self.count, self.count),
-                self.ky + step,
-                y_peer,
-            )
-
-        def start_all(self):
-            for step in range(A):
-                self.start(turn(step + 1))
-
-        def pass_on(self, step):
-            group = turn(step)
-            got = rows(self.y, group * self.count, self.count)
-            arrive(got, self.ky + step)
-            mine = rows(self.ref, (group * 2 + yi) * self.count, self.count)
-            total = mine[...].astype(f32) + got[...].astype(f32)
-            if step == 0:
-                self.total[...] = total
+            self.count, self.lanes, self.z_first = count, lanes, z_first
+            self.size = 2 * count if z_first else count
+            self.next = 0
+            self.z_lanes = (0, lanes[1]) if z_first else lanes
+            self.ky, self.kz, self.kl = take(1 if z_first else A), take(A + 1), take_send(A)
+
+        def part(self, wide):
+            return rows(self.ref, wide * self.count, self.count, self.lanes)
+
+        def block(self, z):
+            if self.z_first:
+                return rows(self.ref, z * 2 * self.count, 2 * self.count, self.lanes)
+            return self.part(z * 2 + yi)
+
+        def got_y(self, z):
+            return rows(self.y, z * self.count, self.count, self.lanes)
+
+        def got_z(self, slot):
+            return rows(self.z, slot * self.size, self.size, self.z_lanes)
+
+        def across(self, z):
+            return remote(self.part(z * 2 + 1 - yi), self.got_y(z), self.ky + z, y_peer)
+
+        def along(self, z, to_right):
+            block = self.block(z)
+            if to_right:
+                return remote(block, self.got_z(z), self.kz + z, right_peer)
+            slot = jnp.where(z == zi - 1, A, z)
+            return remote(block, self.got_z(slot), self.kz + slot, left_peer, self.kl + z)
+
+        def start(self, z):
+            if not self.z_first:
+                self.across(z).start()
+
+        def gather_y(self, z):
+            block = self.block(z)[...].astype(f32)
+            if self.z_first:
+                return block
+            arrive(self.got_y(z), self.ky + z)
+            return block + self.got_y(z)[...].astype(f32)
+
+        def stage(self, step):
+            def move(z, to_right, joined):
+                value = self.gather_y(z)
+                if joined:
+                    arrive(self.got_z(z), self.kz + z)
+                    value = value + self.got_z(z)[...].astype(f32)
+                self.block(z)[...] = value.astype(bf16)
+                self.along(z, to_right).start()
+
+            right, left = A - 1 - step + zi, step - (A - 1 - zi)
+            to_right = (right < A) & (right > zi)
+            to_left = (left >= 0) & (left < zi)
+            pl.when(to_right & (zi > 0))(lambda: move(right, True, True))
+            pl.when(to_left & (zi < A - 1))(lambda: move(left, False, True))
+            if not self.z_first:
+                pl.when(to_right & (zi == 0))(lambda: move(right, True, False))
+                pl.when(to_left & (zi == A - 1))(lambda: move(left, False, False))
+
+        def pump(self, count=A):
+            for _ in range(min(count, A - 1 - self.next)):
+                self.stage(self.next)
+                self.next += 1
+
+        def start_ends(self):
+            @pl.when(zi == 0)
+            def _():
+                for z in range(A - 1, 0, -1):
+                    self.along(z, True).start()
+
+            @pl.when(zi == A - 1)
+            def _():
+                for z in range(A - 1):
+                    self.along(z, False).start()
+
+        def add(self, slot):
+            arrive(self.got_z(slot), self.kz + slot)
+            got = self.got_z(slot)[...].astype(f32)
+            if not self.z_first:
+                self.total[...] += got
                 return
-            mine[...] = total.astype(bf16)
-            send(
-                mine,
-                rows(self.z, (step - 1) * self.count, self.count),
-                self.kz + step,
-                z_peer(step),
-            )
+            block = self.block(zi)
+            block[...] = (block[...].astype(f32) + got).astype(bf16)
 
         def finish(self):
-            total = self.total[...]
-            for step in range(1, A):
-                got = rows(self.z, (step - 1) * self.count, self.count)
-                arrive(got, self.kz + step)
-                total = total + got[...].astype(f32)
-            self.total[...] = total
-
-    halves = 2 if RW % 32 == 0 else 1
-    part_size = RW // halves
+            if not self.z_first:
+                self.total[...] = self.gather_y(zi)
+            pl.when(zi > 0)(lambda: self.add(zi))
+            pl.when(zi < A - 1)(lambda: self.add(A))
+            if self.z_first:
+                self.last_across().start()
+
+        def last_across(self):
+            return remote(self.part(zi * 2 + 1 - yi), self.got_y(0), self.ky, y_peer)
+
+        def finish_y(self):
+            if self.z_first:
+                arrive(self.got_y(0), self.ky)
+                mine = self.part(zi * 2 + yi)[...].astype(f32)
+                self.total[...] = mine + self.got_y(0)[...].astype(f32)
+
+        def sent(self):
+            if self.z_first:
+                self.last_across().wait_send()
+            for z in range(A):
+                if not self.z_first:
+                    self.across(z).wait_send()
+                pl.when(zi < z)(lambda: self.along(z, True).wait_send())
+                pl.when(zi > z)(lambda: self.along(z, False).wait_send())
+
+    if A == 4:
+        z_order = []
+        for row in zip((3, 2, 1, 0), (3, 2, 0, 1), (0, 1, 3, 2), (0, 1, 2, 3)):
+            z_order.append(sum(jnp.where(zi == at, z, 0) for at, z in enumerate(row)))
+    else:
+        z_order = range(A)
+
+    GUc = 2 * FM + LANES
+    cuts = ((0, 512), (512, 512), (1024, GUc - 1024))
     g_wq = Gather(s.WQ.at[n], RW)
     g_pt = Gather(s.PT.at[n], RW)
     g_kv = Gather(s.KVF, T)
-    g_dt = [Gather(s.DT, RW, i * part_size, part_size) for i in range(halves)]
-    g_gu = [Gather(s.GU, RW, i * part_size, part_size) for i in range(halves)]
-    f_wq, f_pt = Spread(s.WQ), Spread(s.PT)
+    g_dt = Gather(s.DT, RW)
+    g_gu = [Gather(s.GU, RW, lanes, y_first=i == 2) for i, lanes in enumerate(cuts)]
+    f_wq, f_pt = Spread(g_wq, s.WQ), Spread(g_pt, s.PT)
     h_mix, h_bg, h_og, h_tg = Share(s.MIX, 4), Share(s.BG, 1), Share(o_out, 1), Share(o_tok, 2)
     n_mb = NarrowSum(s.MB, s.MBC, s.MBX, s.MBS)
     n_op = NarrowSum(s.OP, s.OPC, s.OPX, s.OPS)
     w_kv = WideSum(s.KVF, s.DKVY, s.DKVR, s.DKVO, T)
-    w_gu = WideSum(s.GU, s.YGU, s.RGU, o_gu, RW)
+    w_gu = []
+    for i, lanes in enumerate(cuts):
+        refs_z = s.RZF if i == 2 else s.RGU
+        out = o_gu.at[:, pl.ds(*lanes)]
+        w_gu.append(WideSum(s.GU, s.YGU, refs_z, out, RW, lanes, z_first=i == 2))
     w_dt = WideSum(s.PDT, s.YDT, s.RDT, o_dt, RW)
     w_pt = WideSum(s.PPT, s.YPT, s.RPT, o_pt, RW)
     w_q = WideSum(s.PQ, s.YQ, s.RQ, o_q, RW)
     k_a2a, k_gain = take(3), take(3)
+    assert taken[0] <= rsem.shape[0] and taken[1] <= ssem.shape[0]
 
     own = pl.ds(pl.multiple_of(w * RW, RW), RW)
-    s.WQ[n, own, :] = wq_own[...]
-    g_wq.start()
-    g_wq.start_y(0)
-    s.PT[n, own, :] = pt_own[...]
-    s.GU[own, :] = gu_own[...]
-    s.DT[own, :] = dt_own[...]
-
-    column, head = row_iota(256, D) & (LANES - 1), lane_iota(256, D) >> 6
+    blank = lambda count, kind=bf16: jnp.zeros((count, RW), kind)
+    shared_part = jnp.concatenate([qshared[...].astype(f32), blank(LANES - y.SQ, f32)], axis=0)
+    gain_row = row_iota(8, RW)
+    gain_part = jnp.where(
+        gain_row == 0,
+        prenorm[...].astype(f32),
+        jnp.where(gain_row == 1, midnorm[...].astype(f32), 0.0),
+    )
+    second_part = jnp.concatenate(
+        [part[...].astype(f32) for part in (kshared, vshared, qheads, kheads, vheads)]
+        + [gain_part, blank(LANES - y.og - 8, f32)],
+        axis=0,
+    )
+    s.WQ[n, own, :LANES] = shared_part.T.astype(bf16)
+    s.WQ[n, own, LANES:] = second_part.T.astype(bf16)
+    g_wq.launch()
+    g_wq.launch_y()
+    for first in range(0, 256, LANES):
+        s.PT[n, own, first : first + LANES] = project[first : first + LANES, :].T
+    g_pt.launch()
+    for first in range(0, FM, LANES):
+        s.DT[own, first : first + LANES] = downward[first : first + LANES, :].T
+    s.DT[own, FM:] = jnp.concatenate([downward[FM:, :], blank(FP - F)], axis=0).T
+    for first in range(0, FM, LANES):
+        s.GU[own, first : first + LANES] = gating[first : first + LANES, :].T
+        s.GU[own, FM + first : FM + first + LANES] = upward[first : first + LANES, :].T
+    s.GU[own, 2 * FM :] = jnp.concatenate([gating[FM:, :], upward[FM:, :]], axis=0).T
+    g_gu[2].launch_y()
+
+    column, head = row_iota(LANES, D), lane_iota(LANES, D) >> 6
     for r in range(QR):
         s.EQ[r] = jnp.where(column == head * QR + r, 1.0, 0.0).astype(bf16)
-    column, head = row_iota(LANES, D), lane_iota(LANES, D) >> 6
     for r in range(KR):
         s.EK[r] = jnp.where(column == head * KR + r, 1.0, 0.0).astype(bf16)
         s.EK[KR + r] = jnp.where(column == y.heads * KR + head * VR + r, 1.0, 0.0).astype(bf16)
@@ -452,17 +660,22 @@
 
     mask_block(0)
 
-    g_wq.forward_all()
-    g_pt.start()
-    g_pt.start_y(0)
-    g_dt[0].start()
-    for step in range(A):
-        g_wq.landed(step)
-        f_wq.start(step)
-    for step in range(A):
-        f_wq.forward(step)
-    for step in range(A):
-        f_wq.landed(step)
+    g_wq.pump(1)
+    g_pt.launch_y()
+    f_wq.pump(1)
+    g_wq.pump(1)
+    f_wq.pump(1)
+    g_dt.launch()
+    g_dt.launch_y()
+    g_wq.pump()
+    g_pt.pump(1)
+    f_wq.pump(1)
+    g_pt.pump(1)
+    f_wq.pump()
+    g_pt.pump()
+    g_dt.pump(1)
+    f_wq.pump_forward()
+    f_wq.landed()
 
     gains = s.WQ[0, :, LANES:].astype(f32).T
     s.GAIN[0:1, :] = gains[y.og : y.og + 1]
@@ -493,20 +706,26 @@
         [(second_tiles[p], y.ok, p * y.HK, y.HK) for p in range(N)]
         + [(second_tiles[p], y.ov, (N + p) * y.HK, y.HK) for p in range(N)]
     ).astype(bf16)
-    g_kv.start()
-    g_kv.start_y(0)
+    g_kv.launch()
+    g_kv.launch_y()
+    g_gu[0].launch()
+    g_gu[0].launch_y()
 
     query_heads = collect(y.oq, y.HQ)
     heads_high = query_heads.astype(bf16)
     s.QH[:, :LANES] = heads_high
     s.QH[:, LANES:] = (query_heads - heads_high.astype(f32)).astype(bf16)
+
+    def spread_heads(r):
+        return dot_nn(s.QH[:, :LANES], s.EQ[r]) + dot_nn(s.QH[:, LANES:], s.EQ[r])
+
     queries = jnp.zeros((T, D), f32)
     for r in range(QR):
         pieces = canonical_pieces(first_tiles, y.SQ, r * DH, DH, 0, 0)
         pieces += canonical_pieces(first_tiles, y.SQ, r * DH, DH, 0, DH)
         turned = rotated(place_lanes(pieces))
         s.QROT[r] = turned
-        queries = queries + dot_nn(s.QH[...], s.EQ[r]) * jnp.concatenate([turned] * pairs, axis=1)
+        queries = queries + spread_heads(r) * jnp.concatenate([turned] * pairs, axis=1)
     for i in range(pairs):
         tile = (queries[:, i * LANES : (i + 1) * LANES] * (1.0 / QR)).astype(bf16)
         s.QP[i] = tile * jnp.asarray(DH**-0.5, bf16)
@@ -519,15 +738,16 @@
 
     lax.fori_loop(0, N, norm_rows, 0)
 
-    g_kv.forward_all()
-    bulk = g_dt[1:] + g_gu
-    g_pt.forward_all()
-    for g in bulk:
-        g.start()
-    g_dt[0].start_y(0)
-    g_dt[0].forward_all()
-    for g in bulk:
-        g.start_y(0)
+    g_dt.pump(1)
+    f_pt.pump()
+    g_dt.pump()
+    g_kv.pump(1)
+    g_gu[1].launch()
+    g_gu[1].launch_y()
+    g_kv.pump(1)
+    g_kv.pump()
+    f_pt.pump_forward(2)
+    g_gu[0].pump(1)
     g_kv.landed_all()
 
     def expand_block(block):
@@ -587,6 +807,13 @@
         for chunk in range(h_mix.chunks):
             lax.fori_loop(chunk * per, (chunk + 1) * per, forward_step, 0)
             h_mix.start(chunk)
+            if chunk == 0:
+                g_gu[0].pump(1)
+            elif chunk == 1:
+                g_gu[0].pump()
+                g_gu[2].launch()
+            else:
+                g_gu[1].pump(1)
     else:
         s.LSE[...] = jnp.full(s.LSE.shape, masked_score, f32)
         s.RUN[...] = jnp.zeros(s.RUN.shape, f32)
@@ -614,17 +841,15 @@
         for chunk in range(h_mix.chunks):
             h_mix.start(chunk)
 
-    for step in range(A):
-        g_pt.landed(step)
-        f_pt.start(step)
-    h_mix.finish()
-    for step in range(A):
-        f_pt.forward(step)
-    for g in bulk:
-        g.forward_all()
-    for step in range(A):
-        f_pt.landed(step)
-
+    g_gu[0].pump()
+    if y.NB > 1:
+        g_gu[2].launch()
+    f_pt.pump_forward()
+    h_mix.forward_all()
+    g_gu[1].pump()
+    g_gu[2].pump(1)
+    h_mix.landed_all()
+    f_pt.landed()
     def middle_rows(block, _):
         at = pl.ds(pl.multiple_of(block * 2 * T, 2 * T), 2 * T)
         values = tok[at, :].astype(f32)
@@ -637,7 +862,8 @@
         return 0
 
     lax.fori_loop(0, 2, middle_rows, 0)
-    for g in g_dt + g_gu:
+    g_gu[2].pump()
+    for g in [g_dt] + g_gu:
         g.landed_all()
 
     tail_low = lane_iota(2 * T) < DH
@@ -676,19 +902,21 @@
     n_mb.start(False)
     n_mb.pass_on()
 
-    def grad_blocks(target, left, right, exchange):
+    def grad_blocks(target, left, right, exchanges, lanes=slice(None)):
         per = A // 4
         for j in range(4):
-            block = (zi // per + 1 + j) % 4
-            lanes = pl.ds(pl.multiple_of(block * 256, 256), 256)
-            value = dot_tn(left[:, lanes], right[...]).astype(bf16)
-            target[pl.ds(pl.multiple_of(block * 256, 256), 256), :] = value
-            for q in range(per):
-                exchange.start(block * per + q)
-
+            block = z_order[j] if A == 4 else j
+            at = pl.ds(pl.multiple_of(block * 256, 256), 256)
+            target[at, lanes] = dot_tn(left[:, at], right[:, lanes]).astype(bf16)
+            for exchange in exchanges:
+                for q in range(per):
+                    exchange.start(block * per + q)
+
+    grad_blocks(s.PDT, cot, s.HID, [w_dt])
     for g in g_gu:
         g.sent()
-    grad_blocks(s.GU, s.NM, s.GG, w_gu)
+    grad_blocks(s.GU, s.NM, s.GG, [], slice(cuts[2][0], GUc))
+    w_gu[2].start_ends()
 
     mid_back = n_mb.result()
     mid_own = s.MID[own_rows, :]
@@ -709,7 +937,7 @@
         s.DO[2 * p] = part[:, :LANES]
         s.DO[2 * p + 1] = part[:, LANES:]
 
-    def backward_block(block):
+    def backward_block(block, between=lambda part: None):
         s.DKS[...] = jnp.zeros(s.DKS.shape, f32)
         s.DHD[...] = jnp.zeros(s.DHD.shape, f32)
 
@@ -739,7 +967,10 @@
             s.DHD[...] = found
             return 0
 
-        lax.fori_loop(0, pairs, step, 0)
+        quarter = pairs // 4
+        for part in range(4):
+            lax.fori_loop(part * quarter, (part + 1) * quarter, step, 0)
+            between(part)
         at = pl.ds(pl.multiple_of(block * KB, KB), KB)
         low = lane_iota(KB) < DH
         for e in (0, KR):
@@ -750,7 +981,13 @@
     s.QB[...] = jnp.zeros(s.QB.shape, f32)
     g_kv.sent()
     if y.NB == 1:
-        backward_block(0)
+
+        def between(part):
+            if part < 3:
+                w_dt.pump(1)
+                w_gu[2].pump(2 if part == 0 else 1)
+
+        backward_block(0, between)
     else:
 
         def backward_step(block, _):
@@ -760,17 +997,21 @@
             return 0
 
         lax.fori_loop(0, y.NB, backward_step, 0)
-    w_kv.start_all()
-    grad_blocks(s.PDT, cot, s.HID, w_dt)
-
+    for z in z_order:
+        w_kv.start(z)
+    for i in range(2):
+        grad_blocks(s.GU, s.NM, s.GG, [w_gu[i]], slice(cuts[i][0], sum(cuts[i])))
+    w_gu[2].pump()
+    w_gu[2].finish()
+    w_kv.pump(1)
     query_back = jnp.concatenate([s.QB[i] for i in range(pairs)], axis=1)
     heads_back = jnp.zeros((T, LANES), f32)
     shared_back = []
     for r in range(QR):
         turned = s.QROT[r]
         product = (query_back * jnp.concatenate([turned] * pairs, axis=1)).astype(bf16)
-        heads_back = heads_back + dot_nt(product, s.EQ[r, :LANES, :])
-        product = dot_nn(s.QH[...], s.EQ[r]) * query_back
+        heads_back = heads_back + dot_nt(product, s.EQ[r])
+        product = spread_heads(r) * query_back
         total = product[:, :LANES]
         for i in range(1, pairs):
             total = total + product[:, i * LANES : (i + 1) * LANES]
@@ -782,15 +1023,16 @@
     ]
     heads_back = heads_back * (1.0 / QR)
 
+    w_kv.pump(1)
     for far in (True, False):
         block = (1 - xo) if far else xo
         at = pl.ds(pl.multiple_of(block * 2 * T, 2 * T), 2 * T)
         s.OP[at, :] = dot_nt(s.HID[at, :], s.DT[...]).astype(bf16)
         n_op.start(far)
+    w_kv.pump()
     n_op.pass_on()
-
-    for step in list(range(1, A)) + [0]:
-        w_kv.pass_on(step)
+    w_dt.pump()
+    w_dt.finish()
     w_kv.finish()
 
     key_shared = rotated(s.DKVO[:, 0:128], back=True)
@@ -834,9 +1076,10 @@
     o_out[own_rows, :] = (s.MID[own_rows, :] + n_op.result()).astype(bf16)
     h_og.start(0)
 
+    w_gu[0].pump(1)
     h_bg.finish()
-    grad_blocks(s.PPT, s.BG, s.MIX.at[:, pl.ds(pl.multiple_of(n * 256, 256), 256)], w_pt)
-
+    grad_blocks(s.PPT, s.BG, s.MIX.at[:, pl.ds(pl.multiple_of(n * 256, 256), 256)], [w_pt])
+    w_gu[0].pump(1)
     for k, peer in enumerate(narrow_peers):
         arrive(s.QGR.at[peer[1]], k_a2a + k)
     for k in range(3):
@@ -851,29 +1094,72 @@
         jnp.where(lane_row == y.og + 1, gain_rows[1:2], 0.0),
     )
     gain_columns = spread.T
-    per = A // 4
     for j in range(4):
-        block = (zi // per + 1 + j) % 4
+        block = z_order[j] if A == 4 else j
         lanes = pl.ds(pl.multiple_of(block * 256, 256), 256)
         value = jnp.zeros((256, 256), f32)
         for p in range(N):
             value = value + dot_tn(s.NORM[p * T : (p + 1) * T, lanes], s.QGR[p])
         s.PQ[pl.ds(pl.multiple_of(block * 256, 256), 256), :] = value.astype(bf16)
     s.PQ[:, LANES:] = (s.PQ[:, LANES:].astype(f32) + gain_columns).astype(bf16)
-    w_q.start_all()
-
-    for exchange in (w_gu, w_dt, w_pt, w_q):
-        for step in list(range(1, A)) + [0]:
-            exchange.pass_on(step)
-
+    for z in z_order:
+        w_q.start(z)
+
+    w_gu[0].pump()
+    w_gu[1].pump(1)
+    w_gu[0].finish()
+    w_gu[1].pump(1)
+    w_pt.pump(1)
+    w_gu[1].pump()
+    w_pt.pump(1)
+    w_q.pump(1)
     h_tg.finish()
+    write(o_tok, r_tok)
     h_og.finish()
-    for exchange in (w_gu, w_dt, w_pt, w_q):
-        exchange.finish()
-    for g in [g_wq, g_pt] + g_dt:
-        g.sent()
+    write(o_out, r_out)
+    w_gu[1].finish()
+    w_gu[2].finish_y()
+    write(o_gu, r_gu)
+    write(o_dt, r_dt)
+    w_pt.pump()
+    w_q.pump(1)
+    w_pt.finish()
+    write(o_pt, r_pt)
+    w_q.pump()
+    w_q.finish()
+    write(o_q, r_q)
+    for exchange in (g_wq, g_pt, g_dt, f_wq, f_pt, w_kv, w_dt, *w_gu, w_pt, w_q):
+        exchange.sent()
     for copy in pending:
         copy.wait_send()
+    for copy in written:
+        copy.wait()
+
+
+def results_kernel(y, out, tok, gu, dt, pt, q, *outs):
+    o_out, o_tok, o_pre, o_qh, o_qs, o_kh, o_ks, o_vh, o_vs, o_pt, o_mid, o_gate, o_up, o_down = outs
+    FM, F, half = y.FM, y.F, y.F - y.FM
+    o_out[...] = out[...]
+    o_tok[...] = tok[...].astype(f32)
+    o_qs[...] = q[:, :LANES].T[: y.SQ]
+    second = q[:, LANES:].T
+    o_ks[...] = second[y.oK : y.oK + y.SK]
+    o_vs[...] = second[y.oV : y.oV + y.SK]
+    o_qh[...] = second[y.oq : y.oq + y.HQ]
+    o_kh[...] = second[y.ok : y.ok + y.HK]
+    o_vh[...] = second[y.ov : y.ov + y.HK]
+    o_pre[...] = second[y.og : y.og + 1]
+    o_mid[...] = second[y.og + 1 : y.og + 2]
+    for first in range(0, 256, LANES):
+        o_pt[first : first + LANES, :] = pt[:, first : first + LANES].T
+    for first in range(0, FM, LANES):
+        o_down[first : first + LANES, :] = dt[:, first : first + LANES].T
+        o_gate[first : first + LANES, :] = gu[:, first : first + LANES].T
+        o_up[first : first + LANES, :] = gu[:, FM + first : FM + first + LANES].T
+    tail = gu[:, 2 * FM :].T
+    o_gate[FM:, :] = tail[:half]
+    o_up[FM:, :] = tail[half:]
+    o_down[FM:, :] = dt[:, FM:].T[:half]
 
 
 def solution(mesh):
@@ -901,47 +1187,30 @@
         RW, F = gating.shape
         y = make_layout(W, N, T, D, F, L, N * kheads.shape[1] // KR)
         assert R == N
-        FM = y.FM
-        zeros = lambda count: jnp.zeros((RW, count), bf16)
-        wq = jnp.concatenate(
-            [
-                qshared,
-                zeros(LANES - y.SQ),
-                kshared,
-                vshared,
-                qheads,
-                kheads,
-                vheads,
-                prenorm[:, None],
-                midnorm[:, None],
-                zeros(LANES - y.og - 2),
-            ],
-            axis=1,
-        )
-        gu = jnp.concatenate([gating[:, :FM], upward[:, :FM], gating[:, FM:], upward[:, FM:]], axis=1)
-        dt = jnp.pad(downward.T, ((0, 0), (0, y.FP - F)))
-        pt = project.T
         scratch = scratch_list(y)
-        copies = 256 + 48 * y.A
+        arrivals = 33 * y.A + 44
+        sends = arrivals + 14 * y.A
         vmem = pl.BlockSpec(memory_space=pltpu.VMEM)
 
         def kernel(*refs):
             block_kernel(y, tuple(scratch), *refs)
 
         shape = jax.ShapeDtypeStruct
-        out, tok, gu_back, dt_back, pt_back, q_back = pl.pallas_call(
+        width = 2 * y.FM + LANES
+        raw = pl.pallas_call(
             kernel,
             out_shape=(
                 shape((y.M, D), bf16),
                 shape((y.M, D), bf16),
-                shape((RW, 2 * FM + LANES), f32),
+                shape((RW, width), f32),
                 shape((RW, y.FP), f32),
                 shape((RW, 256), f32),
                 shape((RW, 256), f32),
             ),
-            in_specs=[vmem] * 7,
-            out_specs=[vmem] * 6,
-            scratch_shapes=[*scratch.values()] + [pltpu.SemaphoreType.DMA((copies,))] * 2,
+            in_specs=[vmem] * 15,
+            out_specs=[pl.BlockSpec(memory_space=pl.ANY)] * 6,
+            scratch_shapes=[*scratch.values()]
+            + [pltpu.SemaphoreType.DMA((count,)) for count in (sends, arrivals, 6)],
             compiler_params=pltpu.CompilerParams(
                 collective_id=0, has_side_effects=True, vmem_limit_bytes=63 * 2**20
             ),
@@ -949,30 +1218,54 @@
         )(
             tokens.reshape(y.M, D),
             documents,
-            wq,
-            gu,
-            dt,
-            pt,
+            prenorm.reshape(1, RW),
+            qheads.T,
+            qshared.T,
+            kheads.T,
+            kshared.T,
+            vheads.T,
+            vshared.T,
+            project,
+            midnorm.reshape(1, RW),
+            gating.T,
+            upward.T,
+            downward,
             cotangent.reshape(y.M, D),
         )
-        second = lambda first, count: q_back[:, LANES + first : LANES + first + count]
-        half = F - FM
-        return (
-            out.reshape(R, T, D),
-            tok.astype(f32).reshape(R, T, D),
-            second(y.og, 1).reshape(RW),
-            second(y.oq, y.HQ),
-            q_back[:, : y.SQ],
-            second(y.ok, y.HK),
-            second(y.oK, y.SK),
-            second(y.ov, y.HK),
-            second(y.oV, y.SK),
-            pt_back.T,
-            second(y.og + 1, 1).reshape(RW),
-            jnp.concatenate([gu_back[:, :FM], gu_back[:, 2 * FM : 2 * FM + half]], axis=1),
-            jnp.concatenate([gu_back[:, FM : 2 * FM], gu_back[:, 2 * FM + half :]], axis=1),
-            dt_back[:, :F].T,
-        )
+
+        def results(*refs):
+            results_kernel(y, *refs)
+
+        outputs = pl.pallas_call(
+            results,
+            out_shape=(
+                shape((y.M, D), bf16),
+                shape((y.M, D), f32),
+                shape((1, RW), f32),
+                shape((y.HQ, RW), f32),
+                shape((y.SQ, RW), f32),
+                shape((y.HK, RW), f32),
+                shape((y.SK, RW), f32),
+                shape((y.HK, RW), f32),
+                shape((y.SK, RW), f32),
+                shape((256, RW), f32),
+                shape((1, RW), f32),
+                shape((F, RW), f32),
+                shape((F, RW), f32),
+                shape((F, RW), f32),
+            ),
+            in_specs=[vmem] * 6,
+            out_specs=[vmem] * 14,
+            compiler_params=pltpu.CompilerParams(vmem_limit_bytes=63 * 2**20),
+            name="results",
+        )(*raw)
+        turned = (3, 4, 5, 6, 7, 8, 11, 12)
+        outputs = [v.T if i in turned else v for i, v in enumerate(outputs)]
+        outputs[0] = outputs[0].reshape(R, T, D)
+        outputs[1] = outputs[1].reshape(R, T, D)
+        outputs[2] = outputs[2].reshape(RW)
+        outputs[10] = outputs[10].reshape(RW)
+        return tuple(outputs)
 
     split = P("wide", "narrow")
     flipped = P("narrow", "wide")

time: 257 us -> 173 us (0.67)
  Pallas kernels: 225 us -> 172 us
  local copies, waits for them, and re-layouts: 28.7 us -> 0 us
    pallas_call x1, Pallas kernels: 225 us -> 168 us  [on_device(): pl.pallas_call(kernel, out_shape=(shape((y.M, D), bf16), shape((y.M, D),...]
    unnamed x33 -> x0, local copies, waits for them, and re-layouts: 16.6 us -> none
    slice x12 -> x0, local copies, waits for them, and re-layouts: 8.09 us -> none  [the longest x4 2.69 us: on_device(): second = lambda first, count: q_back[:, LANES + first:LANES + first + count]]
    pallas_call x0 -> x1, Pallas kernels: none -> 4.37 us  [on_device(): pl.pallas_call(results, out_shape=(shape((y.M, D), bf16), shape((y.M, D),...]
where the time goes in v2:
time: 173 us
  Pallas kernels  172 us (99%)
    pallas_call x1, Pallas kernels, on_device(): pl.pallas_call(kernel, out_shape=(shape((y.M, D), bf16), shape((y.M, D),...  168 us
    pallas_call x1, Pallas kernels, on_device(): pl.pallas_call(results, out_shape=(shape((y.M, D), bf16), shape((y.M, D),...  4.37 us

profile of v2, /device:TPU:0, one launch (start us, length us, event | category | flops | bytes accessed | tf_op | source)
XLA Modules:
  0.0 173.2 jit_solution(10123183552091288617)
XLA Ops:
  0.7 168.0 %block.1 = (bf16[512,1024]{1,0:T(8,128)(2,1)}, bf16[512,1024]{1,0:T(8,128)(2,1)}, f32[128,1408]{1,0:T(8,128)}, f32[128,768]{1,0:T(8,128)}, f32[128,256]{1,0:T(8,128)}, /*index=5*/f32[128,256]{1,0:T(8,128)}) custom-call(bf16[512,1024]{1,0:T(8,128)(2,1)} %bitcast.24, s32[4,1024]{1,0:T(4,128)} %refs_1_.1, bf16[1,128]{1,0:T(2,128)(2,1)} %bitcast.34, ...), custom_call_target="tpu_custom_call" | custom-call | tf_op jit(solution)/shard_map/block/pallas_call | solution.py:1200
  168.6 4.4 %results.1 = (bf16[512,1024]{1,0:T(8,128)(2,1)}, f32[512,1024]{1,0:T(8,128)}, f32[1,128]{1,0:T(1,128)}, f32[24,128]{1,0:T(8,128)}, f32[96,128]{1,0:T(8,128)}, /*...) custom-call(bf16[512,1024]{1,0:T(8,128)(2,1)} %get-tuple-element.34., ...), custom_call_target="tpu_custom_call" | custom-call | tf_op jit(solution)/shard_map/results/pallas_call | solution.py:1239

commit v3 on v2

v3 whole, which is shorter than its diff:
```python
import math
from types import SimpleNamespace

import jax
import jax.numpy as jnp
from jax import lax
from jax.experimental import pallas as pl
from jax.experimental.pallas import tpu as pltpu
from jax.sharding import PartitionSpec as P

DH = 64
QR = 6
KR = 2
VR = 2
LANES = 128

epsilon = 1e-06
masked_score = -1e30
MESH = pl.DeviceIdType.MESH
y_first_chunks = (2,)
z_first_chunks = (2,)
f32 = jnp.float32
bf16 = jnp.bfloat16


def dot_nn(a, b):
    return lax.dot_general(a, b, (((1,), (0,)), ((), ())), preferred_element_type=f32)


def dot_nt(a, b):
    return lax.dot_general(a, b, (((1,), (1,)), ((), ())), preferred_element_type=f32)


def dot_tn(a, b):
    return lax.dot_general(a, b, (((0,), (0,)), ((), ())), preferred_element_type=f32)


def lane_iota(rows, cols=LANES):
    return lax.broadcasted_iota(jnp.int32, (rows, cols), 1)


def row_iota(rows, cols=LANES):
    return lax.broadcasted_iota(jnp.int32, (rows, cols), 0)


def place_lanes(pieces):
    rows = pieces[0][0].shape[0]
    lane = lane_iota(rows)
    result = jnp.zeros((rows, LANES), f32)
    for tile, start, to, count in pieces:
        shift = (to - start) % LANES
        moved = pltpu.roll(tile, shift, 1) if shift else tile
        result = jnp.where((lane >= to) & (lane < to + count), moved, result)
    return result


def canonical_pieces(tiles, width, first, count, start, to):
    pieces = []
    while count:
        part, inside = divmod(first, width)
        take = min(count, width - inside)
        pieces.append((tiles[part], start + inside, to, take))
        first, to, count = first + take, to + take, count - take
    return pieces


def both_halves(tile):
    low = lane_iota(tile.shape[0]) < DH
    turned = pltpu.roll(tile, DH, 1)
    return jnp.where(low, tile, turned), jnp.where(low, turned, tile)


def swap_quarters(tile):
    low = lane_iota(tile.shape[0]) % DH < DH // 2
    return jnp.where(low, pltpu.roll(tile, LANES - DH // 2, 1), pltpu.roll(tile, DH // 2, 1))


def stack_pair(tile):
    low = lane_iota(tile.shape[0]) < DH
    zero = jnp.zeros_like(tile)
    return jnp.concatenate([jnp.where(low, tile, zero), jnp.where(low, zero, tile)], axis=0)


def unstack_pair(rows):
    half = rows.shape[0] // 2
    low = lane_iota(half) < DH
    return jnp.where(low, rows[:half], rows[half:])


def fold_halves(tile):
    return tile + pltpu.roll(tile, DH, 1)


def row_scale(values):
    return lax.rsqrt(jnp.mean(values * values, axis=-1, keepdims=True) + epsilon)


def make_layout(W, N, T, D, F, L, heads):
    lay = SimpleNamespace()
    lay.W, lay.N, lay.T, lay.D, lay.F, lay.L, lay.heads = W, N, T, D, F, L, heads
    lay.A = W // 2
    lay.RW = D // W
    lay.M = N * T
    lay.FM = F // LANES * LANES
    lay.FP = lay.FM + LANES
    full = lay.FM // 256
    lay.chunks = [(768 * i, 512, 256 * i, 256) for i in range(full)]
    lay.chunks.append((768 * full, 3 * LANES, 256 * full, 256))
    lay.FW = 768 * full + 5 * LANES
    assert lay.FM % 256 == LANES
    lay.pairs = heads // 2
    assert len(lay.chunks) == 3
    lay.KB = L if L <= 1024 else 512
    lay.NB = L // lay.KB
    lay.SQ = QR * DH // N
    lay.SK = KR * DH // N
    lay.HQ = heads * QR // N
    lay.HK = heads * KR // N
    lay.oK, lay.oV = 0, lay.SK
    lay.oq = 2 * lay.SK
    lay.ok = lay.oq + lay.HQ
    lay.ov = lay.ok + lay.HK
    lay.og = lay.ov + lay.HK
    assert N == 4 and W % 8 == 0 and T == LANES and D == heads * DH == 1024
    assert F % LANES == DH and lay.SQ <= LANES and lay.og + 2 <= LANES
    return lay


def scratch_list(y):
    W, N, T, D, L, A, RW, M = y.W, y.N, y.T, y.D, y.L, y.A, y.RW, y.M
    vm = lambda *shape, kind=bf16: pltpu.VMEM(shape, kind)
    GUc = 2 * y.FM + LANES
    return dict(
        WQ=vm(N, D, 256),
        PT=vm(N, D, 256),
        FW=vm(D, y.FW),
        KVF=vm(L, 384),
        KP=vm(y.pairs, LANES, y.KB),
        VP=vm(y.pairs, LANES, y.KB),
        EQ=vm(QR, LANES, D),
        SHARED=vm(2, LANES, y.KB, kind=f32),
        HT=vm(y.pairs, 8, y.KB, kind=f32),
        DHT=vm(y.pairs, 8, y.KB, kind=f32),
        BIAS=vm(T, y.KB, kind=f32),
        DOC=vm(T, LANES, kind=f32),
        ROPE=vm(2, T, LANES, kind=f32),
        GAIN=vm(8, D, kind=f32),
        QROT=vm(QR, T, LANES, kind=f32),
        QH=vm(T, 256),
        QP=vm(y.pairs, T, LANES),
        ATT=vm(y.pairs, T, LANES, kind=f32),
        LSE=vm(y.pairs, 2 * T, LANES, kind=f32),
        RUN=vm(y.pairs if y.NB > 1 else 1, 2 * T, LANES, kind=f32),
        MIX=vm(M, D),
        NORM=vm(M, D),
        MID=vm(M, D, kind=f32),
        NM=vm(M, D),
        R2=vm(M, LANES, kind=f32),
        HID=vm(M, y.FP),
        GG=vm(M, GUc),
        MB=vm(M, D),
        MBC=vm(2, T, D),
        MBX=vm(T, D),
        MBS=vm(T, D),
        OP=vm(M, D),
        OPC=vm(2, T, D),
        OPX=vm(T, D),
        OPS=vm(T, D),
        BG=vm(M, D),
        MG=vm(T, D, kind=f32),
        DO=vm(y.pairs, T, LANES),
        QB=vm(y.pairs, T, LANES, kind=f32),
        DST=vm(2, LANES, y.KB, kind=f32),
        DKVY=vm(A * T, 384),
        DKVR=vm((A + 1) * T, 384),
        DKVO=vm(T, 384, kind=f32),
        QGS=vm(N, T, 256),
        QGR=vm(N, T, 256),
        OUT=vm(M, D),
        TOK=vm(M, D),
        TFW=vm(RW, y.FW, kind=f32),
        TPT=vm(RW, 256, kind=f32),
        TQ=vm(RW, 256, kind=f32),
        GS=vm(8, D, kind=f32),
        GR=vm(3, 8, D, kind=f32),
        YFW=vm(A * RW, y.FW),
        **{
            f"RF{i}": vm((A + 1) * RW * (2 if i in z_first_chunks else 1), wide + units)
            for i, (_, wide, _, units) in enumerate(y.chunks)
        },
        PPT=vm(D, 256),
        YPT=vm(A * RW, 256),
        RPT=vm((A + 1) * RW, 256),
        PQ=vm(D, 256),
        YQ=vm(A * RW, 256),
        RQ=vm((A + 1) * RW, 256),
    )


schedule = (
    "prep_wq", "wq.L", "wq.Ly", "prep_pt", "pt.Ly", "pt.L", "wq.h1", "fwq.s0", "prep_fw", "c.Ly",
    "b.L", "consts", "wq.h2", "fwq.s1", "pt.h1", "b.h1", "fwq.s2", "a.L", "b.Ly", "wq.h3", "b.h2",
    "pt.h2", "fwq.s3", "fwq.f0", "fwq.f1", "fwq.f2", "b.y1", "fpt.s0", "c.L", "b.y2", "a.Ly",
    "fwq.f3", "project", "kv.L", "pt.h3", "kv.h1", "kv.h2", "fpt.s1", "fpt.f0", "kv.Ly", "a.h1",
    "kv.h3", "a.h2", "b.h3", "a.y1", "a.y2", "fpt.s2", "fpt.s3", "c.h1", "queries", "at_x", "at0",
    "at1", "a.h3", "a.y3", "fpt.f1", "fpt.f2", "at2", "at3", "mix.f0", "mix.f1", "c.h2", "fpt.f3",
    "mix.f2", "b.y3", "mix.f3", "middle", "ff_a", "ff_b", "c.h3", "ffCf", "ffCn", "mb.pass",
    "g_c", "wc.ends", "g_b", "mid", "bq0", "op.start", "wc.s1", "bq1", "bq2", "bq3", "wc.s2",
    "op.pass", "kvst", "bg.f", "wb.s0", "pt.g", "wkv.d0", "wb.s1", "op.res", "qb", "wpt.d0",
    "wkv.d1", "wkv.d2", "g_a", "wb.s2", "wa.s0", "wpt.d1", "wkv.fin", "qg", "wc.fin", "wa.s1",
    "fb", "q.g", "og.f", "wa.s2", "wc.finy", "wpt.d2", "tg.f", "wq2.d0", "wq2.d1", "tg.l",
    "wq2.d2", "wa.fin", "wpt.fin", "og.l", "wb.fin", "wq2.fin",
)


def block_kernel(y, names, *refs):
    tok, docs, prenorm, qheads, qshared, kheads, kshared, vheads, vshared = refs[:9]
    project, midnorm, gating, upward, downward, cot = refs[9:15]
    r_out, r_tok, r_fw, r_pt, r_q = refs[15:20]
    s = SimpleNamespace(**dict(zip(names, refs[20:])))
    ssem, rsem, wsem = refs[20 + len(names) :]
    o_out, o_tok, o_fw, o_pt, o_q = s.OUT, s.TOK, s.TFW, s.TPT, s.TQ
    written = []

    def write(src, dst):
        copy = pltpu.make_async_copy(src, dst, wsem.at[len(written)])
        copy.start()
        written.append(copy)

    W, N, T, D, F, L, A, RW, M = y.W, y.N, y.T, y.D, y.F, y.L, y.A, y.RW, y.M
    FM, FP, KB, pairs = y.FM, y.FP, y.KB, y.pairs
    w = lax.axis_index("wide")
    n = lax.axis_index("narrow")
    zi, yi = w // 2, w % 2
    xo, co = n // 2, n % 2
    y_peer = (zi * 2 + 1 - yi, n)
    c_peer = (w, xo * 2 + 1 - co)
    x_peer = (w, (1 - xo) * 2 + co)
    d_peer = (w, (1 - xo) * 2 + 1 - co)
    narrow_peers = (c_peer, x_peer, d_peer)
    taken = [0, rsem.shape[0]]

    def take(count=1):
        taken[0] += count
        return taken[0] - count

    def take_send(count):
        taken[1] += count
        return taken[1] - count

    def remote(src, dst, k, peer, send_k=None):
        return pltpu.make_async_remote_copy(
            src_ref=src,
            dst_ref=dst,
            send_sem=ssem.at[k if send_k is None else send_k],
            recv_sem=rsem.at[k],
            device_id=peer,
            device_id_type=MESH,
        )

    pending = []

    def send(src, dst, k, peer, started=pending):
        copy = remote(src, dst, k, peer)
        copy.start()
        started.append(copy)

    def arrive(dst, k):
        remote(dst, dst, k, y_peer).wait_recv()

    def rows(ref, first, count, lanes=None):
        at = pl.ds(pl.multiple_of(first, 16), count)
        return ref.at[at] if lanes is None else ref.at[at, pl.ds(*lanes)]

    def each_at(distance, act):
        if distance == 0:
            act(zi, None)
            return
        pl.when(zi >= distance)(lambda: act(zi - distance, True))
        pl.when(zi + distance < A)(lambda: act(zi + distance, False))

    right_peer = ((zi + 1) * 2 + yi, n)
    left_peer = ((zi - 1) * 2 + yi, n)

    barrier = pltpu.get_barrier_semaphore()
    z_peers = [(((zi + step) % A) * 2 + yi, n) for step in range(1, A)]
    peers = [y_peer, *narrow_peers, *z_peers]
    for peer in peers:
        pl.semaphore_signal(barrier, inc=1, device_id=peer, device_id_type=MESH)
    pl.semaphore_wait(barrier, len(peers))

    class Gather:
        def __init__(self, ref, count, lanes=None, y_first=False):
            self.ref, self.count, self.lanes, self.y_first = ref, count, lanes, y_first
            self.kz, self.ky, self.kl = take(A), take(A), take_send(A)
            self.next = self.next_y = 1

        def part(self, wide):
            return rows(self.ref, wide * self.count, self.count, self.lanes)

        def block(self, z):
            if self.y_first:
                return rows(self.ref, z * 2 * self.count, 2 * self.count, self.lanes)
            return self.part(z * 2 + yi)

        def along(self, z, to_right):
            block = self.block(z)
            if to_right:
                return remote(block, block, self.kz + z, right_peer)
            return remote(block, block, self.kz + z, left_peer, self.kl + z)

        def across(self, z):
            part = self.part(z * 2 + yi)
            return remote(part, part, self.ky + z, y_peer)

        def landed(self, z):
            arrive(self.part(z * 2 + 1 - yi), self.ky + z)

        def launch_y(self):
            self.across(zi).start()

        def launch(self):
            if self.y_first:
                self.landed(zi)
            pl.when(zi < A - 1)(lambda: self.along(zi, True).start())
            pl.when(zi > 0)(lambda: self.along(zi, False).start())

        def hop(self, distance, across):
            def act(z, to_right):
                arrive(self.block(z), self.kz + z)
                more = zi < A - 1 if to_right else zi > 0
                pl.when(more)(lambda: self.along(z, to_right).start())
                if across and not self.y_first:
                    self.across(z).start()

            each_at(distance, act)

        def pump(self, count=A, across=True):
            for _ in range(min(count, A - self.next)):
                self.hop(self.next, across)
                self.next += 1

        def pump_y(self, count=A):
            for _ in range(min(count, self.next - self.next_y)):
                each_at(self.next_y, lambda z, _: self.across(z).start())
                self.next_y += 1

        def landed_all(self):
            if not self.y_first:
                for z in range(A):
                    self.landed(z)

        def sent(self):
            self.across(zi).wait_send()
            pl.when(zi < A - 1)(lambda: self.along(zi, True).wait_send())
            pl.when(zi > 0)(lambda: self.along(zi, False).wait_send())
            for distance in range(1, A):

                def act(z, to_right):
                    more = zi < A - 1 if to_right else zi > 0
                    pl.when(more)(lambda: self.along(z, to_right).wait_send())
                    if not self.y_first:
                        self.across(z).wait_send()

                each_at(distance, act)

    class Spread:
        def __init__(self, gather, ref):
            self.gather, self.ref = gather, ref
            self.next = self.passed = 0
            self.kx, self.kc, self.kd = take(A), take(A), take(A)

        def part(self, owner, z):
            return rows(self.ref.at[owner], z * 2 * RW, 2 * RW)

        def copies(self, z):
            part = self.part(n, z)
            return remote(part, part, self.kx + z, x_peer), remote(part, part, self.kc + z, c_peer)

        def onward(self, z):
            part = self.part(x_peer[1], z)
            return remote(part, part, self.kd + z, c_peer)

        def start(self, distance):
            def act(z, _):
                self.gather.landed(z)
                for copy in self.copies(z):
                    copy.start()

            each_at(distance, act)

        def pump(self, count=A):
            for _ in range(min(count, A - self.next)):
                self.start(self.next)
                self.next += 1

        def pump_forward(self, count=A):
            for _ in range(min(count, A - self.passed)):
                self.forward(self.passed)
                self.passed += 1

        def forward(self, distance):
            def act(z, _):
                arrive(self.part(x_peer[1], z), self.kx + z)
                self.onward(z).start()

            each_at(distance, act)

        def landed(self):
            for z in range(A):
                arrive(self.part(c_peer[1], z), self.kc + z)
                arrive(self.part(d_peer[1], z), self.kd + z)

        def sent(self):
            for z in range(A):
                for copy in self.copies(z):
                    copy.wait_send()
                self.onward(z).wait_send()

    class Share:
        def __init__(self, ref, chunks):
            self.ref, self.chunks = ref, chunks
            self.kx, self.kc, self.kd = take(chunks), take(chunks), take(chunks)
            self.width = D // chunks

        def part(self, owner, chunk):
            lanes = pl.ds(pl.multiple_of(chunk * self.width, LANES), self.width)
            return self.ref.at[pl.ds(pl.multiple_of(owner * T, T), T), lanes]

        def start(self, chunk):
            send(self.part(n, chunk), self.part(n, chunk), self.kx + chunk, x_peer)
            send(self.part(n, chunk), self.part(n, chunk), self.kc + chunk, c_peer)

        def forward(self, chunk):
            part = self.part(x_peer[1], chunk)
            arrive(part, self.kx + chunk)
            send(part, part, self.kd + chunk, c_peer)

        def landed(self, chunk):
            arrive(self.part(c_peer[1], chunk), self.kc + chunk)
            arrive(self.part(d_peer[1], chunk), self.kd + chunk)

        def forward_all(self):
            for chunk in range(self.chunks):
                self.forward(chunk)

        def landed_all(self):
            for chunk in range(self.chunks):
                self.landed(chunk)

        def finish(self):
            self.forward_all()
            self.landed_all()

    class NarrowSum:
        def __init__(self, part_ref, core_ref, x_ref, send_ref):
            self.ref, self.core, self.x, self.out = part_ref, core_ref, x_ref, send_ref
            self.kc, self.kx = take(2), take(1)

        def part(self, owner):
            return rows(self.ref, owner * T, T)

        def start(self, far):
            owner = ((1 - xo) if far else xo) * 2 + 1 - co
            send(self.part(owner), self.core.at[int(far)], self.kc + int(far), c_peer)

        def pass_on(self):
            arrive(self.core.at[1], self.kc + 1)
            total = self.part((1 - xo) * 2 + co)[...].astype(f32) + self.core[1].astype(f32)
            self.out[...] = total.astype(bf16)
            send(self.out, self.x, self.kx, x_peer)

        def result(self):
            arrive(self.core.at[0], self.kc)
            arrive(self.x, self.kx)
            return (
                self.part(n)[...].astype(f32) + self.core[0].astype(f32) + self.x[...].astype(f32)
            )

    class WideSum:
        def __init__(self, part_ref, y_ref, z_ref, out_ref, count, lanes=None, z_first=False):
            self.ref, self.y, self.z, self.total = part_ref, y_ref, z_ref, out_ref
            self.count, self.lanes, self.z_first = count, lanes, z_first
            self.size = 2 * count if z_first else count
            self.next = 0
            self.z_lanes = lanes and (0, lanes[1])
            self.ky, self.kz, self.kl = take(1 if z_first else A), take(A + 1), take_send(A)

        def part(self, wide):
            return rows(self.ref, wide * self.count, self.count, self.lanes)

        def block(self, z):
            if self.z_first:
                return rows(self.ref, z * 2 * self.count, 2 * self.count, self.lanes)
            return self.part(z * 2 + yi)

        def got_y(self, z):
            return rows(self.y, z * self.count, self.count, self.lanes)

        def got_z(self, slot):
            return rows(self.z, slot * self.size, self.size, self.z_lanes)

        def across(self, z):
            return remote(self.part(z * 2 + 1 - yi), self.got_y(z), self.ky + z, y_peer)

        def along(self, z, to_right):
            block = self.block(z)
            if to_right:
                return remote(block, self.got_z(z), self.kz + z, right_peer)
            slot = jnp.where(z == zi - 1, A, z)
            return remote(block, self.got_z(slot), self.kz + slot, left_peer, self.kl + z)

        def start(self, z):
            if not self.z_first:
                self.across(z).start()

        def gather_y(self, z):
            block = self.block(z)[...].astype(f32)
            if self.z_first:
                return block
            arrive(self.got_y(z), self.ky + z)
            return block + self.got_y(z)[...].astype(f32)

        def stage(self, step):
            def move(z, to_right, joined):
                value = self.gather_y(z)
                if joined:
                    arrive(self.got_z(z), self.kz + z)
                    value = value + self.got_z(z)[...].astype(f32)
                self.block(z)[...] = value.astype(bf16)
                self.along(z, to_right).start()

            right, left = A - 1 - step + zi, step - (A - 1 - zi)
            to_right = (right < A) & (right > zi)
            to_left = (left >= 0) & (left < zi)
            pl.when(to_right & (zi > 0))(lambda: move(right, True, True))
            pl.when(to_left & (zi < A - 1))(lambda: move(left, False, True))
            if not self.z_first:
                pl.when(to_right & (zi == 0))(lambda: move(right, True, False))
                pl.when(to_left & (zi == A - 1))(lambda: move(left, False, False))

        def pump(self, count=A):
            for _ in range(min(count, A - 1 - self.next)):
                self.stage(self.next)
                self.next += 1

        def send_direct(self, count=A):
            for k in range(self.next, min(self.next + count, A - 1)):
                self.next += 1
                z = z_order[k] if A == 4 else (zi + 1 + k) % A
                block = self.block(z)
                block[...] = self.gather_y(z).astype(bf16)
                self.direct(z).start()

        def direct(self, z):
            return remote(
                self.block(z), self.got_z(zi), self.kz + zi, (z * 2 + yi, n), self.kl + z
            )

        def finish_direct(self):
            self.total[...] = self.gather_y(zi)
            for step in range(1, A):
                self.add((zi + step) % A)

        def sent_direct(self):
            for z in range(A):
                self.across(z).wait_send()
                pl.when(zi != z)(lambda: self.direct(z).wait_send())

        def start_ends(self):
            @pl.when(zi == 0)
            def _():
                for z in range(A - 1, 0, -1):
                    self.along(z, True).start()

            @pl.when(zi == A - 1)
            def _():
                for z in range(A - 1):
                    self.along(z, False).start()

        def add(self, slot):
            arrive(self.got_z(slot), self.kz + slot)
            got = self.got_z(slot)[...].astype(f32)
            if not self.z_first:
                self.total[...] += got
                return
            block = self.block(zi)
            block[...] = (block[...].astype(f32) + got).astype(bf16)

        def finish(self):
            if not self.z_first:
                self.total[...] = self.gather_y(zi)
            pl.when(zi > 0)(lambda: self.add(zi))
            pl.when(zi < A - 1)(lambda: self.add(A))
            if self.z_first:
                self.last_across().start()

        def last_across(self):
            return remote(self.part(zi * 2 + 1 - yi), self.got_y(0), self.ky, y_peer)

        def finish_y(self):
            if self.z_first:
                arrive(self.got_y(0), self.ky)
                mine = self.part(zi * 2 + yi)[...].astype(f32)
                self.total[...] = mine + self.got_y(0)[...].astype(f32)

        def sent(self):
            if self.z_first:
                self.last_across().wait_send()
            for z in range(A):
                if not self.z_first:
                    self.across(z).wait_send()
                pl.when(zi < z)(lambda: self.along(z, True).wait_send())
                pl.when(zi > z)(lambda: self.along(z, False).wait_send())

    if A == 4:
        z_order = []
        for row in zip((3, 2, 1, 0), (3, 2, 0, 1), (0, 1, 3, 2), (0, 1, 2, 3)):
            z_order.append(sum(jnp.where(zi == at, z, 0) for at, z in enumerate(row)))
    else:
        z_order = range(A)

    chunks = y.chunks
    last = len(chunks) - 1
    cuts = [(base, wide + units) for base, wide, _, units in chunks]
    g_wq = Gather(s.WQ.at[n], RW)
    g_pt = Gather(s.PT.at[n], RW)
    g_kv = Gather(s.KVF, T)
    g_fw = [Gather(s.FW, RW, lanes, i in y_first_chunks) for i, lanes in enumerate(cuts)]
    f_wq, f_pt = Spread(g_wq, s.WQ), Spread(g_pt, s.PT)
    h_mix, h_bg, h_og, h_tg = Share(s.MIX, 4), Share(s.BG, 1), Share(o_out, 1), Share(o_tok, 2)
    n_mb = NarrowSum(s.MB, s.MBC, s.MBX, s.MBS)
    n_op = NarrowSum(s.OP, s.OPC, s.OPX, s.OPS)
    w_kv = WideSum(s.KVF, s.DKVY, s.DKVR, s.DKVO, T)
    w_fw = []
    for i, lanes in enumerate(cuts):
        out = o_fw.at[:, pl.ds(*lanes)]
        got = (s.RF0, s.RF1, s.RF2)[i]
        w_fw.append(WideSum(s.FW, s.YFW, got, out, RW, lanes, i in z_first_chunks))
    w_pt = WideSum(s.PPT, s.YPT, s.RPT, o_pt, RW)
    w_q = WideSum(s.PQ, s.YQ, s.RQ, o_q, RW)
    k_a2a, k_gain = take(3), take(3)
    assert taken[0] <= rsem.shape[0] and taken[1] <= ssem.shape[0]

    ops = {}

    def op(name):
        def keep(act):
            ops[name] = act
            return act

        return keep

    def gather_ops(name, gather, split):
        ops[f"{name}.L"], ops[f"{name}.Ly"] = gather.launch, gather.launch_y
        for i in range(1, 4):
            count = A if i == 3 else 1
            ops[f"{name}.h{i}"] = lambda count=count: gather.pump(count, not split)
            if split and not gather.y_first:
                ops[f"{name}.y{i}"] = lambda count=count: gather.pump_y(count)

    def spread_ops(name, spread):
        for i in range(4):
            count = A if i == 3 else 1
            ops[f"{name}.s{i}"] = lambda count=count: spread.pump(count)
            ops[f"{name}.f{i}"] = lambda count=count: spread.pump_forward(count)

    def sum_ops(name, exchange, finish, direct=False):
        for i in range(3):
            count = A if i == 2 else 1
            if direct:
                ops[f"{name}.d{i}"] = lambda count=count: exchange.send_direct(count)
            else:
                extra = 1 if exchange.z_first and i == 1 else 0
                ops[f"{name}.s{i}"] = lambda count=count + extra: exchange.pump(count)
        if exchange.z_first:
            ops[f"{name}.ends"] = exchange.start_ends
            ops[f"{name}.finy"] = finish
            ops[f"{name}.fin"] = exchange.finish
        else:
            ops[f"{name}.fin"] = finish

    gather_ops("wq", g_wq, False)
    gather_ops("pt", g_pt, False)
    gather_ops("kv", g_kv, False)
    spread_ops("fwq", f_wq)
    spread_ops("fpt", f_pt)

    def chunk_finish(i):
        exchange, lanes = w_fw[i], pl.ds(*cuts[i])
        (exchange.finish_y if exchange.z_first else exchange.finish)()
        write(exchange.total, r_fw.at[:, lanes])

    for i, name in enumerate("abc"):
        gather_ops(name, g_fw[i], True)
        sum_ops("w" + name, w_fw[i], lambda i=i: chunk_finish(i))

    def direct_finish(exchange, target=None):
        exchange.finish_direct()
        if target is not None:
            write(exchange.total, target)

    sum_ops("wkv", w_kv, lambda: direct_finish(w_kv), True)
    sum_ops("wpt", w_pt, lambda: direct_finish(w_pt, r_pt), True)
    sum_ops("wq2", w_q, lambda: direct_finish(w_q, r_q), True)

    own = pl.ds(pl.multiple_of(w * RW, RW), RW)
    own_rows = pl.ds(pl.multiple_of(n * T, T), T)
    blank = lambda count, kind=bf16: jnp.zeros((count, RW), kind)
    held = SimpleNamespace()

    @op("prep_wq")
    def _():
        shared_part = jnp.concatenate([qshared[...].astype(f32), blank(LANES - y.SQ, f32)], axis=0)
        gain_row = row_iota(8, RW)
        gain_part = jnp.where(
            gain_row == 0,
            prenorm[...].astype(f32),
            jnp.where(gain_row == 1, midnorm[...].astype(f32), 0.0),
        )
        second_part = jnp.concatenate(
            [part[...].astype(f32) for part in (kshared, vshared, qheads, kheads, vheads)]
            + [gain_part, blank(LANES - y.og - 8, f32)],
            axis=0,
        )
        s.WQ[n, own, :LANES] = shared_part.T.astype(bf16)
        s.WQ[n, own, LANES:] = second_part.T.astype(bf16)

    @op("prep_pt")
    def _():
        for first in range(0, 256, LANES):
            s.PT[n, own, first : first + LANES] = project[first : first + LANES, :].T

    @op("prep_fw")
    def _():
        for base, wide, unit, _ in chunks[:last]:
            for part, weight in enumerate((gating, upward, downward)):
                for first in range(0, 256, LANES):
                    to = base + part * 256 + first
                    s.FW[own, to : to + LANES] = weight[unit + first : unit + first + LANES, :].T
        base, wide, unit, _ = chunks[last]
        s.FW[own, base : base + LANES] = gating[unit:FM, :].T
        s.FW[own, base + LANES : base + 2 * LANES] = upward[unit:FM, :].T
        s.FW[own, base + 2 * LANES : base + wide] = jnp.concatenate(
            [gating[FM:, :], upward[FM:, :]], axis=0
        ).T
        s.FW[own, base + wide : base + wide + LANES] = downward[unit:FM, :].T
        s.FW[own, base + wide + LANES :] = jnp.concatenate(
            [downward[FM:, :], blank(FP - F)], axis=0
        ).T

    def own_row(values):
        mine = row_iota(N, values.shape[1]) == n
        return jnp.sum(jnp.where(mine, values.astype(f32), 0.0), axis=0, keepdims=True)

    def mask_block(block):
        first = block * KB
        key_docs = own_row(docs[:, pl.ds(pl.multiple_of(first, KB), KB)])
        allowed = (lane_iota(T, KB) + first <= row_iota(T, KB) + w * T) & (
            key_docs == s.DOC[:, :1]
        )
        s.BIAS[...] = jnp.where(allowed, 0.0, masked_score)

    @op("consts")
    def _():
        column, head = row_iota(LANES, D), lane_iota(LANES, D) >> 6
        for r in range(QR):
            s.EQ[r] = jnp.where(column == head * QR + r, 1.0, 0.0).astype(bf16)
        place = (w * T + row_iota(T)).astype(f32)
        lane = lane_iota(T)
        angle = place * jnp.exp((lane % (DH // 2)).astype(f32) * (-math.log(10000.0) / (DH // 2)))
        s.ROPE[0] = jnp.cos(angle)
        s.ROPE[1] = jnp.where(lane % DH < DH // 2, -jnp.sin(angle), jnp.sin(angle))

        own_docs = own_row(docs[:, pl.ds(pl.multiple_of(w * T, T), T)])
        own_docs = jnp.transpose(jnp.broadcast_to(own_docs, (T, T)))
        s.DOC[...] = own_docs

        mask_block(0)

    def rotated(tile, back=False):
        turned = swap_quarters(tile) * s.ROPE[1]
        return tile * s.ROPE[0] - turned if back else tile * s.ROPE[0] + turned

    def collect(start, width):
        pieces = []
        for p in range(N):
            pieces += [(held.second_tiles[p], start, p * width, width)]
        return place_lanes(pieces)

    @op("project")
    def _():
        f_wq.landed()
        gains = s.WQ[0, :, LANES:].astype(f32).T
        s.GAIN[0:1, :] = gains[y.og : y.og + 1]
        s.GAIN[1:2, :] = gains[y.og + 1 : y.og + 2]

        x_own = tok[own_rows, :].astype(f32)
        r1_own = row_scale(x_own)
        normed_own = (x_own * r1_own * s.GAIN[0:1, :]).astype(bf16)
        factors = [dot_nn(normed_own, s.WQ[p]) for p in range(N)]
        held.first_tiles = [part[:, :LANES] for part in factors]
        held.second_tiles = [part[:, LANES:] for part in factors]

        kv_own = pl.ds(pl.multiple_of(w * T, T), T)
        s.KVF[kv_own, 0:128] = rotated(collect(y.oK, y.SK)).astype(bf16)
        s.KVF[kv_own, 128:256] = collect(y.oV, y.SK).astype(bf16)
        s.KVF[kv_own, 256:384] = place_lanes(
            [(held.second_tiles[p], y.ok, p * y.HK, y.HK) for p in range(N)]
            + [(held.second_tiles[p], y.ov, (N + p) * y.HK, y.HK) for p in range(N)]
        ).astype(bf16)

    def spread_heads(r):
        return dot_nn(s.QH[:, :LANES], s.EQ[r]) + dot_nn(s.QH[:, LANES:], s.EQ[r])

    @op("queries")
    def _():
        query_heads = collect(y.oq, y.HQ)
        heads_high = query_heads.astype(bf16)
        s.QH[:, :LANES] = heads_high
        s.QH[:, LANES:] = (query_heads - heads_high.astype(f32)).astype(bf16)

        queries = jnp.zeros((T, D), f32)
        for r in range(QR):
            pieces = canonical_pieces(held.first_tiles, y.SQ, r * DH, DH, 0, 0)
            pieces += canonical_pieces(held.first_tiles, y.SQ, r * DH, DH, 0, DH)
            turned = rotated(place_lanes(pieces))
            s.QROT[r] = turned
            queries = queries + spread_heads(r) * jnp.concatenate([turned] * pairs, axis=1)
        for i in range(pairs):
            tile = (queries[:, i * LANES : (i + 1) * LANES] * (1.0 / QR)).astype(bf16)
            s.QP[i] = tile * jnp.asarray(DH**-0.5, bf16)

        def norm_rows(block, _):
            at = pl.ds(pl.multiple_of(block * T, T), T)
            values = tok[at, :].astype(f32)
            s.NORM[at, :] = (values * row_scale(values) * s.GAIN[0:1, :]).astype(bf16)
            return 0

        lax.fori_loop(0, N, norm_rows, 0)

    def expand_block(block):
        at = pl.ds(pl.multiple_of(block * KB, KB), KB)
        s.SHARED[0] = s.KVF[at, 0:128].astype(f32).T
        s.SHARED[1] = s.KVF[at, 128:256].astype(f32).T
        heads = s.KVF[at, 256:384].astype(f32).T
        for i in range(pairs):
            for kind in range(2):
                first = kind * y.heads * KR + 4 * i
                s.HT[i, 4 * kind : 4 * kind + 4, :] = heads[first : first + 4]

        def expand(i, _):
            for kind, ref in enumerate((s.KP, s.VP)):
                one, two = s.SHARED[kind, :DH, :], s.SHARED[kind, DH:, :]
                for half in range(2):
                    row = 4 * kind + 2 * half
                    joined = s.HT[i, row : row + 1, :] * one + s.HT[i, row + 1 : row + 2, :] * two
                    ref[i, half * DH : (half + 1) * DH, :] = (joined * 0.5).astype(bf16)
            return 0

        lax.fori_loop(0, pairs, expand, 0)

    def pair_bias():
        bias = s.BIAS[...]
        return jnp.concatenate([bias, bias], axis=0)

    def forward_pair(i):
        scores = dot_nn(stack_pair(s.QP[i]), s.KP[i]) + pair_bias()
        top = jnp.max(scores, axis=1, keepdims=True)
        if y.NB > 1:
            old_top = s.LSE[i][:, :1]
            top = jnp.maximum(top, old_top)
        weights = jnp.exp(scores - top)
        total = jnp.sum(weights, axis=1, keepdims=True)
        rows_out = dot_nt(weights.astype(bf16), s.VP[i])
        if y.NB > 1:
            factor = jnp.exp(old_top - top)
            total = total + s.RUN[i][:, :1] * factor
            s.LSE[i] = jnp.broadcast_to(top, (2 * T, LANES))
            s.RUN[i] = jnp.broadcast_to(total, (2 * T, LANES))
            keep = stack_pair(s.ATT[i]) * factor
            s.ATT[i] = unstack_pair(rows_out + keep)
        return top, total, rows_out

    def store_mixture(i, attended, top, total):
        s.ATT[i] = attended
        s.LSE[i] = jnp.broadcast_to(top + jnp.log(total), (2 * T, LANES))
        s.MIX[own_rows, pl.ds(pl.multiple_of(i * LANES, LANES), LANES)] = attended.astype(bf16)

    def forward_step(i, _):
        top, total, rows_out = forward_pair(i)
        store_mixture(i, unstack_pair(rows_out / total), top, total)
        return 0

    @op("at_x")
    def _():
        g_kv.landed_all()
        if y.NB == 1:
            expand_block(0)
            return
        s.LSE[...] = jnp.full(s.LSE.shape, masked_score, f32)
        s.RUN[...] = jnp.zeros(s.RUN.shape, f32)
        s.ATT[...] = jnp.zeros(s.ATT.shape, f32)

        def forward_block(block, _):
            mask_block(block)
            expand_block(block)

            def step(i, _):
                forward_pair(i)
                return 0

            lax.fori_loop(0, pairs, step, 0)
            return 0

        lax.fori_loop(0, y.NB, forward_block, 0)

        def finish_step(i, _):
            total = s.RUN[i][:, :1]
            store_mixture(i, unstack_pair(stack_pair(s.ATT[i]) / total), s.LSE[i][:, :1], total)
            return 0

        lax.fori_loop(0, pairs, finish_step, 0)

    def forward_chunk(chunk):
        per = pairs // h_mix.chunks
        if y.NB == 1:
            lax.fori_loop(chunk * per, (chunk + 1) * per, forward_step, 0)
        h_mix.start(chunk)

    for i in range(h_mix.chunks):
        ops[f"at{i}"] = lambda i=i: forward_chunk(i)
        ops[f"mix.f{i}"] = lambda i=i: h_mix.forward(i)

    @op("middle")
    def _():
        h_mix.landed_all()
        f_pt.landed()
        def middle_rows(block, _):
            at = pl.ds(pl.multiple_of(block * 2 * T, 2 * T), 2 * T)
            values = tok[at, :].astype(f32)
            for p in range(N):
                values = values + dot_nt(s.MIX[at, p * 256 : (p + 1) * 256], s.PT[p])
            scale = row_scale(values)
            s.MID[at, :] = values
            s.R2[at, :] = jnp.broadcast_to(scale, (2 * T, LANES))
            s.NM[at, :] = (values * scale * s.GAIN[1:2, :]).astype(bf16)
            return 0

        lax.fori_loop(0, 2, middle_rows, 0)

    def gates(gate, up, pushed):
        chance = 1.0 / (1.0 + jnp.exp(-gate))
        silu = gate * chance
        back = pushed * up * chance * (1.0 + gate * (1.0 - chance))
        return silu * up, back, pushed * silu

    tail_low = lane_iota(2 * T) < DH

    def dense_rows(chunk, far):
        base, wide, unit, units = chunks[chunk]
        first = sum(part[1] for part in chunks[:chunk])
        block = (1 - xo) if far else xo
        at = pl.ds(pl.multiple_of(block * 2 * T, 2 * T), 2 * T)
        both = dot_nn(s.NM[at, :], s.FW[:, base : base + wide])
        back = dot_nn(cot[at, :], s.FW[:, base + wide : base + wide + units])
        width = 256 if chunk < last else LANES
        hidden, gate_back, up_back = gates(
            both[:, :width], both[:, width : 2 * width], back[:, :width]
        )
        s.HID[at, unit : unit + width] = hidden.astype(bf16)
        s.GG[at, first : first + width] = gate_back.astype(bf16)
        s.GG[at, first + width : first + 2 * width] = up_back.astype(bf16)
        if chunk == last:
            tail = both[:, 2 * width :]
            hidden, gate_back, up_back = gates(tail, pltpu.roll(tail, DH, 1), back[:, width:])
            s.HID[at, unit + width :] = jnp.where(tail_low, hidden, 0.0).astype(bf16)
            up_back = pltpu.roll(up_back, DH, 1)
            s.GG[at, first + 2 * width :] = jnp.where(tail_low, gate_back, up_back).astype(bf16)
        mid = dot_nt(s.GG[at, first : first + wide], s.FW[:, base : base + wide])
        out = dot_nt(s.HID[at, unit : unit + units], s.FW[:, base + wide : base + wide + units])
        if chunk:
            mid = mid + s.MB[at, :].astype(f32)
            out = out + s.OP[at, :].astype(f32)
        s.MB[at, :] = mid.astype(bf16)
        s.OP[at, :] = out.astype(bf16)

    def grad_blocks(parts, exchange):
        per = A // 4
        for j in range(4):
            block = z_order[j] if A == 4 else j
            at = pl.ds(pl.multiple_of(block * 256, 256), 256)
            for target, to, left, right, lanes in parts:
                value = dot_tn(left[:, at], right[:, lanes]).astype(bf16)
                target[at, to : to + value.shape[1]] = value
            if not exchange.z_first:
                for q in range(per):
                    exchange.start(block * per + q)

    def dense_grads(chunk):
        base, wide, unit, units = chunks[chunk]
        first = sum(part[1] for part in chunks[:chunk])
        g_fw[chunk].sent()
        grad_blocks(
            [
                (s.FW, base, s.NM, s.GG, slice(first, first + wide)),
                (s.FW, base + wide, cot, s.HID, slice(unit, unit + units)),
            ],
            w_fw[chunk],
        )


    def dense_chunk(chunk):
        g_fw[chunk].landed_all()
        dense_rows(chunk, True)
        dense_rows(chunk, False)

    for i, name in enumerate("abc"):
        ops["ff_" + name] = lambda i=i: dense_chunk(i)
        ops["g_" + name] = lambda i=i: dense_grads(i)

    def last_dense(far):
        if far:
            g_fw[last].landed_all()
        dense_rows(last, far)
        n_mb.start(far)

    ops["ffCf"] = lambda: last_dense(True)
    ops["ffCn"] = lambda: last_dense(False)
    ops["mb.pass"] = n_mb.pass_on

    @op("op.start")
    def _():
        n_op.start(True)
        n_op.start(False)

    ops["op.pass"] = n_op.pass_on

    @op("mid")
    def _():
        mid_back = n_mb.result()
        mid_own = s.MID[own_rows, :]
        r2_own = s.R2[own_rows, :][:, :1]
        scaled = mid_back * s.GAIN[1:2, :]
        s.GS[1:2, :] = jnp.sum(mid_back * mid_own * r2_own, axis=0, keepdims=True)
        middle_gradient = (
            cot[own_rows, :].astype(f32)
            + r2_own * scaled
            - mid_own * (r2_own * r2_own * r2_own) * jnp.mean(scaled * mid_own, axis=-1, keepdims=True)
        )
        s.MG[...] = middle_gradient
        branch = middle_gradient.astype(bf16)
        s.BG[own_rows, :] = branch
        h_bg.start(0)
        for p in range(N):
            part = dot_nn(branch, s.PT[p]).astype(bf16)
            s.DO[2 * p] = part[:, :LANES]
            s.DO[2 * p + 1] = part[:, LANES:]

    def backward_part(block, part):
        if part == 0:
            s.DST[...] = jnp.zeros(s.DST.shape, f32)

        def step(i, _):
            query, pushed = s.QP[i], s.DO[i]
            query2, pushed2 = stack_pair(query), stack_pair(pushed)
            product = pushed.astype(f32) * s.ATT[i]
            delta = jnp.sum(stack_pair(product), axis=1, keepdims=True)
            scores = dot_nn(query2, s.KP[i]) + pair_bias()
            chance = jnp.exp(scores - jnp.concatenate([s.LSE[i]] * (KB // LANES), axis=1))
            gradient = (chance * (dot_nn(pushed2, s.VP[i]) - delta)).astype(bf16)
            s.QB[i] = s.QB[i] + unstack_pair(dot_nt(gradient, s.KP[i])) * DH**-0.5
            key_back = dot_tn(query2, gradient)
            value_back = dot_tn(pushed2, chance.astype(bf16))
            for kind, back in enumerate((key_back, value_back)):
                for r in range(KR):
                    shared = slice(r * DH, (r + 1) * DH)
                    found = s.DST[kind, shared, :]
                    for half in range(2):
                        mine = back[half * DH : (half + 1) * DH]
                        row = 4 * kind + 2 * half + r
                        found = found + s.HT[i, row : row + 1, :] * mine
                        s.DHT[i, row : row + 1, :] = jnp.sum(
                            mine * s.SHARED[kind, shared, :], axis=0, keepdims=True
                        )
                    s.DST[kind, shared, :] = found
            return 0

        quarter = pairs // 4
        lax.fori_loop(part * quarter, (part + 1) * quarter, step, 0)
        if part < 3:
            return
        at = pl.ds(pl.multiple_of(block * KB, KB), KB)
        for kind in range(2):
            s.KVF[at, kind * 128 : kind * 128 + 128] = (s.DST[kind] * 0.5).T.astype(bf16)
        heads = [s.DHT[i, 4 * kind : 4 * kind + 4, :] for kind in range(2) for i in range(pairs)]
        heads.append(jnp.zeros((LANES - 8 * pairs, KB), f32))
        s.KVF[at, 256:384] = (jnp.concatenate(heads, axis=0) * 0.5).T.astype(bf16)

    def backward_quarter(part):
        if part == 0:
            s.QB[...] = jnp.zeros(s.QB.shape, f32)
            g_kv.sent()
        if y.NB == 1:
            backward_part(0, part)
        elif part == 0:

            def backward_step(block, _):
                mask_block(block)
                expand_block(block)
                for each in range(4):
                    backward_part(block, each)
                return 0

            lax.fori_loop(0, y.NB, backward_step, 0)

    for i in range(4):
        ops[f"bq{i}"] = lambda i=i: backward_quarter(i)

    @op("kvst")
    def _():
        for z in z_order:
            w_kv.start(z)

    ops["bg.f"] = h_bg.forward_all

    @op("pt.g")
    def _():
        h_bg.landed_all()
        mine = pl.ds(pl.multiple_of(n * 256, 256), 256)
        grad_blocks([(s.PPT, 0, s.BG, s.MIX, mine)], w_pt)

    @op("qb")
    def _():
        query_back = jnp.concatenate([s.QB[i] for i in range(pairs)], axis=1)
        heads_back = jnp.zeros((T, LANES), f32)
        shared_back = []
        for r in range(QR):
            turned = s.QROT[r]
            product = (query_back * jnp.concatenate([turned] * pairs, axis=1)).astype(bf16)
            heads_back = heads_back + dot_nt(product, s.EQ[r])
            product = spread_heads(r) * query_back
            total = product[:, :LANES]
            for i in range(1, pairs):
                total = total + product[:, i * LANES : (i + 1) * LANES]
            shared_back.append(fold_halves(total))
        low = lane_iota(T) < DH
        held.shared_tiles = [
            rotated(jnp.where(low, shared_back[2 * t], shared_back[2 * t + 1]), back=True) * (1.0 / QR)
            for t in range(QR // 2)
        ]
        held.heads_back = heads_back * (1.0 / QR)

    @op("op.res")
    def _():
        o_out[own_rows, :] = (s.MID[own_rows, :] + n_op.result()).astype(bf16)
        h_og.start(0)

    ops["og.f"] = h_og.forward_all

    @op("og.l")
    def _():
        h_og.landed_all()
        write(o_out, r_out)

    ops["tg.f"] = h_tg.forward_all

    @op("tg.l")
    def _():
        h_tg.landed_all()
        write(o_tok, r_tok)

    @op("qg")
    def _():
        key_shared = rotated(s.DKVO[:, 0:128], back=True)
        value_shared = s.DKVO[:, 128:256]
        head_tile = s.DKVO[:, 256:384]
        for p in range(N):
            s.QGS[p, :, :LANES] = place_lanes(
                canonical_pieces(held.shared_tiles, LANES, p * y.SQ, y.SQ, 0, 0)
            ).astype(bf16)
            s.QGS[p, :, LANES:] = place_lanes(
                [
                    (key_shared, p * y.SK, y.oK, y.SK),
                    (value_shared, p * y.SK, y.oV, y.SK),
                    (held.heads_back, p * y.HQ, y.oq, y.HQ),
                    (head_tile, p * y.HK, y.ok, y.HK),
                    (head_tile, (N + p) * y.HK, y.ov, y.HK),
                ]
            ).astype(bf16)
        for k, peer in enumerate(narrow_peers):
            send(s.QGS.at[peer[1]], s.QGR.at[n], k_a2a + k, peer)
        s.QGR[n] = s.QGS[n]

    @op("fb")
    def _():
        first_back = jnp.zeros((T, D), f32)
        for p in range(N):
            first_back = first_back + dot_nt(s.QGS[p], s.WQ[p])
        x_own = tok[own_rows, :].astype(f32)
        r1_own = row_scale(x_own)
        s.GS[0:1, :] = jnp.sum(first_back * x_own * r1_own, axis=0, keepdims=True)
        for k, peer in enumerate(narrow_peers):
            send(s.GS, s.GR.at[k], k_gain + k, peer)
        scaled = first_back * s.GAIN[0:1, :]
        tokens_gradient = (
            s.MG[...]
            + r1_own * scaled
            - x_own * (r1_own * r1_own * r1_own) * jnp.mean(scaled * x_own, axis=-1, keepdims=True)
        )
        o_tok[own_rows, :] = tokens_gradient.astype(bf16)
        for chunk in range(h_tg.chunks):
            h_tg.start(chunk)

    @op("q.g")
    def _():
        for k, peer in enumerate(narrow_peers):
            arrive(s.QGR.at[peer[1]], k_a2a + k)
        for k in range(3):
            arrive(s.GR.at[k], k_gain + k)
        gain_rows = s.GS[...]
        for k in range(3):
            gain_rows = gain_rows + s.GR[k]
        lane_row = row_iota(LANES, D)
        spread = jnp.where(
            lane_row == y.og,
            gain_rows[0:1],
            jnp.where(lane_row == y.og + 1, gain_rows[1:2], 0.0),
        )
        gain_columns = spread.T
        for j in range(4):
            block = z_order[j] if A == 4 else j
            lanes = pl.ds(pl.multiple_of(block * 256, 256), 256)
            value = jnp.zeros((256, 256), f32)
            for p in range(N):
                value = value + dot_tn(s.NORM[p * T : (p + 1) * T, lanes], s.QGR[p])
            s.PQ[pl.ds(pl.multiple_of(block * 256, 256), 256), :] = value.astype(bf16)
        s.PQ[:, LANES:] = (s.PQ[:, LANES:].astype(f32) + gain_columns).astype(bf16)
        for z in z_order:
            w_q.start(z)

    for name in schedule:
        ops[name]()

    for exchange in (g_wq, g_pt, f_wq, f_pt, *w_fw):
        exchange.sent()
    for exchange in (w_kv, w_pt, w_q):
        exchange.sent_direct()
    for copy in pending:
        copy.wait_send()
    for copy in written:
        copy.wait()


def results_kernel(y, out, tok, fw, pt, q, *outs):
    o_out, o_tok, o_pre, o_qh, o_qs, o_kh, o_ks, o_vh, o_vs, o_pt, o_mid, o_gate, o_up, o_down = outs
    FM, F, half = y.FM, y.F, y.F - y.FM
    o_out[...] = out[...]
    o_tok[...] = tok[...].astype(f32)
    o_qs[...] = q[:, :LANES].T[: y.SQ]
    second = q[:, LANES:].T
    o_ks[...] = second[y.oK : y.oK + y.SK]
    o_vs[...] = second[y.oV : y.oV + y.SK]
    o_qh[...] = second[y.oq : y.oq + y.HQ]
    o_kh[...] = second[y.ok : y.ok + y.HK]
    o_vh[...] = second[y.ov : y.ov + y.HK]
    o_pre[...] = second[y.og : y.og + 1]
    o_mid[...] = second[y.og + 1 : y.og + 2]
    for first in range(0, 256, LANES):
        o_pt[first : first + LANES, :] = pt[:, first : first + LANES].T
    *whole_chunks, (base, wide, unit, _) = y.chunks
    for at, _, start, _ in whole_chunks:
        for part, target in enumerate((o_gate, o_up, o_down)):
            for first in range(0, 256, LANES):
                place = at + part * 256 + first
                target[start + first : start + first + LANES, :] = fw[:, place : place + LANES].T
    o_gate[unit:FM, :] = fw[:, base : base + LANES].T
    o_up[unit:FM, :] = fw[:, base + LANES : base + 2 * LANES].T
    tail = fw[:, base + 2 * LANES : base + wide].T
    o_gate[FM:, :] = tail[:half]
    o_up[FM:, :] = tail[half:]
    o_down[unit:FM, :] = fw[:, base + wide : base + wide + LANES].T
    o_down[FM:, :] = fw[:, base + wide + LANES :].T[:half]


def solution(mesh):
    W, N = mesh.shape["wide"], mesh.shape["narrow"]

    def on_device(
        tokens,
        documents,
        prenorm,
        qheads,
        qshared,
        kheads,
        kshared,
        vheads,
        vshared,
        project,
        midnorm,
        gating,
        upward,
        downward,
        cotangent,
    ):
        R, T, D = tokens.shape
        L = documents.shape[1]
        RW, F = gating.shape
        y = make_layout(W, N, T, D, F, L, N * kheads.shape[1] // KR)
        assert R == N
        scratch = scratch_list(y)
        line, direct = y.A + 2, 2 * y.A + 1
        arrivals = 18 * y.A + 36 + 3 * direct
        arrivals += sum(line if i in z_first_chunks else direct for i in range(3))
        sends = arrivals + 12 * y.A
        vmem = pl.BlockSpec(memory_space=pltpu.VMEM)

        def kernel(*refs):
            block_kernel(y, tuple(scratch), *refs)

        shape = jax.ShapeDtypeStruct
        raw = pl.pallas_call(
            kernel,
            out_shape=(
                shape((y.M, D), bf16),
                shape((y.M, D), bf16),
                shape((RW, y.FW), f32),
                shape((RW, 256), f32),
                shape((RW, 256), f32),
            ),
            in_specs=[vmem] * 15,
            out_specs=[pl.BlockSpec(memory_space=pl.ANY)] * 5,
            scratch_shapes=[*scratch.values()]
            + [pltpu.SemaphoreType.DMA((count,)) for count in (sends, arrivals, 7)],
            compiler_params=pltpu.CompilerParams(
                collective_id=0, has_side_effects=True, vmem_limit_bytes=63 * 2**20
            ),
            name="block",
        )(
            tokens.reshape(y.M, D),
            documents,
            prenorm.reshape(1, RW),
            qheads.T,
            qshared.T,
            kheads.T,
            kshared.T,
            vheads.T,
            vshared.T,
            project,
            midnorm.reshape(1, RW),
            gating.T,
            upward.T,
            downward,
            cotangent.reshape(y.M, D),
        )

        def results(*refs):
            results_kernel(y, *refs)

        outputs = pl.pallas_call(
            results,
            out_shape=(
                shape((y.M, D), bf16),
                shape((y.M, D), f32),
                shape((1, RW), f32),
                shape((y.HQ, RW), f32),
                shape((y.SQ, RW), f32),
                shape((y.HK, RW), f32),
                shape((y.SK, RW), f32),
                shape((y.HK, RW), f32),
                shape((y.SK, RW), f32),
                shape((256, RW), f32),
                shape((1, RW), f32),
                shape((F, RW), f32),
                shape((F, RW), f32),
                shape((F, RW), f32),
            ),
            in_specs=[vmem] * 5,
            out_specs=[vmem] * 14,
            compiler_params=pltpu.CompilerParams(vmem_limit_bytes=63 * 2**20),
            name="results",
        )(*raw)
        turned = (3, 4, 5, 6, 7, 8, 11, 12)
        outputs = [v.T if i in turned else v for i, v in enumerate(outputs)]
        outputs[0] = outputs[0].reshape(R, T, D)
        outputs[1] = outputs[1].reshape(R, T, D)
        outputs[2] = outputs[2].reshape(RW)
        outputs[10] = outputs[10].reshape(RW)
        return tuple(outputs)

    split = P("wide", "narrow")
    flipped = P("narrow", "wide")
    whole = P(None, "wide", None)
    gain = P("wide")
    return jax.shard_map(
        on_device,
        mesh=mesh,
        in_specs=(
            whole,
            P(),
            gain,
            split,
            split,
            split,
            split,
            split,
            split,
            flipped,
            gain,
            split,
            split,
            flipped,
            whole,
        ),
        out_specs=(
            whole,
            whole,
            gain,
            split,
            split,
            split,
            split,
            split,
            split,
            flipped,
            gain,
            split,
            split,
            flipped,
        ),
        check_vma=False,
    )
```

time: 173 us -> 153 us (0.88)
  Pallas kernels: 172 us -> 152 us
    pallas_call x1, Pallas kernels: 168 us -> 147 us  [on_device(): pl.pallas_call(kernel, out_shape=(shape((y.M, D), bf16), shape((y.M, D),...]
where the time goes in v3:
time: 153 us
  Pallas kernels  152 us (99%)
    pallas_call x1, Pallas kernels, on_device(): pl.pallas_call(kernel, out_shape=(shape((y.M, D), bf16), shape((y.M, D),...  147 us
    pallas_call x1, Pallas kernels, on_device(): pl.pallas_call(results, out_shape=(shape((y.M, D), bf16), shape((y.M, D),...  4.46 us

profile of v3, /device:TPU:0, one launch (start us, length us, event | category | flops | bytes accessed | tf_op | source)
XLA Modules:
  0.0 152.6 jit_solution(10584380467350509546)
XLA Ops:
  0.7 147.3 %block.1 = (bf16[512,1024]{1,0:T(8,128)(2,1)}, bf16[512,1024]{1,0:T(8,128)(2,1)}, f32[128,2176]{1,0:T(8,128)}, f32[128,256]{1,0:T(8,128)}, f32[128,256]{1,0:T(8,128)}) custom-call(bf16[512,1024]{1,0:T(8,128)(2,1)} %bitcast.24, s32[4,1024]{1,0:T(4,128)} %refs_1_.1, bf16[1,128]{1,0:T(2,128)(2,1)} %bitcast.34, bf16[24,128]{1,0:T(8,128)(2,1)} %bitcast.31, ...), custom_call_target="tpu_custom_call" | custom-call | tf_op jit(solution)/shard_map/block/pallas_call | solution.py:1322
  147.9 4.5 %results.1 = (bf16[512,1024]{1,0:T(8,128)(2,1)}, f32[512,1024]{1,0:T(8,128)}, f32[1,128]{1,0:T(1,128)}, f32[24,128]{1,0:T(8,128)}, f32[96,128]{1,0:T(8,128)}, /*...) custom-call(bf16[512,1024]{1,0:T(8,128)(2,1)} %get-tuple-element.33., ...), custom_call_target="tpu_custom_call" | custom-call | tf_op jit(solution)/shard_map/results/pallas_call | solution.py:1360

commit v4 on v3

--- a/solution.py
+++ b/solution.py
@@ -17,8 +17,12 @@
 epsilon = 1e-06
 masked_score = -1e30
 MESH = pl.DeviceIdType.MESH
-y_first_chunks = (2,)
-z_first_chunks = (2,)
+y_first_chunks = (1,)
+z_first_chunks = (0,)
+chunk_order = (0, 2, 1)
+y_first_gathers = ()
+z_first_sums = ()
+direct_sums = ("wkv", "wqa", "wqb")
 f32 = jnp.float32
 bf16 = jnp.bfloat16
 
@@ -64,12 +68,6 @@
     return pieces
 
 
-def both_halves(tile):
-    low = lane_iota(tile.shape[0]) < DH
-    turned = pltpu.roll(tile, DH, 1)
-    return jnp.where(low, tile, turned), jnp.where(low, turned, tile)
-
-
 def swap_quarters(tile):
     low = lane_iota(tile.shape[0]) % DH < DH // 2
     return jnp.where(low, pltpu.roll(tile, LANES - DH // 2, 1), pltpu.roll(tile, DH // 2, 1))
@@ -85,6 +83,22 @@
     half = rows.shape[0] // 2
     low = lane_iota(half) < DH
     return jnp.where(low, rows[:half], rows[half:])
+
+
+def pack_heads(tile):
+    quarter = tile.shape[0] // 4
+    low = lane_iota(quarter) < DH
+    parts = [tile[i * quarter : (i + 1) * quarter] for i in range(4)]
+    pairs = [
+        jnp.where(low, parts[i], pltpu.roll(parts[i + 1], DH, 1)) for i in (0, 2)
+    ]
+    return jnp.concatenate(pairs, axis=1)
+
+
+def unpack_heads(rows):
+    tiles = (rows[:, :LANES], rows[:, LANES:])
+    parts = [part for tile in tiles for part in (tile, pltpu.roll(tile, DH, 1))]
+    return jnp.concatenate(parts, axis=0)
 
 
 def fold_halves(tile):
@@ -101,6 +115,7 @@
     lay.A = W // 2
     lay.RW = D // W
     lay.M = N * T
+    lay.KT = T + T // 4
     lay.FM = F // LANES * LANES
     lay.FP = lay.FM + LANES
     full = lay.FM // 256
@@ -131,10 +146,16 @@
     vm = lambda *shape, kind=bf16: pltpu.VMEM(shape, kind)
     GUc = 2 * y.FM + LANES
     return dict(
+        PIN=vm(256, RW),
+        GIN=vm(y.F, RW),
+        UIN=vm(y.F, RW),
+        DIN=vm(y.F, RW),
+        XIN=vm(M, D),
+        CIN=vm(M, D),
         WQ=vm(N, D, 256),
         PT=vm(N, D, 256),
         FW=vm(D, y.FW),
-        KVF=vm(L, 384),
+        KVF=vm(L // T * y.KT, 256),
         KP=vm(y.pairs, LANES, y.KB),
         VP=vm(y.pairs, LANES, y.KB),
         EQ=vm(QR, LANES, D),
@@ -171,9 +192,9 @@
         DO=vm(y.pairs, T, LANES),
         QB=vm(y.pairs, T, LANES, kind=f32),
         DST=vm(2, LANES, y.KB, kind=f32),
-        DKVY=vm(A * T, 384),
-        DKVR=vm((A + 1) * T, 384),
-        DKVO=vm(T, 384, kind=f32),
+        DKVY=vm(A * y.KT, 256),
+        DKVR=vm((A + 1) * y.KT * (1 + ("wkv" in z_first_sums)), 256),
+        DKVO=vm(y.KT, 256, kind=f32),
         QGS=vm(N, T, 256),
         QGR=vm(N, T, 256),
         OUT=vm(M, D),
@@ -190,35 +211,37 @@
         },
         PPT=vm(D, 256),
         YPT=vm(A * RW, 256),
-        RPT=vm((A + 1) * RW, 256),
+        RPT=vm((A + 1) * RW * (1 + ("wpt" in z_first_sums)), 256),
         PQ=vm(D, 256),
         YQ=vm(A * RW, 256),
-        RQ=vm((A + 1) * RW, 256),
+        RQ0=vm((A + 1) * RW, LANES),
+        RQ1=vm((A + 1) * RW, LANES),
     )
 
 
 schedule = (
-    "prep_wq", "wq.L", "wq.Ly", "prep_pt", "pt.Ly", "pt.L", "wq.h1", "fwq.s0", "prep_fw", "c.Ly",
-    "b.L", "consts", "wq.h2", "fwq.s1", "pt.h1", "b.h1", "fwq.s2", "a.L", "b.Ly", "wq.h3", "b.h2",
-    "pt.h2", "fwq.s3", "fwq.f0", "fwq.f1", "fwq.f2", "b.y1", "fpt.s0", "c.L", "b.y2", "a.Ly",
-    "fwq.f3", "project", "kv.L", "pt.h3", "kv.h1", "kv.h2", "fpt.s1", "fpt.f0", "kv.Ly", "a.h1",
-    "kv.h3", "a.h2", "b.h3", "a.y1", "a.y2", "fpt.s2", "fpt.s3", "c.h1", "queries", "at_x", "at0",
-    "at1", "a.h3", "a.y3", "fpt.f1", "fpt.f2", "at2", "at3", "mix.f0", "mix.f1", "c.h2", "fpt.f3",
-    "mix.f2", "b.y3", "mix.f3", "middle", "ff_a", "ff_b", "c.h3", "ffCf", "ffCn", "mb.pass",
-    "g_c", "wc.ends", "g_b", "mid", "bq0", "op.start", "wc.s1", "bq1", "bq2", "bq3", "wc.s2",
-    "op.pass", "kvst", "bg.f", "wb.s0", "pt.g", "wkv.d0", "wb.s1", "op.res", "qb", "wpt.d0",
-    "wkv.d1", "wkv.d2", "g_a", "wb.s2", "wa.s0", "wpt.d1", "wkv.fin", "qg", "wc.fin", "wa.s1",
-    "fb", "q.g", "og.f", "wa.s2", "wc.finy", "wpt.d2", "tg.f", "wq2.d0", "wq2.d1", "tg.l",
-    "wq2.d2", "wa.fin", "wpt.fin", "og.l", "wb.fin", "wq2.fin",
+    "prep_wq", "wq.L", "prep_pt", "pt.L", "wq.Ly", "wq.h1", "fwq.s0", "prep_fw", "pt.h1", "wq.h2",
+    "a.L", "fwq.s1", "b.L", "pt.Ly", "wq.h3", "fwq.f0", "c.Ly", "fwq.s2", "fwq.s3", "fwq.f1",
+    "a.h1", "consts", "b.Ly", "a.Ly", "fwq.f2", "fwq.f3", "pt.h2", "project", "kv.L", "b.h1",
+    "fpt.s0", "fpt.s1", "kv.h1", "pt.h3", "kv.Ly", "kv.h2", "kv.h3", "a.h2", "fpt.s2", "b.h2",
+    "c.L", "a.y1", "a.y2", "fpt.f0", "queries", "fpt.s3", "at_x", "a.h3", "at0", "at1", "a.y3",
+    "at2", "mix.f0", "at3", "b.y1", "fpt.f1", "b.y2", "mix.f1", "mix.f2", "b.h3", "fpt.f2",
+    "fpt.f3", "mix.f3", "c.h1", "b.y3", "middle", "ff_a", "g_a", "wa.ends", "c.h2", "ff_b", "g_b",
+    "c.h3", "ffCf", "ffCn", "mb.pass", "wa.s1", "g_c", "wa.s2", "wb.s0", "mid", "bq0", "bq1",
+    "wc.s0", "bq2", "op.start", "bq3", "op.pass", "bg.f", "wb.s1", "wc.s1", "kvst", "qb", "qg1",
+    "fb1", "op.res", "wkv.d0", "q.g1", "wkv.d1", "pt.g", "wkv.d2", "wb.s2", "wqa.d0", "wkv.fin",
+    "qg", "fb", "wpt.s0", "wa.fin", "wqa.d1", "wpt.s1", "wb.fin", "wqa.d2", "wc.s2", "wpt.s2",
+    "q.g", "og.f", "wqb.d0", "wqa.fin", "wc.fin", "wqb.d1", "og.l", "wqb.d2", "wpt.fin", "tg.f",
+    "tg.l", "wa.finy", "wqb.fin",
 )
 
 
 def block_kernel(y, names, *refs):
-    tok, docs, prenorm, qheads, qshared, kheads, kshared, vheads, vshared = refs[:9]
-    project, midnorm, gating, upward, downward, cot = refs[9:15]
+    docs, prenorm, qheads, qshared, kheads, kshared, vheads, vshared, midnorm = refs[:9]
+    sources = refs[9:15]
     r_out, r_tok, r_fw, r_pt, r_q = refs[15:20]
     s = SimpleNamespace(**dict(zip(names, refs[20:])))
-    ssem, rsem, wsem = refs[20 + len(names) :]
+    ssem, rsem, wsem, lsem = refs[20 + len(names) :]
     o_out, o_tok, o_fw, o_pt, o_q = s.OUT, s.TOK, s.TFW, s.TPT, s.TQ
     written = []
 
@@ -226,6 +249,12 @@
         copy = pltpu.make_async_copy(src, dst, wsem.at[len(written)])
         copy.start()
         written.append(copy)
+
+    project, gating, upward, downward, tok, cot = s.PIN, s.GIN, s.UIN, s.DIN, s.XIN, s.CIN
+    loads = []
+    for source, target in zip(sources, (project, gating, upward, downward, tok, cot)):
+        loads.append(pltpu.make_async_copy(source, target, lsem.at[len(loads)]))
+        loads[-1].start()
 
     W, N, T, D, F, L, A, RW, M = y.W, y.N, y.T, y.D, y.F, y.L, y.A, y.RW, y.M
     FM, FP, KB, pairs = y.FM, y.FP, y.KB, y.pairs
@@ -238,35 +267,38 @@
     x_peer = (w, (1 - xo) * 2 + co)
     d_peer = (w, (1 - xo) * 2 + 1 - co)
     narrow_peers = (c_peer, x_peer, d_peer)
-    taken = [0, rsem.shape[0]]
+    taken = [0, 0]
 
     def take(count=1):
         taken[0] += count
         return taken[0] - count
 
-    def take_send(count):
+    def take_send(count=1):
         taken[1] += count
         return taken[1] - count
 
-    def remote(src, dst, k, peer, send_k=None):
+    def remote(src, dst, k, peer, send_k):
         return pltpu.make_async_remote_copy(
             src_ref=src,
             dst_ref=dst,
-            send_sem=ssem.at[k if send_k is None else send_k],
+            send_sem=ssem.at[send_k],
             recv_sem=rsem.at[k],
             device_id=peer,
             device_id_type=MESH,
         )
 
+    def all_sent(ref, send_k):
+        remote(ref, ref, 0, y_peer, send_k).wait_send()
+
     pending = []
 
-    def send(src, dst, k, peer, started=pending):
-        copy = remote(src, dst, k, peer)
+    def send(src, dst, k, peer):
+        copy = remote(src, dst, k, peer, take_send())
         copy.start()
-        started.append(copy)
+        pending.append(copy)
 
     def arrive(dst, k):
-        remote(dst, dst, k, y_peer).wait_recv()
+        remote(dst, dst, k, y_peer, 0).wait_recv()
 
     def rows(ref, first, count, lanes=None):
         at = pl.ds(pl.multiple_of(first, 16), count)
@@ -292,7 +324,9 @@
     class Gather:
         def __init__(self, ref, count, lanes=None, y_first=False):
             self.ref, self.count, self.lanes, self.y_first = ref, count, lanes, y_first
-            self.kz, self.ky, self.kl = take(A), take(A), take_send(A)
+            self.kz, self.ky = take(A), take(A)
+            self.sy, self.sr = take_send(), take_send()
+            self.sl = take_send() if y_first else self.sr
             self.next = self.next_y = 1
 
         def part(self, wide):
@@ -306,12 +340,12 @@
         def along(self, z, to_right):
             block = self.block(z)
             if to_right:
-                return remote(block, block, self.kz + z, right_peer)
-            return remote(block, block, self.kz + z, left_peer, self.kl + z)
+                return remote(block, block, self.kz + z, right_peer, self.sr)
+            return remote(block, block, self.kz + z, left_peer, self.sl)
 
         def across(self, z):
             part = self.part(z * 2 + yi)
-            return remote(part, part, self.ky + z, y_peer)
+            return remote(part, part, self.ky + z, y_peer, self.sy)
 
         def landed(self, z):
             arrive(self.part(z * 2 + 1 - yi), self.ky + z)
@@ -351,39 +385,42 @@
                     self.landed(z)
 
         def sent(self):
-            self.across(zi).wait_send()
-            pl.when(zi < A - 1)(lambda: self.along(zi, True).wait_send())
-            pl.when(zi > 0)(lambda: self.along(zi, False).wait_send())
-            for distance in range(1, A):
-
-                def act(z, to_right):
-                    more = zi < A - 1 if to_right else zi > 0
-                    pl.when(more)(lambda: self.along(z, to_right).wait_send())
-                    if not self.y_first:
-                        self.across(z).wait_send()
-
-                each_at(distance, act)
+            def blocks(count):
+                return rows(self.ref, 0, count * self.count, self.lanes)
+
+            all_sent(blocks(1 if self.y_first else A), self.sy)
+            if self.y_first:
+                for z in range(A - 1):
+                    pl.when(zi == z)(lambda: all_sent(blocks(2 * z + 2), self.sr))
+                    pl.when(zi == z + 1)(lambda: all_sent(blocks(2 * (A - z - 1)), self.sl))
+                return
+            inner = (zi > 0) & (zi < A - 1)
+            pl.when(inner)(lambda: all_sent(blocks(A + 1), self.sr))
+            pl.when(jnp.logical_not(inner))(lambda: all_sent(blocks(1), self.sr))
 
     class Spread:
         def __init__(self, gather, ref):
             self.gather, self.ref = gather, ref
             self.next = self.passed = 0
             self.kx, self.kc, self.kd = take(A), take(A), take(A)
+            self.sx, self.sc, self.sd = take_send(), take_send(), take_send()
 
         def part(self, owner, z):
             return rows(self.ref.at[owner], z * 2 * RW, 2 * RW)
 
         def copies(self, z):
             part = self.part(n, z)
-            return remote(part, part, self.kx + z, x_peer), remote(part, part, self.kc + z, c_peer)
+            to_x = remote(part, part, self.kx + z, x_peer, self.sx)
+            return to_x, remote(part, part, self.kc + z, c_peer, self.sc)
 
         def onward(self, z):
             part = self.part(x_peer[1], z)
-            return remote(part, part, self.kd + z, c_peer)
+            return remote(part, part, self.kd + z, c_peer, self.sd)
 
         def start(self, distance):
             def act(z, _):
-                self.gather.landed(z)
+                if not self.gather.y_first:
+                    self.gather.landed(z)
                 for copy in self.copies(z):
                     copy.start()
 
@@ -412,10 +449,8 @@
                 arrive(self.part(d_peer[1], z), self.kd + z)
 
         def sent(self):
-            for z in range(A):
-                for copy in self.copies(z):
-                    copy.wait_send()
-                self.onward(z).wait_send()
+            for k in (self.sx, self.sc, self.sd):
+                all_sent(self.ref.at[n], k)
 
     class Share:
         def __init__(self, ref, chunks):
@@ -484,7 +519,8 @@
             self.size = 2 * count if z_first else count
             self.next = 0
             self.z_lanes = lanes and (0, lanes[1])
-            self.ky, self.kz, self.kl = take(1 if z_first else A), take(A + 1), take_send(A)
+            self.ky, self.kz = take(1 if z_first else A), take(A + 1)
+            self.sy, self.sz = take_send(), take_send()
 
         def part(self, wide):
             return rows(self.ref, wide * self.count, self.count, self.lanes)
@@ -501,14 +537,14 @@
             return rows(self.z, slot * self.size, self.size, self.z_lanes)
 
         def across(self, z):
-            return remote(self.part(z * 2 + 1 - yi), self.got_y(z), self.ky + z, y_peer)
+            return remote(self.part(z * 2 + 1 - yi), self.got_y(z), self.ky + z, y_peer, self.sy)
 
         def along(self, z, to_right):
             block = self.block(z)
             if to_right:
-                return remote(block, self.got_z(z), self.kz + z, right_peer)
+                return remote(block, self.got_z(z), self.kz + z, right_peer, self.sz)
             slot = jnp.where(z == zi - 1, A, z)
-            return remote(block, self.got_z(slot), self.kz + slot, left_peer, self.kl + z)
+            return remote(block, self.got_z(slot), self.kz + slot, left_peer, self.sz)
 
         def start(self, z):
             if not self.z_first:
@@ -554,18 +590,13 @@
 
         def direct(self, z):
             return remote(
-                self.block(z), self.got_z(zi), self.kz + zi, (z * 2 + yi, n), self.kl + z
+                self.block(z), self.got_z(zi), self.kz + zi, (z * 2 + yi, n), self.sz
             )
 
         def finish_direct(self):
             self.total[...] = self.gather_y(zi)
             for step in range(1, A):
                 self.add((zi + step) % A)
-
-        def sent_direct(self):
-            for z in range(A):
-                self.across(z).wait_send()
-                pl.when(zi != z)(lambda: self.direct(z).wait_send())
 
         def start_ends(self):
             @pl.when(zi == 0)
@@ -596,7 +627,7 @@
                 self.last_across().start()
 
         def last_across(self):
-            return remote(self.part(zi * 2 + 1 - yi), self.got_y(0), self.ky, y_peer)
+            return remote(self.part(zi * 2 + 1 - yi), self.got_y(0), self.ky, y_peer, self.sy)
 
         def finish_y(self):
             if self.z_first:
@@ -605,13 +636,11 @@
                 self.total[...] = mine + self.got_y(0)[...].astype(f32)
 
         def sent(self):
-            if self.z_first:
-                self.last_across().wait_send()
-            for z in range(A):
-                if not self.z_first:
-                    self.across(z).wait_send()
-                pl.when(zi < z)(lambda: self.along(z, True).wait_send())
-                pl.when(zi > z)(lambda: self.along(z, False).wait_send())
+            def parts(count):
+                return rows(self.ref, 0, count * self.count, self.lanes)
+
+            all_sent(parts(1 if self.z_first else A), self.sy)
+            all_sent(parts((A - 1) * (2 if self.z_first else 1)), self.sz)
 
     if A == 4:
         z_order = []
@@ -623,24 +652,25 @@
     chunks = y.chunks
     last = len(chunks) - 1
     cuts = [(base, wide + units) for base, wide, _, units in chunks]
-    g_wq = Gather(s.WQ.at[n], RW)
-    g_pt = Gather(s.PT.at[n], RW)
-    g_kv = Gather(s.KVF, T)
+    g_wq = Gather(s.WQ.at[n], RW, y_first="wq" in y_first_gathers)
+    g_pt = Gather(s.PT.at[n], RW, y_first="pt" in y_first_gathers)
+    g_kv = Gather(s.KVF, y.KT, y_first="kv" in y_first_gathers)
     g_fw = [Gather(s.FW, RW, lanes, i in y_first_chunks) for i, lanes in enumerate(cuts)]
     f_wq, f_pt = Spread(g_wq, s.WQ), Spread(g_pt, s.PT)
     h_mix, h_bg, h_og, h_tg = Share(s.MIX, 4), Share(s.BG, 1), Share(o_out, 1), Share(o_tok, 2)
     n_mb = NarrowSum(s.MB, s.MBC, s.MBX, s.MBS)
     n_op = NarrowSum(s.OP, s.OPC, s.OPX, s.OPS)
-    w_kv = WideSum(s.KVF, s.DKVY, s.DKVR, s.DKVO, T)
+    w_kv = WideSum(s.KVF, s.DKVY, s.DKVR, s.DKVO, y.KT, z_first="wkv" in z_first_sums)
     w_fw = []
     for i, lanes in enumerate(cuts):
         out = o_fw.at[:, pl.ds(*lanes)]
         got = (s.RF0, s.RF1, s.RF2)[i]
         w_fw.append(WideSum(s.FW, s.YFW, got, out, RW, lanes, i in z_first_chunks))
-    w_pt = WideSum(s.PPT, s.YPT, s.RPT, o_pt, RW)
-    w_q = WideSum(s.PQ, s.YQ, s.RQ, o_q, RW)
-    k_a2a, k_gain = take(3), take(3)
-    assert taken[0] <= rsem.shape[0] and taken[1] <= ssem.shape[0]
+    w_pt = WideSum(s.PPT, s.YPT, s.RPT, o_pt, RW, z_first="wpt" in z_first_sums)
+    w_q, tiles = [], [(0, LANES), (LANES, LANES)]
+    for lanes, got in zip(tiles, (s.RQ0, s.RQ1)):
+        w_q.append(WideSum(s.PQ, s.YQ, got, o_q.at[:, pl.ds(*lanes)], RW, lanes))
+    k_a2a, k_gain = (take(3), take(3)), take(3)
 
     ops = {}
 
@@ -665,10 +695,10 @@
             ops[f"{name}.s{i}"] = lambda count=count: spread.pump(count)
             ops[f"{name}.f{i}"] = lambda count=count: spread.pump_forward(count)
 
-    def sum_ops(name, exchange, finish, direct=False):
+    def sum_ops(name, exchange, finish):
         for i in range(3):
             count = A if i == 2 else 1
-            if direct:
+            if name in direct_sums:
                 ops[f"{name}.d{i}"] = lambda count=count: exchange.send_direct(count)
             else:
                 extra = 1 if exchange.z_first and i == 1 else 0
@@ -686,23 +716,35 @@
     spread_ops("fwq", f_wq)
     spread_ops("fpt", f_pt)
 
-    def chunk_finish(i):
+    def chunk_finish(i, name):
         exchange, lanes = w_fw[i], pl.ds(*cuts[i])
-        (exchange.finish_y if exchange.z_first else exchange.finish)()
+        if name in direct_sums:
+            exchange.finish_direct()
+        else:
+            (exchange.finish_y if exchange.z_first else exchange.finish)()
         write(exchange.total, r_fw.at[:, lanes])
 
-    for i, name in enumerate("abc"):
+    for i, name in zip(chunk_order, "abc"):
         gather_ops(name, g_fw[i], True)
-        sum_ops("w" + name, w_fw[i], lambda i=i: chunk_finish(i))
-
-    def direct_finish(exchange, target=None):
-        exchange.finish_direct()
+        sum_ops("w" + name, w_fw[i], lambda i=i, name="w" + name: chunk_finish(i, name))
+
+    def factor_finish(name, exchange, target=None):
+        if name in direct_sums:
+            exchange.finish_direct()
+        else:
+            (exchange.finish_y if exchange.z_first else exchange.finish)()
         if target is not None:
             write(exchange.total, target)
 
-    sum_ops("wkv", w_kv, lambda: direct_finish(w_kv), True)
-    sum_ops("wpt", w_pt, lambda: direct_finish(w_pt, r_pt), True)
-    sum_ops("wq2", w_q, lambda: direct_finish(w_q, r_q), True)
+    sum_ops("wkv", w_kv, lambda: factor_finish("wkv", w_kv))
+    sum_ops("wpt", w_pt, lambda: factor_finish("wpt", w_pt, r_pt))
+    for i, name in enumerate(("wqa", "wqb")):
+        target = r_q.at[:, pl.ds(*tiles[i])]
+        sum_ops(
+            name,
+            w_q[i],
+            lambda i=i, name=name, target=target: factor_finish(name, w_q[i], target),
+        )
 
     own = pl.ds(pl.multiple_of(w * RW, RW), RW)
     own_rows = pl.ds(pl.multiple_of(n * T, T), T)
@@ -728,11 +770,14 @@
 
     @op("prep_pt")
     def _():
+        loads[0].wait()
         for first in range(0, 256, LANES):
             s.PT[n, own, first : first + LANES] = project[first : first + LANES, :].T
 
     @op("prep_fw")
     def _():
+        for load in loads[1:4]:
+            load.wait()
         for base, wide, unit, _ in chunks[:last]:
             for part, weight in enumerate((gating, upward, downward)):
                 for first in range(0, 256, LANES):
@@ -790,6 +835,7 @@
 
     @op("project")
     def _():
+        loads[4].wait()
         f_wq.landed()
         gains = s.WQ[0, :, LANES:].astype(f32).T
         s.GAIN[0:1, :] = gains[y.og : y.og + 1]
@@ -803,12 +849,14 @@
         held.second_tiles = [part[:, LANES:] for part in factors]
 
         kv_own = pl.ds(pl.multiple_of(w * T, T), T)
-        s.KVF[kv_own, 0:128] = rotated(collect(y.oK, y.SK)).astype(bf16)
-        s.KVF[kv_own, 128:256] = collect(y.oV, y.SK).astype(bf16)
-        s.KVF[kv_own, 256:384] = place_lanes(
+        kv_own = pl.multiple_of(w * y.KT, 32)
+        s.KVF[pl.ds(kv_own, T), 0:128] = rotated(collect(y.oK, y.SK)).astype(bf16)
+        s.KVF[pl.ds(kv_own, T), 128:256] = collect(y.oV, y.SK).astype(bf16)
+        heads = place_lanes(
             [(held.second_tiles[p], y.ok, p * y.HK, y.HK) for p in range(N)]
             + [(held.second_tiles[p], y.ov, (N + p) * y.HK, y.HK) for p in range(N)]
-        ).astype(bf16)
+        )
+        s.KVF[pl.ds(kv_own + T, T // 4), :] = pack_heads(heads).astype(bf16)
 
     def spread_heads(r):
         return dot_nn(s.QH[:, :LANES], s.EQ[r]) + dot_nn(s.QH[:, LANES:], s.EQ[r])
@@ -840,10 +888,15 @@
         lax.fori_loop(0, N, norm_rows, 0)
 
     def expand_block(block):
-        at = pl.ds(pl.multiple_of(block * KB, KB), KB)
-        s.SHARED[0] = s.KVF[at, 0:128].astype(f32).T
-        s.SHARED[1] = s.KVF[at, 128:256].astype(f32).T
-        heads = s.KVF[at, 256:384].astype(f32).T
+        tiles = []
+        for t in range(KB // T):
+            first = pl.multiple_of((block * (KB // T) + t) * y.KT, 32)
+            lanes = slice(t * T, (t + 1) * T)
+            for kind in range(2):
+                shared = s.KVF[pl.ds(first, T), kind * 128 : kind * 128 + 128]
+                s.SHARED[kind, :, lanes] = shared.astype(f32).T
+            tiles.append(unpack_heads(s.KVF[pl.ds(first + T, T // 4), :].astype(f32)).T)
+        heads = jnp.concatenate(tiles, axis=1)
         for i in range(pairs):
             for kind in range(2):
                 first = kind * y.heads * KR + 4 * i
@@ -934,6 +987,7 @@
 
     @op("middle")
     def _():
+        loads[5].wait()
         h_mix.landed_all()
         f_pt.landed()
         def middle_rows(block, _):
@@ -979,7 +1033,7 @@
             s.GG[at, first + 2 * width :] = jnp.where(tail_low, gate_back, up_back).astype(bf16)
         mid = dot_nt(s.GG[at, first : first + wide], s.FW[:, base : base + wide])
         out = dot_nt(s.HID[at, unit : unit + units], s.FW[:, base + wide : base + wide + units])
-        if chunk:
+        if chunk != chunk_order[0]:
             mid = mid + s.MB[at, :].astype(f32)
             out = out + s.OP[at, :].astype(f32)
         s.MB[at, :] = mid.astype(bf16)
@@ -1015,14 +1069,14 @@
         dense_rows(chunk, True)
         dense_rows(chunk, False)
 
-    for i, name in enumerate("abc"):
+    for i, name in zip(chunk_order, "abc"):
         ops["ff_" + name] = lambda i=i: dense_chunk(i)
         ops["g_" + name] = lambda i=i: dense_grads(i)
 
     def last_dense(far):
         if far:
-            g_fw[last].landed_all()
-        dense_rows(last, far)
+            g_fw[chunk_order[-1]].landed_all()
+        dense_rows(chunk_order[-1], far)
         n_mb.start(far)
 
     ops["ffCf"] = lambda: last_dense(True)
@@ -1091,11 +1145,16 @@
         if part < 3:
             return
         at = pl.ds(pl.multiple_of(block * KB, KB), KB)
-        for kind in range(2):
-            s.KVF[at, kind * 128 : kind * 128 + 128] = (s.DST[kind] * 0.5).T.astype(bf16)
         heads = [s.DHT[i, 4 * kind : 4 * kind + 4, :] for kind in range(2) for i in range(pairs)]
         heads.append(jnp.zeros((LANES - 8 * pairs, KB), f32))
-        s.KVF[at, 256:384] = (jnp.concatenate(heads, axis=0) * 0.5).T.astype(bf16)
+        heads = jnp.concatenate(heads, axis=0) * 0.5
+        for t in range(KB // T):
+            first = pl.multiple_of((block * (KB // T) + t) * y.KT, 32)
+            lanes = slice(t * T, (t + 1) * T)
+            for kind in range(2):
+                shared = (s.DST[kind, :, lanes] * 0.5).T
+                s.KVF[pl.ds(first, T), kind * 128 : kind * 128 + 128] = shared.astype(bf16)
+            s.KVF[pl.ds(first + T, T // 4), :] = pack_heads(heads[:, lanes].T).astype(bf16)
 
     def backward_quarter(part):
         if part == 0:
@@ -1170,15 +1229,55 @@
         h_tg.landed_all()
         write(o_tok, r_tok)
 
-    @op("qg")
-    def _():
-        key_shared = rotated(s.DKVO[:, 0:128], back=True)
-        value_shared = s.DKVO[:, 128:256]
-        head_tile = s.DKVO[:, 256:384]
+    def exchange_factors(tile):
+        lanes = pl.ds(*tiles[tile])
+        for k, peer in enumerate(narrow_peers):
+            to = s.QGR.at[n, :, lanes]
+            send(s.QGS.at[peer[1], :, lanes], to, k_a2a[tile] + k, peer)
+        s.QGR[n, :, lanes] = s.QGS[n, :, lanes]
+
+    def factors_through(tile):
+        lanes = pl.ds(*tiles[tile])
+        total = jnp.zeros((T, D), f32)
+        for p in range(N):
+            total = total + dot_nt(s.QGS[p, :, lanes], s.WQ[p, :, lanes])
+        return total
+
+    def factor_gradients(tile):
+        lanes = pl.ds(*tiles[tile])
+        for k, peer in enumerate(narrow_peers):
+            arrive(s.QGR.at[peer[1], :, lanes], k_a2a[tile] + k)
+        for j in range(4):
+            block = pl.ds(pl.multiple_of(j * 256, 256), 256)
+            value = jnp.zeros((256, LANES), f32)
+            for p in range(N):
+                value = value + dot_tn(s.NORM[p * T : (p + 1) * T, block], s.QGR[p, :, lanes])
+            s.PQ[block, lanes] = value.astype(bf16)
+
+    @op("qg1")
+    def _():
         for p in range(N):
             s.QGS[p, :, :LANES] = place_lanes(
                 canonical_pieces(held.shared_tiles, LANES, p * y.SQ, y.SQ, 0, 0)
             ).astype(bf16)
+        exchange_factors(0)
+
+    @op("fb1")
+    def _():
+        held.first_back = factors_through(0)
+
+    @op("q.g1")
+    def _():
+        factor_gradients(0)
+        for z in z_order:
+            w_q[0].start(z)
+
+    @op("qg")
+    def _():
+        key_shared = rotated(s.DKVO[:T, 0:128], back=True)
+        value_shared = s.DKVO[:T, 128:256]
+        head_tile = unpack_heads(s.DKVO[T:, :])
+        for p in range(N):
             s.QGS[p, :, LANES:] = place_lanes(
                 [
                     (key_shared, p * y.SK, y.oK, y.SK),
@@ -1188,15 +1287,11 @@
                     (head_tile, (N + p) * y.HK, y.ov, y.HK),
                 ]
             ).astype(bf16)
-        for k, peer in enumerate(narrow_peers):
-            send(s.QGS.at[peer[1]], s.QGR.at[n], k_a2a + k, peer)
-        s.QGR[n] = s.QGS[n]
+        exchange_factors(1)
 
     @op("fb")
     def _():
-        first_back = jnp.zeros((T, D), f32)
-        for p in range(N):
-            first_back = first_back + dot_nt(s.QGS[p], s.WQ[p])
+        first_back = held.first_back + factors_through(1)
         x_own = tok[own_rows, :].astype(f32)
         r1_own = row_scale(x_own)
         s.GS[0:1, :] = jnp.sum(first_back * x_own * r1_own, axis=0, keepdims=True)
@@ -1214,10 +1309,9 @@
 
     @op("q.g")
     def _():
-        for k, peer in enumerate(narrow_peers):
-            arrive(s.QGR.at[peer[1]], k_a2a + k)
         for k in range(3):
             arrive(s.GR.at[k], k_gain + k)
+        factor_gradients(1)
         gain_rows = s.GS[...]
         for k in range(3):
             gain_rows = gain_rows + s.GR[k]
@@ -1228,37 +1322,63 @@
             jnp.where(lane_row == y.og + 1, gain_rows[1:2], 0.0),
         )
         gain_columns = spread.T
-        for j in range(4):
-            block = z_order[j] if A == 4 else j
-            lanes = pl.ds(pl.multiple_of(block * 256, 256), 256)
-            value = jnp.zeros((256, 256), f32)
-            for p in range(N):
-                value = value + dot_tn(s.NORM[p * T : (p + 1) * T, lanes], s.QGR[p])
-            s.PQ[pl.ds(pl.multiple_of(block * 256, 256), 256), :] = value.astype(bf16)
         s.PQ[:, LANES:] = (s.PQ[:, LANES:].astype(f32) + gain_columns).astype(bf16)
         for z in z_order:
-            w_q.start(z)
+            w_q[1].start(z)
 
     for name in schedule:
         ops[name]()
 
-    for exchange in (g_wq, g_pt, f_wq, f_pt, *w_fw):
+    for exchange in (g_wq, g_pt, f_wq, f_pt, *w_fw, w_kv, w_pt, *w_q):
         exchange.sent()
-    for exchange in (w_kv, w_pt, w_q):
-        exchange.sent_direct()
+    assert (taken[0], taken[1]) == (rsem.shape[0], ssem.shape[0])
     for copy in pending:
         copy.wait_send()
     for copy in written:
         copy.wait()
 
 
-def results_kernel(y, out, tok, fw, pt, q, *outs):
-    o_out, o_tok, o_pre, o_qh, o_qs, o_kh, o_ks, o_vh, o_vs, o_pt, o_mid, o_gate, o_up, o_down = outs
+def results_kernel(y, out, tok, fw, pt, q, *refs):
+    r_out, r_tok, r_pt, r_gate, r_up, r_down = refs[:6]
+    o_pre, o_qh, o_qs, o_kh, o_ks, o_vh, o_vs, o_mid = refs[6:14]
+    in_fw, in_pt, in_q, in_tok, in_out, o_tok, o_pt, o_gate, o_up, o_down, sems = refs[14:]
     FM, F, half = y.FM, y.F, y.F - y.FM
-    o_out[...] = out[...]
-    o_tok[...] = tok[...].astype(f32)
-    o_qs[...] = q[:, :LANES].T[: y.SQ]
-    second = q[:, LANES:].T
+    used = []
+
+    def start(src, dst):
+        copy = pltpu.make_async_copy(src, dst, sems.at[len(used)])
+        copy.start()
+        used.append(copy)
+        return copy
+
+    got_fw, got_pt, got_q = start(fw, in_fw), start(pt, in_pt), start(q, in_q)
+    got_tok, got_out = start(tok, in_tok), start(out, in_out)
+    got_fw.wait()
+    *whole_chunks, (base, wide, unit, _) = y.chunks
+    for part, (target, result) in enumerate(((o_gate, r_gate), (o_up, r_up), (o_down, r_down))):
+        for at, _, first_unit, _ in whole_chunks:
+            for first in range(0, 256, LANES):
+                place = at + part * 256 + first
+                to = first_unit + first
+                target[to : to + LANES, :] = in_fw[:, place : place + LANES].T
+        place = base + (wide if part == 2 else part * LANES)
+        target[unit:FM, :] = in_fw[:, place : place + LANES].T
+        tail = base + (wide + LANES if part == 2 else 2 * LANES)
+        tail = in_fw[:, tail : tail + LANES].T
+        target[FM:, :] = tail[half:] if part == 1 else tail[:half]
+        start(target, result)
+    got_tok.wait()
+    o_tok[...] = in_tok[...].astype(f32)
+    start(o_tok, r_tok)
+    got_out.wait()
+    start(in_out, r_out)
+    got_pt.wait()
+    for first in range(0, 256, LANES):
+        o_pt[first : first + LANES, :] = in_pt[:, first : first + LANES].T
+    start(o_pt, r_pt)
+    got_q.wait()
+    o_qs[...] = in_q[:, :LANES].T[: y.SQ]
+    second = in_q[:, LANES:].T
     o_ks[...] = second[y.oK : y.oK + y.SK]
     o_vs[...] = second[y.oV : y.oV + y.SK]
     o_qh[...] = second[y.oq : y.oq + y.HQ]
@@ -1266,21 +1386,8 @@
     o_vh[...] = second[y.ov : y.ov + y.HK]
     o_pre[...] = second[y.og : y.og + 1]
     o_mid[...] = second[y.og + 1 : y.og + 2]
-    for first in range(0, 256, LANES):
-        o_pt[first : first + LANES, :] = pt[:, first : first + LANES].T
-    *whole_chunks, (base, wide, unit, _) = y.chunks
-    for at, _, start, _ in whole_chunks:
-        for part, target in enumerate((o_gate, o_up, o_down)):
-            for first in range(0, 256, LANES):
-                place = at + part * 256 + first
-                target[start + first : start + first + LANES, :] = fw[:, place : place + LANES].T
-    o_gate[unit:FM, :] = fw[:, base : base + LANES].T
-    o_up[unit:FM, :] = fw[:, base + LANES : base + 2 * LANES].T
-    tail = fw[:, base + 2 * LANES : base + wide].T
-    o_gate[FM:, :] = tail[:half]
-    o_up[FM:, :] = tail[half:]
-    o_down[unit:FM, :] = fw[:, base + wide : base + wide + LANES].T
-    o_down[FM:, :] = fw[:, base + wide + LANES :].T[:half]
+    for copy in used[5:]:
+        copy.wait()
 
 
 def solution(mesh):
@@ -1309,10 +1416,9 @@
         y = make_layout(W, N, T, D, F, L, N * kheads.shape[1] // KR)
         assert R == N
         scratch = scratch_list(y)
-        line, direct = y.A + 2, 2 * y.A + 1
-        arrivals = 18 * y.A + 36 + 3 * direct
-        arrivals += sum(line if i in z_first_chunks else direct for i in range(3))
-        sends = arrivals + 12 * y.A
+        z_first = len(z_first_chunks) + len(z_first_sums)
+        arrivals = 18 * y.A + 39 + z_first * (y.A + 2) + (7 - z_first) * (2 * y.A + 1)
+        sends = 71 + len(y_first_chunks) + len(y_first_gathers)
         vmem = pl.BlockSpec(memory_space=pltpu.VMEM)
 
         def kernel(*refs):
@@ -1328,16 +1434,15 @@
                 shape((RW, 256), f32),
                 shape((RW, 256), f32),
             ),
-            in_specs=[vmem] * 15,
+            in_specs=[vmem] * 9 + [pl.BlockSpec(memory_space=pl.ANY)] * 6,
             out_specs=[pl.BlockSpec(memory_space=pl.ANY)] * 5,
             scratch_shapes=[*scratch.values()]
-            + [pltpu.SemaphoreType.DMA((count,)) for count in (sends, arrivals, 7)],
+            + [pltpu.SemaphoreType.DMA((count,)) for count in (sends, arrivals, 8, 6)],
             compiler_params=pltpu.CompilerParams(
                 collective_id=0, has_side_effects=True, vmem_limit_bytes=63 * 2**20
             ),
             name="block",
         )(
-            tokens.reshape(y.M, D),
             documents,
             prenorm.reshape(1, RW),
             qheads.T,
@@ -1346,47 +1451,43 @@
             kshared.T,
             vheads.T,
             vshared.T,
+            midnorm.reshape(1, RW),
             project,
-            midnorm.reshape(1, RW),
             gating.T,
             upward.T,
             downward,
+            tokens.reshape(y.M, D),
             cotangent.reshape(y.M, D),
         )
 
         def results(*refs):
             results_kernel(y, *refs)
 
+        large = ((y.M, D), bf16), ((y.M, D), f32), ((256, RW), f32), *[((F, RW), f32)] * 3
+        small = [(count, RW) for count in (1, y.HQ, y.SQ, y.HK, y.SK, y.HK, y.SK, 1)]
+        held = [((RW, y.FW), f32), ((RW, 256), f32), ((RW, 256), f32), ((y.M, D), bf16), *large]
         outputs = pl.pallas_call(
             results,
-            out_shape=(
-                shape((y.M, D), bf16),
-                shape((y.M, D), f32),
-                shape((1, RW), f32),
-                shape((y.HQ, RW), f32),
-                shape((y.SQ, RW), f32),
-                shape((y.HK, RW), f32),
-                shape((y.SK, RW), f32),
-                shape((y.HK, RW), f32),
-                shape((y.SK, RW), f32),
-                shape((256, RW), f32),
-                shape((1, RW), f32),
-                shape((F, RW), f32),
-                shape((F, RW), f32),
-                shape((F, RW), f32),
-            ),
-            in_specs=[vmem] * 5,
-            out_specs=[vmem] * 14,
+            out_shape=[shape(*each) for each in large] + [shape(each, f32) for each in small],
+            in_specs=[pl.BlockSpec(memory_space=pl.ANY)] * 5,
+            out_specs=[pl.BlockSpec(memory_space=pl.ANY)] * 6 + [vmem] * 8,
+            scratch_shapes=[pltpu.VMEM(*each) for each in held] + [pltpu.SemaphoreType.DMA((11,))],
             compiler_params=pltpu.CompilerParams(vmem_limit_bytes=63 * 2**20),
             name="results",
         )(*raw)
-        turned = (3, 4, 5, 6, 7, 8, 11, 12)
-        outputs = [v.T if i in turned else v for i, v in enumerate(outputs)]
-        outputs[0] = outputs[0].reshape(R, T, D)
-        outputs[1] = outputs[1].reshape(R, T, D)
-        outputs[2] = outputs[2].reshape(RW)
-        outputs[10] = outputs[10].reshape(RW)
-        return tuple(outputs)
+        out, tok, pt_back, gate, up, down, pre, qh, qs, kh, ks, vh, vs, mid = outputs
+        tokens_like = lambda values: values.reshape(R, T, D)
+        return (
+            tokens_like(out),
+            tokens_like(tok),
+            pre.reshape(RW),
+            *[each.T for each in (qh, qs, kh, ks, vh, vs)],
+            pt_back,
+            mid.reshape(RW),
+            gate.T,
+            up.T,
+            down,
+        )
 
     split = P("wide", "narrow")
     flipped = P("narrow", "wide")

time: 153 us -> 135 us (0.88)
  Pallas kernels: 152 us -> 134 us
    pallas_call x1, Pallas kernels: 147 us -> 130 us  [on_device(): pl.pallas_call(kernel, out_shape=(shape((y.M, D), bf16), shape((y.M, D),...]
where the time goes in v4:
time: 135 us
  Pallas kernels  134 us (99%)
    pallas_call x1, Pallas kernels, on_device(): pl.pallas_call(kernel, out_shape=(shape((y.M, D), bf16), shape((y.M, D),...  130 us
    pallas_call x1, Pallas kernels, on_device(): pl.pallas_call(results, out_shape=[shape(*each) for each in large] + [sha...  4.22 us

profile of v4, /device:TPU:0, one launch (start us, length us, event | category | flops | bytes accessed | tf_op | source)
XLA Modules:
  0.0 135.0 jit_solution(10615155044836823165)
XLA Ops:
  0.7 129.9 %block.1 = (bf16[512,1024]{1,0:T(8,128)(2,1)}, bf16[512,1024]{1,0:T(8,128)(2,1)}, f32[128,2176]{1,0:T(8,128)}, f32[128,256]{1,0:T(8,128)}, f32[128,256]{1,0:T(8,128)}) custom-call(s32[4,1024]{1,0:T(4,128)} %refs_0_.1, bf16[1,128]{1,0:T(2,128)(2,1)} %bitcast.34, bf16[24,128]{1,0:T(8,128)(2,1)} %bitcast.31, bf16[96,128]{1,0:T(8,128)(2,1)} %bitcast.28, ...), custom_call_target="tpu_custom_call" | custom-call | tf_op jit(solution)/shard_map/block/pallas_call | solution.py:1428
  130.6 4.2 %results.1 = (bf16[512,1024]{1,0:T(8,128)(2,1)}, f32[512,1024]{1,0:T(8,128)}, f32[256,128]{1,0:T(8,128)}, f32[704,128]{1,0:T(8,128)}, f32[704,128]{1,0:T(8,128)}...) custom-call(bf16[512,1024]{1,0:T(8,128)(2,1)} %get-tuple-element.33., ...), custom_call_target="tpu_custom_call" | custom-call | tf_op jit(solution)/shard_map/results/pallas_call | solution.py:1469

commit v5 on v4

--- a/solution.py
+++ b/solution.py
@@ -17,9 +17,9 @@
 epsilon = 1e-06
 masked_score = -1e30
 MESH = pl.DeviceIdType.MESH
-y_first_chunks = (1,)
-z_first_chunks = (0,)
-chunk_order = (0, 2, 1)
+gather_parts = (((768, False),), ((512, True), (256, False)), ((384, True), (256, False)))
+sum_parts = (((512, False), (256, True)), ((512, False), (256, True)), ((640, False),))
+chunk_order = (0, 1, 2)
 y_first_gathers = ()
 z_first_sums = ()
 direct_sums = ("wkv", "wqa", "wqb")
@@ -206,8 +206,9 @@
         GR=vm(3, 8, D, kind=f32),
         YFW=vm(A * RW, y.FW),
         **{
-            f"RF{i}": vm((A + 1) * RW * (2 if i in z_first_chunks else 1), wide + units)
-            for i, (_, wide, _, units) in enumerate(y.chunks)
+            f"RF{i}{j}": vm((A + 1) * RW * (1 + z_first), lanes)
+            for i, parts in enumerate(sum_parts)
+            for j, (lanes, z_first) in enumerate(parts)
         },
         PPT=vm(D, 256),
         YPT=vm(A * RW, 256),
@@ -219,21 +220,29 @@
     )
 
 
-schedule = (
-    "prep_wq", "wq.L", "prep_pt", "pt.L", "wq.Ly", "wq.h1", "fwq.s0", "prep_fw", "pt.h1", "wq.h2",
-    "a.L", "fwq.s1", "b.L", "pt.Ly", "wq.h3", "fwq.f0", "c.Ly", "fwq.s2", "fwq.s3", "fwq.f1",
-    "a.h1", "consts", "b.Ly", "a.Ly", "fwq.f2", "fwq.f3", "pt.h2", "project", "kv.L", "b.h1",
-    "fpt.s0", "fpt.s1", "kv.h1", "pt.h3", "kv.Ly", "kv.h2", "kv.h3", "a.h2", "fpt.s2", "b.h2",
-    "c.L", "a.y1", "a.y2", "fpt.f0", "queries", "fpt.s3", "at_x", "a.h3", "at0", "at1", "a.y3",
-    "at2", "mix.f0", "at3", "b.y1", "fpt.f1", "b.y2", "mix.f1", "mix.f2", "b.h3", "fpt.f2",
-    "fpt.f3", "mix.f3", "c.h1", "b.y3", "middle", "ff_a", "g_a", "wa.ends", "c.h2", "ff_b", "g_b",
-    "c.h3", "ffCf", "ffCn", "mb.pass", "wa.s1", "g_c", "wa.s2", "wb.s0", "mid", "bq0", "bq1",
-    "wc.s0", "bq2", "op.start", "bq3", "op.pass", "bg.f", "wb.s1", "wc.s1", "kvst", "qb", "qg1",
-    "fb1", "op.res", "wkv.d0", "q.g1", "wkv.d1", "pt.g", "wkv.d2", "wb.s2", "wqa.d0", "wkv.fin",
-    "qg", "fb", "wpt.s0", "wa.fin", "wqa.d1", "wpt.s1", "wb.fin", "wqa.d2", "wc.s2", "wpt.s2",
-    "q.g", "og.f", "wqb.d0", "wqa.fin", "wc.fin", "wqb.d1", "og.l", "wqb.d2", "wpt.fin", "tg.f",
-    "tg.l", "wa.finy", "wqb.fin",
-)
+def schedule(do):
+    return (
+        do.prep_wq, do.wf_Ly, do.wq_L, do.prep_pt, do.wq_Ly, do.prep_fw, do.b_Ly, do.wf_L,
+        do.pt_L, do.wq_h1, do.fwq_s0, do.wf_h1, do.pt_Ly, do.c2_L, do.fwf_s0, do.wq_h2, do.a_L,
+        do.fwq_s1, do.wf_h2, do.fwq_f0, do.wq_h3, do.c2_Ly, do.pt_h1, do.a_Ly, do.consts,
+        do.fwq_s2, do.fwq_s3, do.fpt_s0, do.fwf_f0, do.fwq_f1, do.wf_h3, do.a_h1, do.fwf_s1,
+        do.fwq_f2, do.pt_h2, do.fwq_f3, do.project, do.c_Ly, do.fpt_s1, do.kv_L, do.fwf_s2,
+        do.c2_h1, do.kv_Ly, do.kv_h1, do.fpt_f0, do.pt_h3, do.fpt_s2, do.b2_L, do.fwf_f1,
+        do.kv_h2, do.b2_Ly, do.a_h2, do.fwf_f2, do.fwf_s3, do.kv_h3, do.fpt_s3, do.c2_h2,
+        do.fpt_f1, do.b2_h1, do.b_L, do.a_y1, do.a_y2, do.fwf_f3, do.queries, do.b2_y1, do.fpt_f2,
+        do.at_x, do.at0, do.at1, do.at2, do.b2_h2, do.c2_h3, do.a_h3, do.a_y3, do.at3, do.mix_f0,
+        do.b2_y2, do.b_h1, do.c2_y1, do.fpt_f3, do.c_L, do.b2_h3, do.b2_y3, do.mix_f1, do.c2_y2,
+        do.mix_f2, do.mix_f3, do.c2_y3, do.middle, do.ff_a, do.g_a, do.wa2_ends, do.b_h2, do.c_h1,
+        do.wa_s0, do.b_h3, do.ff_b, do.g_b, do.wb2_ends, do.c_h2, do.c_h3, do.ffCf, do.wb_s0,
+        do.wa2_s1, do.mb_pass, do.wa_s1, do.ffCn, do.wa2_s2, do.wb2_s1, do.g_c, do.wb2_s2,
+        do.op_start, do.wb_s1, do.mid, do.bq0, do.wc_s0, do.wa_s2, do.bq1, do.bq2, do.op_pass,
+        do.wb_s2, do.bq3, do.kvst, do.wc_s1, do.qb, do.qg1, do.wkv_d0, do.bg_f, do.pt_g,
+        do.wkv_d1, do.wkv_d2, do.op_res, do.wpt_s0, do.q_g1, do.wc_s2, do.wkv_fin, do.qg, do.fb1,
+        do.fb, do.wpt_s1, do.og_f, do.tg_s, do.wqa_d0, do.wa2_fin, do.wqa_d1, do.wa_fin,
+        do.wb_fin, do.q_g, do.wb2_fin, do.wqa_d2, do.og_l, do.wpt_s2, do.wqb_d0, do.wc_fin,
+        do.wqa_fin, do.wa2_finy, do.wqb_d1, do.wqb_d2, do.tg_f, do.tg_l, do.wb2_finy, do.wpt_fin,
+        do.wqb_fin,
+    )
 
 
 def block_kernel(y, names, *refs):
@@ -322,9 +331,10 @@
     pl.semaphore_wait(barrier, len(peers))
 
     class Gather:
-        def __init__(self, ref, count, lanes=None, y_first=False):
+        def __init__(self, ref, count, lanes=None, y_first=False, apart=False):
             self.ref, self.count, self.lanes, self.y_first = ref, count, lanes, y_first
-            self.kz, self.ky = take(A), take(A)
+            self.apart = apart and not y_first
+            self.kz, self.ky = take(A), take(A if self.apart else 1)
             self.sy, self.sr = take_send(), take_send()
             self.sl = take_send() if y_first else self.sr
             self.next = self.next_y = 1
@@ -345,10 +355,10 @@
 
         def across(self, z):
             part = self.part(z * 2 + yi)
-            return remote(part, part, self.ky + z, y_peer, self.sy)
+            return remote(part, part, self.ky + (z if self.apart else 0), y_peer, self.sy)
 
         def landed(self, z):
-            arrive(self.part(z * 2 + 1 - yi), self.ky + z)
+            arrive(self.part(z * 2 + 1 - yi), self.ky + (z if self.apart else 0))
 
         def launch_y(self):
             self.across(zi).start()
@@ -381,8 +391,7 @@
 
         def landed_all(self):
             if not self.y_first:
-                for z in range(A):
-                    self.landed(z)
+                arrive(rows(self.ref, 0, A * self.count, self.lanes), self.ky)
 
         def sent(self):
             def blocks(count):
@@ -400,22 +409,22 @@
 
     class Spread:
         def __init__(self, gather, ref):
-            self.gather, self.ref = gather, ref
+            self.gather, self.ref, self.lanes = gather, ref, gather.lanes
             self.next = self.passed = 0
-            self.kx, self.kc, self.kd = take(A), take(A), take(A)
+            self.kx, self.kc, self.kd = take(A), take(), take()
             self.sx, self.sc, self.sd = take_send(), take_send(), take_send()
 
         def part(self, owner, z):
-            return rows(self.ref.at[owner], z * 2 * RW, 2 * RW)
+            return rows(self.ref.at[owner], z * 2 * RW, 2 * RW, self.lanes)
 
         def copies(self, z):
             part = self.part(n, z)
             to_x = remote(part, part, self.kx + z, x_peer, self.sx)
-            return to_x, remote(part, part, self.kc + z, c_peer, self.sc)
+            return to_x, remote(part, part, self.kc, c_peer, self.sc)
 
         def onward(self, z):
             part = self.part(x_peer[1], z)
-            return remote(part, part, self.kd + z, c_peer, self.sd)
+            return remote(part, part, self.kd, c_peer, self.sd)
 
         def start(self, distance):
             def act(z, _):
@@ -444,18 +453,17 @@
             each_at(distance, act)
 
         def landed(self):
-            for z in range(A):
-                arrive(self.part(c_peer[1], z), self.kc + z)
-                arrive(self.part(d_peer[1], z), self.kd + z)
+            for peer, k in ((c_peer, self.kc), (d_peer, self.kd)):
+                arrive(rows(self.ref.at[peer[1]], 0, D, self.lanes), k)
 
         def sent(self):
             for k in (self.sx, self.sc, self.sd):
-                all_sent(self.ref.at[n], k)
+                all_sent(rows(self.ref.at[n], 0, D, self.lanes), k)
 
     class Share:
         def __init__(self, ref, chunks):
             self.ref, self.chunks = ref, chunks
-            self.kx, self.kc, self.kd = take(chunks), take(chunks), take(chunks)
+            self.kx, self.kc, self.kd = take(chunks), take(), take()
             self.width = D // chunks
 
         def part(self, owner, chunk):
@@ -464,28 +472,20 @@
 
         def start(self, chunk):
             send(self.part(n, chunk), self.part(n, chunk), self.kx + chunk, x_peer)
-            send(self.part(n, chunk), self.part(n, chunk), self.kc + chunk, c_peer)
+            send(self.part(n, chunk), self.part(n, chunk), self.kc, c_peer)
 
         def forward(self, chunk):
             part = self.part(x_peer[1], chunk)
             arrive(part, self.kx + chunk)
-            send(part, part, self.kd + chunk, c_peer)
-
-        def landed(self, chunk):
-            arrive(self.part(c_peer[1], chunk), self.kc + chunk)
-            arrive(self.part(d_peer[1], chunk), self.kd + chunk)
+            send(part, part, self.kd, c_peer)
 
         def forward_all(self):
             for chunk in range(self.chunks):
                 self.forward(chunk)
 
         def landed_all(self):
-            for chunk in range(self.chunks):
-                self.landed(chunk)
-
-        def finish(self):
-            self.forward_all()
-            self.landed_all()
+            for peer, k in ((c_peer, self.kc), (d_peer, self.kd)):
+                arrive(rows(self.ref, peer[1] * T, T), k)
 
     class NarrowSum:
         def __init__(self, part_ref, core_ref, x_ref, send_ref):
@@ -513,13 +513,15 @@
             )
 
     class WideSum:
-        def __init__(self, part_ref, y_ref, z_ref, out_ref, count, lanes=None, z_first=False):
+        def __init__(
+            self, part_ref, y_ref, z_ref, out_ref, count, lanes=None, z_first=False, straight=False
+        ):
             self.ref, self.y, self.z, self.total = part_ref, y_ref, z_ref, out_ref
             self.count, self.lanes, self.z_first = count, lanes, z_first
             self.size = 2 * count if z_first else count
             self.next = 0
             self.z_lanes = lanes and (0, lanes[1])
-            self.ky, self.kz = take(1 if z_first else A), take(A + 1)
+            self.ky, self.kz = take(1 if z_first else A), take(1 if straight else A + 1)
             self.sy, self.sz = take_send(), take_send()
 
         def part(self, wide):
@@ -590,13 +592,15 @@
 
         def direct(self, z):
             return remote(
-                self.block(z), self.got_z(zi), self.kz + zi, (z * 2 + yi, n), self.sz
+                self.block(z), self.got_z(zi), self.kz, (z * 2 + yi, n), self.sz
             )
 
         def finish_direct(self):
-            self.total[...] = self.gather_y(zi)
+            total = self.gather_y(zi)
+            arrive(rows(self.z, 0, (A - 1) * self.size, self.z_lanes), self.kz)
             for step in range(1, A):
-                self.add((zi + step) % A)
+                total = total + self.got_z((zi + step) % A)[...].astype(f32)
+            self.total[...] = total
 
         def start_ends(self):
             @pl.when(zi == 0)
@@ -652,24 +656,36 @@
     chunks = y.chunks
     last = len(chunks) - 1
     cuts = [(base, wide + units) for base, wide, _, units in chunks]
-    g_wq = Gather(s.WQ.at[n], RW, y_first="wq" in y_first_gathers)
-    g_pt = Gather(s.PT.at[n], RW, y_first="pt" in y_first_gathers)
+    g_wq = Gather(s.WQ.at[n], RW, (LANES, LANES), "wq" in y_first_gathers, True)
+    g_wf = Gather(s.WQ.at[n], RW, (0, LANES), "wf" in y_first_gathers, True)
+    g_pt = Gather(s.PT.at[n], RW, y_first="pt" in y_first_gathers, apart=True)
     g_kv = Gather(s.KVF, y.KT, y_first="kv" in y_first_gathers)
-    g_fw = [Gather(s.FW, RW, lanes, i in y_first_chunks) for i, lanes in enumerate(cuts)]
-    f_wq, f_pt = Spread(g_wq, s.WQ), Spread(g_pt, s.PT)
+
+    def in_parts(chunk, parts):
+        first = cuts[chunk][0]
+        for lanes, flag in parts[chunk]:
+            yield (first, lanes), flag
+            first += lanes
+
+    g_fw = [[Gather(s.FW, RW, *part) for part in in_parts(i, gather_parts)] for i in range(3)]
+    f_wq, f_wf, f_pt = Spread(g_wq, s.WQ), Spread(g_wf, s.WQ), Spread(g_pt, s.PT)
     h_mix, h_bg, h_og, h_tg = Share(s.MIX, 4), Share(s.BG, 1), Share(o_out, 1), Share(o_tok, 2)
     n_mb = NarrowSum(s.MB, s.MBC, s.MBX, s.MBS)
     n_op = NarrowSum(s.OP, s.OPC, s.OPX, s.OPS)
-    w_kv = WideSum(s.KVF, s.DKVY, s.DKVR, s.DKVO, y.KT, z_first="wkv" in z_first_sums)
-    w_fw = []
-    for i, lanes in enumerate(cuts):
-        out = o_fw.at[:, pl.ds(*lanes)]
-        got = (s.RF0, s.RF1, s.RF2)[i]
-        w_fw.append(WideSum(s.FW, s.YFW, got, out, RW, lanes, i in z_first_chunks))
-    w_pt = WideSum(s.PPT, s.YPT, s.RPT, o_pt, RW, z_first="wpt" in z_first_sums)
+    kind_of = lambda name: (name in z_first_sums, name in direct_sums)
+    w_kv = WideSum(s.KVF, s.DKVY, s.DKVR, s.DKVO, y.KT, None, *kind_of("wkv"))
+    w_fw = [[], [], []]
+    for i in range(3):
+        for j, (lanes, z_first) in enumerate(in_parts(i, sum_parts)):
+            out, got = o_fw.at[:, pl.ds(*lanes)], vars(s)[f"RF{i}{j}"]
+            name = f"w{'abc'[chunk_order.index(i)]}{'2' if j else ''}"
+            straight = name in direct_sums
+            w_fw[i].append(WideSum(s.FW, s.YFW, got, out, RW, lanes, z_first, straight))
+    w_pt = WideSum(s.PPT, s.YPT, s.RPT, o_pt, RW, None, *kind_of("wpt"))
     w_q, tiles = [], [(0, LANES), (LANES, LANES)]
-    for lanes, got in zip(tiles, (s.RQ0, s.RQ1)):
-        w_q.append(WideSum(s.PQ, s.YQ, got, o_q.at[:, pl.ds(*lanes)], RW, lanes))
+    for lanes, got, name in zip(tiles, (s.RQ0, s.RQ1), ("wqa", "wqb")):
+        out = o_q.at[:, pl.ds(*lanes)]
+        w_q.append(WideSum(s.PQ, s.YQ, got, out, RW, lanes, *kind_of(name)))
     k_a2a, k_gain = (take(3), take(3)), take(3)
 
     ops = {}
@@ -682,51 +698,55 @@
         return keep
 
     def gather_ops(name, gather, split):
-        ops[f"{name}.L"], ops[f"{name}.Ly"] = gather.launch, gather.launch_y
+        ops[f"{name}_L"], ops[f"{name}_Ly"] = gather.launch, gather.launch_y
         for i in range(1, 4):
             count = A if i == 3 else 1
-            ops[f"{name}.h{i}"] = lambda count=count: gather.pump(count, not split)
+            ops[f"{name}_h{i}"] = lambda count=count: gather.pump(count, not split)
             if split and not gather.y_first:
-                ops[f"{name}.y{i}"] = lambda count=count: gather.pump_y(count)
+                ops[f"{name}_y{i}"] = lambda count=count: gather.pump_y(count)
 
     def spread_ops(name, spread):
         for i in range(4):
             count = A if i == 3 else 1
-            ops[f"{name}.s{i}"] = lambda count=count: spread.pump(count)
-            ops[f"{name}.f{i}"] = lambda count=count: spread.pump_forward(count)
+            ops[f"{name}_s{i}"] = lambda count=count: spread.pump(count)
+            ops[f"{name}_f{i}"] = lambda count=count: spread.pump_forward(count)
 
     def sum_ops(name, exchange, finish):
         for i in range(3):
             count = A if i == 2 else 1
             if name in direct_sums:
-                ops[f"{name}.d{i}"] = lambda count=count: exchange.send_direct(count)
+                ops[f"{name}_d{i}"] = lambda count=count: exchange.send_direct(count)
             else:
                 extra = 1 if exchange.z_first and i == 1 else 0
-                ops[f"{name}.s{i}"] = lambda count=count + extra: exchange.pump(count)
+                ops[f"{name}_s{i}"] = lambda count=count + extra: exchange.pump(count)
         if exchange.z_first:
-            ops[f"{name}.ends"] = exchange.start_ends
-            ops[f"{name}.finy"] = finish
-            ops[f"{name}.fin"] = exchange.finish
+            ops[f"{name}_ends"] = exchange.start_ends
+            ops[f"{name}_finy"] = finish
+            ops[f"{name}_fin"] = exchange.finish
         else:
-            ops[f"{name}.fin"] = finish
+            ops[f"{name}_fin"] = finish
 
     gather_ops("wq", g_wq, False)
+    gather_ops("wf", g_wf, False)
     gather_ops("pt", g_pt, False)
     gather_ops("kv", g_kv, False)
     spread_ops("fwq", f_wq)
+    spread_ops("fwf", f_wf)
     spread_ops("fpt", f_pt)
 
-    def chunk_finish(i, name):
-        exchange, lanes = w_fw[i], pl.ds(*cuts[i])
+    def chunk_finish(exchange, name):
         if name in direct_sums:
             exchange.finish_direct()
         else:
             (exchange.finish_y if exchange.z_first else exchange.finish)()
-        write(exchange.total, r_fw.at[:, lanes])
+        write(exchange.total, r_fw.at[:, pl.ds(*exchange.lanes)])
 
     for i, name in zip(chunk_order, "abc"):
-        gather_ops(name, g_fw[i], True)
-        sum_ops("w" + name, w_fw[i], lambda i=i, name="w" + name: chunk_finish(i, name))
+        for gather, part in zip(g_fw[i], ("", "2")):
+            gather_ops(name + part, gather, True)
+        for exchange, part in zip(w_fw[i], ("", "2")):
+            part = f"w{name}{part}"
+            sum_ops(part, exchange, lambda at=exchange, name=part: chunk_finish(at, name))
 
     def factor_finish(name, exchange, target=None):
         if name in direct_sums:
@@ -844,9 +864,8 @@
         x_own = tok[own_rows, :].astype(f32)
         r1_own = row_scale(x_own)
         normed_own = (x_own * r1_own * s.GAIN[0:1, :]).astype(bf16)
-        factors = [dot_nn(normed_own, s.WQ[p]) for p in range(N)]
-        held.first_tiles = [part[:, :LANES] for part in factors]
-        held.second_tiles = [part[:, LANES:] for part in factors]
+        held.normed_own = normed_own
+        held.second_tiles = [dot_nn(normed_own, s.WQ[p, :, LANES:]) for p in range(N)]
 
         kv_own = pl.ds(pl.multiple_of(w * T, T), T)
         kv_own = pl.multiple_of(w * y.KT, 32)
@@ -863,6 +882,8 @@
 
     @op("queries")
     def _():
+        f_wf.landed()
+        held.first_tiles = [dot_nn(held.normed_own, s.WQ[p, :, :LANES]) for p in range(N)]
         query_heads = collect(y.oq, y.HQ)
         heads_high = query_heads.astype(bf16)
         s.QH[:, :LANES] = heads_high
@@ -983,7 +1004,7 @@
 
     for i in range(h_mix.chunks):
         ops[f"at{i}"] = lambda i=i: forward_chunk(i)
-        ops[f"mix.f{i}"] = lambda i=i: h_mix.forward(i)
+        ops[f"mix_f{i}"] = lambda i=i: h_mix.forward(i)
 
     @op("middle")
     def _():
@@ -1039,33 +1060,29 @@
         s.MB[at, :] = mid.astype(bf16)
         s.OP[at, :] = out.astype(bf16)
 
-    def grad_blocks(parts, exchange):
+    def grad_blocks(target, to, left, right, lanes, exchange, begin):
         per = A // 4
         for j in range(4):
             block = z_order[j] if A == 4 else j
             at = pl.ds(pl.multiple_of(block * 256, 256), 256)
-            for target, to, left, right, lanes in parts:
-                value = dot_tn(left[:, at], right[:, lanes]).astype(bf16)
-                target[at, to : to + value.shape[1]] = value
-            if not exchange.z_first:
+            value = dot_tn(left[:, at], right[:, lanes]).astype(bf16)
+            target[at, to : to + value.shape[1]] = value
+            if begin and not exchange.z_first:
                 for q in range(per):
                     exchange.start(block * per + q)
 
     def dense_grads(chunk):
         base, wide, unit, units = chunks[chunk]
         first = sum(part[1] for part in chunks[:chunk])
-        g_fw[chunk].sent()
-        grad_blocks(
-            [
-                (s.FW, base, s.NM, s.GG, slice(first, first + wide)),
-                (s.FW, base + wide, cot, s.HID, slice(unit, unit + units)),
-            ],
-            w_fw[chunk],
-        )
-
+        for gather in g_fw[chunk]:
+            gather.sent()
+        one, two = w_fw[chunk][0], w_fw[chunk][-1]
+        grad_blocks(s.FW, base, s.NM, s.GG, slice(first, first + wide), one, one is not two)
+        grad_blocks(s.FW, base + wide, cot, s.HID, slice(unit, unit + units), two, True)
 
     def dense_chunk(chunk):
-        g_fw[chunk].landed_all()
+        for gather in g_fw[chunk]:
+            gather.landed_all()
         dense_rows(chunk, True)
         dense_rows(chunk, False)
 
@@ -1075,20 +1092,21 @@
 
     def last_dense(far):
         if far:
-            g_fw[chunk_order[-1]].landed_all()
+            for gather in g_fw[chunk_order[-1]]:
+                gather.landed_all()
         dense_rows(chunk_order[-1], far)
         n_mb.start(far)
 
     ops["ffCf"] = lambda: last_dense(True)
     ops["ffCn"] = lambda: last_dense(False)
-    ops["mb.pass"] = n_mb.pass_on
-
-    @op("op.start")
+    ops["mb_pass"] = n_mb.pass_on
+
+    @op("op_start")
     def _():
         n_op.start(True)
         n_op.start(False)
 
-    ops["op.pass"] = n_op.pass_on
+    ops["op_pass"] = n_op.pass_on
 
     @op("mid")
     def _():
@@ -1181,13 +1199,13 @@
         for z in z_order:
             w_kv.start(z)
 
-    ops["bg.f"] = h_bg.forward_all
-
-    @op("pt.g")
+    ops["bg_f"] = h_bg.forward_all
+
+    @op("pt_g")
     def _():
         h_bg.landed_all()
         mine = pl.ds(pl.multiple_of(n * 256, 256), 256)
-        grad_blocks([(s.PPT, 0, s.BG, s.MIX, mine)], w_pt)
+        grad_blocks(s.PPT, 0, s.BG, s.MIX, mine, w_pt, True)
 
     @op("qb")
     def _():
@@ -1210,21 +1228,21 @@
         ]
         held.heads_back = heads_back * (1.0 / QR)
 
-    @op("op.res")
+    @op("op_res")
     def _():
         o_out[own_rows, :] = (s.MID[own_rows, :] + n_op.result()).astype(bf16)
         h_og.start(0)
 
-    ops["og.f"] = h_og.forward_all
-
-    @op("og.l")
+    ops["og_f"] = h_og.forward_all
+
+    @op("og_l")
     def _():
         h_og.landed_all()
         write(o_out, r_out)
 
-    ops["tg.f"] = h_tg.forward_all
-
-    @op("tg.l")
+    ops["tg_f"] = h_tg.forward_all
+
+    @op("tg_l")
     def _():
         h_tg.landed_all()
         write(o_tok, r_tok)
@@ -1266,7 +1284,7 @@
     def _():
         held.first_back = factors_through(0)
 
-    @op("q.g1")
+    @op("q_g1")
     def _():
         factor_gradients(0)
         for z in z_order:
@@ -1291,12 +1309,18 @@
 
     @op("fb")
     def _():
-        first_back = held.first_back + factors_through(1)
+        first_back = held.first_back = held.first_back + factors_through(1)
         x_own = tok[own_rows, :].astype(f32)
         r1_own = row_scale(x_own)
         s.GS[0:1, :] = jnp.sum(first_back * x_own * r1_own, axis=0, keepdims=True)
         for k, peer in enumerate(narrow_peers):
             send(s.GS, s.GR.at[k], k_gain + k, peer)
+
+    @op("tg_s")
+    def _():
+        first_back = held.first_back
+        x_own = tok[own_rows, :].astype(f32)
+        r1_own = row_scale(x_own)
         scaled = first_back * s.GAIN[0:1, :]
         tokens_gradient = (
             s.MG[...]
@@ -1307,7 +1331,7 @@
         for chunk in range(h_tg.chunks):
             h_tg.start(chunk)
 
-    @op("q.g")
+    @op("q_g")
     def _():
         for k in range(3):
             arrive(s.GR.at[k], k_gain + k)
@@ -1326,36 +1350,53 @@
         for z in z_order:
             w_q[1].start(z)
 
-    for name in schedule:
-        ops[name]()
-
-    for exchange in (g_wq, g_pt, f_wq, f_pt, *w_fw, w_kv, w_pt, *w_q):
+    for act in schedule(SimpleNamespace(**ops)):
+        act()
+
+    for exchange in (g_wq, g_wf, g_pt, f_wq, f_wf, f_pt, *sum(w_fw, []), w_kv, w_pt, *w_q):
         exchange.sent()
-    assert (taken[0], taken[1]) == (rsem.shape[0], ssem.shape[0])
+    assert (taken[0], taken[1]) == (rsem.shape[0], ssem.shape[0]), taken
     for copy in pending:
         copy.wait_send()
     for copy in written:
         copy.wait()
 
 
-def results_kernel(y, out, tok, fw, pt, q, *refs):
-    r_out, r_tok, r_pt, r_gate, r_up, r_down = refs[:6]
-    o_pre, o_qh, o_qs, o_kh, o_ks, o_vh, o_vs, o_mid = refs[6:14]
-    in_fw, in_pt, in_q, in_tok, in_out, o_tok, o_pt, o_gate, o_up, o_down, sems = refs[14:]
+def results_kernel(y, *refs):
+    sources, targets, sems = refs[:5], refs[5:19], refs[-1]
+    held = refs[19:-1]
+    in_q, in_pt, in_fw, in_tok, in_out = held[:5]
+    o_tok, o_pt, o_gate, o_up, o_down, o_pre, o_qh, o_qs, o_kh, o_ks, o_vh, o_vs, o_mid = held[5:]
     FM, F, half = y.FM, y.F, y.F - y.FM
+    loads = [pltpu.make_async_copy(*pair, sems.at[i]) for i, pair in enumerate(zip(sources, held))]
+    for load in loads:
+        load.start()
     used = []
 
-    def start(src, dst):
-        copy = pltpu.make_async_copy(src, dst, sems.at[len(used)])
-        copy.start()
-        used.append(copy)
-        return copy
-
-    got_fw, got_pt, got_q = start(fw, in_fw), start(pt, in_pt), start(q, in_q)
-    got_tok, got_out = start(tok, in_tok), start(out, in_out)
-    got_fw.wait()
+    def give(ref):
+        place = len(used)
+        used.append(pltpu.make_async_copy(ref, targets[place], sems.at[5 + place]))
+        used[-1].start()
+
+    loads[0].wait()
+    o_qs[...] = in_q[:, :LANES].T[: y.SQ]
+    second = in_q[:, LANES:].T
+    o_ks[...] = second[y.oK : y.oK + y.SK]
+    o_vs[...] = second[y.oV : y.oV + y.SK]
+    o_qh[...] = second[y.oq : y.oq + y.HQ]
+    o_kh[...] = second[y.ok : y.ok + y.HK]
+    o_vh[...] = second[y.ov : y.ov + y.HK]
+    o_pre[...] = second[y.og : y.og + 1]
+    o_mid[...] = second[y.og + 1 : y.og + 2]
+    for ref in (o_pre, o_qh, o_qs, o_kh, o_ks, o_vh, o_vs, o_mid):
+        give(ref)
+    loads[1].wait()
+    for first in range(0, 256, LANES):
+        o_pt[first : first + LANES, :] = in_pt[:, first : first + LANES].T
+    give(o_pt)
+    loads[2].wait()
     *whole_chunks, (base, wide, unit, _) = y.chunks
-    for part, (target, result) in enumerate(((o_gate, r_gate), (o_up, r_up), (o_down, r_down))):
+    for part, target in enumerate((o_gate, o_up, o_down)):
         for at, _, first_unit, _ in whole_chunks:
             for first in range(0, 256, LANES):
                 place = at + part * 256 + first
@@ -1366,27 +1407,13 @@
         tail = base + (wide + LANES if part == 2 else 2 * LANES)
         tail = in_fw[:, tail : tail + LANES].T
         target[FM:, :] = tail[half:] if part == 1 else tail[:half]
-        start(target, result)
-    got_tok.wait()
+        give(target)
+    loads[3].wait()
     o_tok[...] = in_tok[...].astype(f32)
-    start(o_tok, r_tok)
-    got_out.wait()
-    start(in_out, r_out)
-    got_pt.wait()
-    for first in range(0, 256, LANES):
-        o_pt[first : first + LANES, :] = in_pt[:, first : first + LANES].T
-    start(o_pt, r_pt)
-    got_q.wait()
-    o_qs[...] = in_q[:, :LANES].T[: y.SQ]
-    second = in_q[:, LANES:].T
-    o_ks[...] = second[y.oK : y.oK + y.SK]
-    o_vs[...] = second[y.oV : y.oV + y.SK]
-    o_qh[...] = second[y.oq : y.oq + y.HQ]
-    o_kh[...] = second[y.ok : y.ok + y.HK]
-    o_vh[...] = second[y.ov : y.ov + y.HK]
-    o_pre[...] = second[y.og : y.og + 1]
-    o_mid[...] = second[y.og + 1 : y.og + 2]
-    for copy in used[5:]:
+    give(o_tok)
+    loads[4].wait()
+    give(in_out)
+    for copy in used:
         copy.wait()
 
 
@@ -1416,9 +1443,15 @@
         y = make_layout(W, N, T, D, F, L, N * kheads.shape[1] // KR)
         assert R == N
         scratch = scratch_list(y)
-        z_first = len(z_first_chunks) + len(z_first_sums)
-        arrivals = 18 * y.A + 39 + z_first * (y.A + 2) + (7 - z_first) * (2 * y.A + 1)
-        sends = 71 + len(y_first_chunks) + len(y_first_gathers)
+        gathers = [flag for parts in gather_parts for _, flag in parts]
+        sums = [flag for parts in sum_parts for _, flag in parts]
+        y_first, z_first = sum(gathers) + len(y_first_gathers), sum(sums) + len(z_first_sums)
+        gathers, sums = 4 + len(gathers), 4 + len(sums)
+        arrivals = gathers * (y.A + 1) + (3 - len(y_first_gathers)) * (y.A - 1)
+        arrivals += 3 * (y.A + 2) + (8 + 4 * 2) + 6 + 9
+        arrivals += z_first * (y.A + 2) + (sums - z_first) * (2 * y.A + 1)
+        arrivals -= len(direct_sums) * y.A
+        sends = 2 * gathers + y_first + 2 * sums + 48
         vmem = pl.BlockSpec(memory_space=pltpu.VMEM)
 
         def kernel(*refs):
@@ -1437,7 +1470,7 @@
             in_specs=[vmem] * 9 + [pl.BlockSpec(memory_space=pl.ANY)] * 6,
             out_specs=[pl.BlockSpec(memory_space=pl.ANY)] * 5,
             scratch_shapes=[*scratch.values()]
-            + [pltpu.SemaphoreType.DMA((count,)) for count in (sends, arrivals, 8, 6)],
+            + [pltpu.SemaphoreType.DMA((count,)) for count in (sends, arrivals, sums + 1, 6)],
             compiler_params=pltpu.CompilerParams(
                 collective_id=0, has_side_effects=True, vmem_limit_bytes=63 * 2**20
             ),
@@ -1463,19 +1496,21 @@
         def results(*refs):
             results_kernel(y, *refs)
 
-        large = ((y.M, D), bf16), ((y.M, D), f32), ((256, RW), f32), *[((F, RW), f32)] * 3
-        small = [(count, RW) for count in (1, y.HQ, y.SQ, y.HK, y.SK, y.HK, y.SK, 1)]
-        held = [((RW, y.FW), f32), ((RW, 256), f32), ((RW, 256), f32), ((y.M, D), bf16), *large]
+        large = [((256, RW), f32), *[((F, RW), f32)] * 3, ((y.M, D), f32), ((y.M, D), bf16)]
+        small = [((count, RW), f32) for count in (1, y.HQ, y.SQ, y.HK, y.SK, y.HK, y.SK, 1)]
+        held = [((RW, 256), f32), ((RW, 256), f32), ((RW, y.FW), f32), *[((y.M, D), bf16)] * 2]
+        held += [large[4], *large[:4], *small]
+        anywhere = pl.BlockSpec(memory_space=pl.ANY)
         outputs = pl.pallas_call(
             results,
-            out_shape=[shape(*each) for each in large] + [shape(each, f32) for each in small],
-            in_specs=[pl.BlockSpec(memory_space=pl.ANY)] * 5,
-            out_specs=[pl.BlockSpec(memory_space=pl.ANY)] * 6 + [vmem] * 8,
-            scratch_shapes=[pltpu.VMEM(*each) for each in held] + [pltpu.SemaphoreType.DMA((11,))],
+            out_shape=[shape(*each) for each in small + large],
+            in_specs=[anywhere] * 5,
+            out_specs=[anywhere] * 14,
+            scratch_shapes=[pltpu.VMEM(*each) for each in held] + [pltpu.SemaphoreType.DMA((19,))],
             compiler_params=pltpu.CompilerParams(vmem_limit_bytes=63 * 2**20),
             name="results",
-        )(*raw)
-        out, tok, pt_back, gate, up, down, pre, qh, qs, kh, ks, vh, vs, mid = outputs
+        )(*raw[::-1])
+        pre, qh, qs, kh, ks, vh, vs, mid, pt_back, gate, up, down, tok, out = outputs
         tokens_like = lambda values: values.reshape(R, T, D)
         return (
             tokens_like(out),

time: 135 us -> 128 us (0.948)
  Pallas kernels: 134 us -> 127 us
    pallas_call x1, Pallas kernels: 130 us -> 123 us  [on_device(): pl.pallas_call(kernel, out_shape=(shape((y.M, D), bf16), shape((y.M, D),...]
where the time goes in v5:
time: 128 us
  Pallas kernels  127 us (99%)
    pallas_call x1, Pallas kernels, on_device(): pl.pallas_call(kernel, out_shape=(shape((y.M, D), bf16), shape((y.M, D),...  123 us
    pallas_call x1, Pallas kernels, on_device(): pl.pallas_call(results, out_shape=[shape(*each) for each in small + large...  3.75 us

profile of v5, /device:TPU:0, one launch (start us, length us, event | category | flops | bytes accessed | tf_op | source)
XLA Modules:
  0.0 127.9 jit_solution(6173362814202332589)
XLA Ops:
  0.7 123.3 %block.1 = (bf16[512,1024]{1,0:T(8,128)(2,1)}, bf16[512,1024]{1,0:T(8,128)(2,1)}, f32[128,2176]{1,0:T(8,128)}, f32[128,256]{1,0:T(8,128)}, f32[128,256]{1,0:T(8,128)}) custom-call(s32[4,1024]{1,0:T(4,128)} %refs_0_.1, bf16[1,128]{1,0:T(2,128)(2,1)} %bitcast.34, bf16[24,128]{1,0:T(8,128)(2,1)} %bitcast.31, bf16[96,128]{1,0:T(8,128)(2,1)} %bitcast.28, ...), custom_call_target="tpu_custom_call" | custom-call | tf_op jit(solution)/shard_map/block/pallas_call | solution.py:1461
  123.9 3.8 %results.1 = (f32[1,128]{1,0:T(1,128)}, f32[24,128]{1,0:T(8,128)}, f32[96,128]{1,0:T(8,128)}, f32[8,128]{1,0:T(8,128)}, f32[32,128]{1,0:T(8,128)}, /*index=5*/f3...) custom-call(f32[128,256]{1,0:T(8,128)} %get-tuple-element.33.refs_0_, ...), custom_call_target="tpu_custom_call" | custom-call | tf_op jit(solution)/shard_map/results/pallas_call | solution.py:1504

commit v6 on v5

--- a/solution.py
+++ b/solution.py
@@ -202,8 +202,9 @@
         TFW=vm(RW, y.FW, kind=f32),
         TPT=vm(RW, 256, kind=f32),
         TQ=vm(RW, 256, kind=f32),
-        GS=vm(8, D, kind=f32),
-        GR=vm(3, 8, D, kind=f32),
+        GC=vm(D, LANES, kind=f32),
+        GS=vm(8, D // 4, kind=f32),
+        GR=vm(3, 8, D // 4, kind=f32),
         YFW=vm(A * RW, y.FW),
         **{
             f"RF{i}{j}": vm((A + 1) * RW * (1 + z_first), lanes)
@@ -232,13 +233,13 @@
         do.fpt_f1, do.b2_h1, do.b_L, do.a_y1, do.a_y2, do.fwf_f3, do.queries, do.b2_y1, do.fpt_f2,
         do.at_x, do.at0, do.at1, do.at2, do.b2_h2, do.c2_h3, do.a_h3, do.a_y3, do.at3, do.mix_f0,
         do.b2_y2, do.b_h1, do.c2_y1, do.fpt_f3, do.c_L, do.b2_h3, do.b2_y3, do.mix_f1, do.c2_y2,
-        do.mix_f2, do.mix_f3, do.c2_y3, do.middle, do.ff_a, do.g_a, do.wa2_ends, do.b_h2, do.c_h1,
-        do.wa_s0, do.b_h3, do.ff_b, do.g_b, do.wb2_ends, do.c_h2, do.c_h3, do.ffCf, do.wb_s0,
-        do.wa2_s1, do.mb_pass, do.wa_s1, do.ffCn, do.wa2_s2, do.wb2_s1, do.g_c, do.wb2_s2,
-        do.op_start, do.wb_s1, do.mid, do.bq0, do.wc_s0, do.wa_s2, do.bq1, do.bq2, do.op_pass,
-        do.wb_s2, do.bq3, do.kvst, do.wc_s1, do.qb, do.qg1, do.wkv_d0, do.bg_f, do.pt_g,
-        do.wkv_d1, do.wkv_d2, do.op_res, do.wpt_s0, do.q_g1, do.wc_s2, do.wkv_fin, do.qg, do.fb1,
-        do.fb, do.wpt_s1, do.og_f, do.tg_s, do.wqa_d0, do.wa2_fin, do.wqa_d1, do.wa_fin,
+        do.mix_f2, do.mix_f3, do.c2_y3, do.middle, do.ff_a, do.g_a, do.g_a2, do.wa2_ends, do.b_h2,
+        do.c_h1, do.wa_s0, do.b_h3, do.ff_b, do.g_b, do.g_b2, do.wb2_ends, do.c_h2, do.c_h3,
+        do.ffCf, do.wb_s0, do.wa2_s1, do.mb_pass, do.wa_s1, do.ffCn, do.wa2_s2, do.wb2_s1, do.g_c,
+        do.wb2_s2, do.op_start, do.wb_s1, do.mid, do.bq0, do.wc_s0, do.wa_s2, do.bq1, do.bq2,
+        do.op_pass, do.wb_s2, do.bq3, do.kvst, do.wc_s1, do.qb, do.qg1, do.wkv_d0, do.bg_f,
+        do.pt_g, do.wkv_d1, do.wkv_d2, do.op_res, do.wpt_s0, do.q_g1, do.wc_s2, do.wkv_fin, do.qg,
+        do.fb1, do.fb, do.wpt_s1, do.og_f, do.tg_s, do.wqa_d0, do.wa2_fin, do.wqa_d1, do.wa_fin,
         do.wb_fin, do.q_g, do.wb2_fin, do.wqa_d2, do.og_l, do.wpt_s2, do.wqb_d0, do.wc_fin,
         do.wqa_fin, do.wa2_finy, do.wqb_d1, do.wqb_d2, do.tg_f, do.tg_l, do.wb2_finy, do.wpt_fin,
         do.wqb_fin,
@@ -1071,14 +1072,17 @@
                 for q in range(per):
                     exchange.start(block * per + q)
 
-    def dense_grads(chunk):
+    def dense_grads(chunk, part):
         base, wide, unit, units = chunks[chunk]
         first = sum(part[1] for part in chunks[:chunk])
-        for gather in g_fw[chunk]:
-            gather.sent()
         one, two = w_fw[chunk][0], w_fw[chunk][-1]
-        grad_blocks(s.FW, base, s.NM, s.GG, slice(first, first + wide), one, one is not two)
-        grad_blocks(s.FW, base + wide, cot, s.HID, slice(unit, unit + units), two, True)
+        if part == 0:
+            for gather in g_fw[chunk]:
+                gather.sent()
+            grad_blocks(s.FW, base, s.NM, s.GG, slice(first, first + wide), one, one is not two)
+        if part == 1 or one is two:
+            units = slice(unit, unit + units)
+            grad_blocks(s.FW, base + wide, cot, s.HID, units, two, True)
 
     def dense_chunk(chunk):
         for gather in g_fw[chunk]:
@@ -1088,7 +1092,8 @@
 
     for i, name in zip(chunk_order, "abc"):
         ops["ff_" + name] = lambda i=i: dense_chunk(i)
-        ops["g_" + name] = lambda i=i: dense_grads(i)
+        for part, end in enumerate(("", "2")[: len(w_fw[i])]):
+            ops["g_" + name + end] = lambda i=i, part=part: dense_grads(i, part)
 
     def last_dense(far):
         if far:
@@ -1108,13 +1113,18 @@
 
     ops["op_pass"] = n_op.pass_on
 
+    def keep_gain(which, row):
+        for i in range(4):
+            place = 4 * which + i
+            s.GS[place : place + 1, :] = row[:, i * (D // 4) : (i + 1) * (D // 4)]
+
     @op("mid")
     def _():
         mid_back = n_mb.result()
         mid_own = s.MID[own_rows, :]
         r2_own = s.R2[own_rows, :][:, :1]
         scaled = mid_back * s.GAIN[1:2, :]
-        s.GS[1:2, :] = jnp.sum(mid_back * mid_own * r2_own, axis=0, keepdims=True)
+        keep_gain(1, jnp.sum(mid_back * mid_own * r2_own, axis=0, keepdims=True))
         middle_gradient = (
             cot[own_rows, :].astype(f32)
             + r2_own * scaled
@@ -1261,16 +1271,20 @@
             total = total + dot_nt(s.QGS[p, :, lanes], s.WQ[p, :, lanes])
         return total
 
-    def factor_gradients(tile):
+    def factor_gradients(tile, added=None):
         lanes = pl.ds(*tiles[tile])
         for k, peer in enumerate(narrow_peers):
             arrive(s.QGR.at[peer[1], :, lanes], k_a2a[tile] + k)
         for j in range(4):
-            block = pl.ds(pl.multiple_of(j * 256, 256), 256)
+            at = pl.ds(j * 256, 256)
             value = jnp.zeros((256, LANES), f32)
             for p in range(N):
-                value = value + dot_tn(s.NORM[p * T : (p + 1) * T, block], s.QGR[p, :, lanes])
-            s.PQ[block, lanes] = value.astype(bf16)
+                value = value + dot_tn(s.NORM[p * T : (p + 1) * T, at], s.QGR[p, :, lanes])
+            if added is not None:
+                value = value + added[at, :]
+            s.PQ[at, lanes] = value.astype(bf16)
+        for z in z_order:
+            w_q[tile].start(z)
 
     @op("qg1")
     def _():
@@ -1287,8 +1301,6 @@
     @op("q_g1")
     def _():
         factor_gradients(0)
-        for z in z_order:
-            w_q[0].start(z)
 
     @op("qg")
     def _():
@@ -1312,7 +1324,7 @@
         first_back = held.first_back = held.first_back + factors_through(1)
         x_own = tok[own_rows, :].astype(f32)
         r1_own = row_scale(x_own)
-        s.GS[0:1, :] = jnp.sum(first_back * x_own * r1_own, axis=0, keepdims=True)
+        keep_gain(0, jnp.sum(first_back * x_own * r1_own, axis=0, keepdims=True))
         for k, peer in enumerate(narrow_peers):
             send(s.GS, s.GR.at[k], k_gain + k, peer)
 
@@ -1335,20 +1347,21 @@
     def _():
         for k in range(3):
             arrive(s.GR.at[k], k_gain + k)
-        factor_gradients(1)
-        gain_rows = s.GS[...]
+        packed = s.GS[...]
         for k in range(3):
-            gain_rows = gain_rows + s.GR[k]
+            packed = packed + s.GR[k]
+        gain_rows = [
+            jnp.concatenate([packed[i : i + 1] for i in range(first, first + 4)], axis=1)
+            for first in (0, 4)
+        ]
         lane_row = row_iota(LANES, D)
         spread = jnp.where(
             lane_row == y.og,
-            gain_rows[0:1],
-            jnp.where(lane_row == y.og + 1, gain_rows[1:2], 0.0),
+            gain_rows[0],
+            jnp.where(lane_row == y.og + 1, gain_rows[1], 0.0),
         )
-        gain_columns = spread.T
-        s.PQ[:, LANES:] = (s.PQ[:, LANES:].astype(f32) + gain_columns).astype(bf16)
-        for z in z_order:
-            w_q[1].start(z)
+        s.GC[...] = spread.T
+        factor_gradients(1, s.GC)
 
     for act in schedule(SimpleNamespace(**ops)):
         act()

time: 128 us -> 127 us (level)
  no operation moved by 1% of the time
where the time goes in v6:
time: 127 us
  Pallas kernels  126 us (99%)
    pallas_call x1, Pallas kernels, on_device(): pl.pallas_call(kernel, out_shape=(shape((y.M, D), bf16), shape((y.M, D),...  123 us
    pallas_call x1, Pallas kernels, on_device(): pl.pallas_call(results, out_shape=[shape(*each) for each in small + large...  3.75 us

profile of v6, /device:TPU:0, one launch (start us, length us, event | category | flops | bytes accessed | tf_op | source)
XLA Modules:
  0.0 127.3 jit_solution(10218400374530560243)
XLA Ops:
  0.7 122.7 %block.1 = (bf16[512,1024]{1,0:T(8,128)(2,1)}, bf16[512,1024]{1,0:T(8,128)(2,1)}, f32[128,2176]{1,0:T(8,128)}, f32[128,256]{1,0:T(8,128)}, f32[128,256]{1,0:T(8,128)}) custom-call(s32[4,1024]{1,0:T(4,128)} %refs_0_.1, bf16[1,128]{1,0:T(2,128)(2,1)} %bitcast.34, bf16[24,128]{1,0:T(8,128)(2,1)} %bitcast.31, bf16[96,128]{1,0:T(8,128)(2,1)} %bitcast.28, ...), custom_call_target="tpu_custom_call" | custom-call | tf_op jit(solution)/shard_map/block/pallas_call | solution.py:1474
  123.4 3.8 %results.1 = (f32[1,128]{1,0:T(1,128)}, f32[24,128]{1,0:T(8,128)}, f32[96,128]{1,0:T(8,128)}, f32[8,128]{1,0:T(8,128)}, f32[32,128]{1,0:T(8,128)}, /*index=5*/f3...) custom-call(f32[128,256]{1,0:T(8,128)} %get-tuple-element.33.refs_0_, ...), custom_call_target="tpu_custom_call" | custom-call | tf_op jit(solution)/shard_map/results/pallas_call | solution.py:1517
